TPU v7x, 32 devices: a whole 2x2x4 slice. The times are simulated.
32 devices in a mesh: seq: 8 (over z, core), img: 4 (over y, x).
Axes of the slice: x: 2, y: 2, z: 4, core: 2. Of those that a mesh axis runs over, the one named last changes fastest.
Arguments:
- images: bfloat16 [4, 2048, 1024], P('img', 'seq'), may hold values from -6 to 6
- cotangent: bfloat16 [4, 2048, 1024], P('img', 'seq'), may hold values from -6 to 6
- qkv_weight: float32 [1024, 3072], P(('seq', 'img')), may hold values from -0.1875 to 0.1875
- out_weight: float32 [1024, 1024], P(('seq', 'img')), may hold values from -1 to 1
- up_weight: float32 [1024, 4096], P(('seq', 'img')), may hold values from -0.1875 to 0.1875
- down_weight: float32 [4096, 1024], P(('seq', 'img')), may hold values from -0.09375 to 0.09375
- norm_params: float32 [4, 1024], P(None, ('seq', 'img')), may hold values from -1 to 5, as said below
- qkv_first: float32 [1024, 3072], P(('seq', 'img')), may hold values from -5.6372688e-05 to 5.6372688e-05
- out_first: float32 [1024, 1024], P(('seq', 'img')), may hold values from -5.6372688e-05 to 5.6372688e-05
- up_first: float32 [1024, 4096], P(('seq', 'img')), may hold values from -5.6372688e-05 to 5.6372688e-05
- down_first: float32 [4096, 1024], P(('seq', 'img')), may hold values from -5.6372688e-05 to 5.6372688e-05
- norm_first: float32 [4, 1024], P(None, ('seq', 'img')), may hold values from -0.00022549075 to 0.00022549075
- qkv_second: float32 [1024, 3072], P(('seq', 'img')), may hold values from 7.9447e-11 to 3.17788e-10, as said below
- out_second: float32 [1024, 1024], P(('seq', 'img')), may hold values from 7.9447e-11 to 3.17788e-10, as said below
- up_second: float32 [1024, 4096], P(('seq', 'img')), may hold values from 7.9447e-11 to 3.17788e-10, as said below
- down_second: float32 [4096, 1024], P(('seq', 'img')), may hold values from 7.9447e-11 to 3.17788e-10, as said below
- norm_second: float32 [4, 1024], P(None, ('seq', 'img')), may hold values from 1.271152e-09 to 5.084608e-09, as said below
Outputs:
- activations: bfloat16 [4, 2048, 1024], P('img', 'seq')
- input_grad: bfloat16 [4, 2048, 1024], P('img', 'seq')
- grad_norm: float32 [], replicated
- qkv_new: float32 [1024, 3072], P(('seq', 'img'))
- out_new: float32 [1024, 1024], P(('seq', 'img'))
- up_new: float32 [1024, 4096], P(('seq', 'img'))
- down_new: float32 [4096, 1024], P(('seq', 'img'))
- norm_new: float32 [4, 1024], P(None, ('seq', 'img'))
- qkv_first_new: float32 [1024, 3072], P(('seq', 'img'))
- out_first_new: float32 [1024, 1024], P(('seq', 'img'))
- up_first_new: float32 [1024, 4096], P(('seq', 'img'))
- down_first_new: float32 [4096, 1024], P(('seq', 'img'))
- norm_first_new: float32 [4, 1024], P(None, ('seq', 'img'))
- qkv_second_new: float32 [1024, 3072], P(('seq', 'img'))
- out_second_new: float32 [1024, 1024], P(('seq', 'img'))
- up_second_new: float32 [1024, 4096], P(('seq', 'img'))
- down_second_new: float32 [4096, 1024], P(('seq', 'img'))
- norm_second_new: float32 [4, 1024], P(None, ('seq', 'img'))
Inputs may be any that keep to these rules, and one draw needn't show every extreme that they name: `norm_params`: rows 0 and 2 hold positive gains, rows 1 and 3 biases. `qkv_second`: positive. `out_second`: positive. `up_second`: positive. `down_second`: positive. `norm_second`: positive.
All inputs are finite; a program needn't handle non-finite values.
Results may differ from a plain program's by a relative error of at most 0.009.
Values may be sent and summed in bfloat16 or wider, within the bound.
No kernel may reach another device: no remote copies, remote signals or barrier semaphores. Data moves between devices by JAX's collectives and lax.ppermute only.
A program may use at most 256 MiB of HBM per device.

v0:
```python
import functools

import jax
import jax.numpy as jnp
from jax import lax
from jax.experimental import pallas as pl
from jax.experimental.pallas import tpu as pltpu
from jax.sharding import PartitionSpec as P

HEAD_DIM = 64
STEP = 10
NORM_EPS = 1e-05
BETA_ONE = 0.9
BETA_TWO = 0.999
ADAM_EPS = 1e-08
WEIGHT_DECAY = 0.1
CLIP_LIMIT = 1.0
LANES = 128

LOW = jnp.bfloat16
WIDE = jnp.float32
ALL = ("z", "c", "y", "x")
SWAP = [(0, 1), (1, 0)]


def swap(value, axis):
    return lax.ppermute(value, axis, SWAP)


def shift(value, step, wrap=True):
    size = lax.axis_size("z")
    pairs = [(i, (i + step) % size) for i in range(size) if wrap or 0 <= i + step < size]
    return lax.ppermute(value, "z", pairs)


def mine(pair_axis_first):
    return jnp.where(lax.axis_index("c") == 0, pair_axis_first[0], pair_axis_first[1])


def other(pair_axis_first):
    return jnp.where(lax.axis_index("c") == 0, pair_axis_first[1], pair_axis_first[0])


def in_order(own, mate, axis=0):
    first = lax.axis_index("c") == 0
    return jnp.concatenate([jnp.where(first, own, mate), jnp.where(first, mate, own)], axis)


def after(value, *before):
    return lax.optimization_barrier((*before, value))[-1]


def column_first(shard):
    return [shard] + [shift(shard, k) for k in range(1, lax.axis_size("z"))]


def plane_last(column, between=()):
    half = column.shape[0] // 2
    along_x, along_y = swap(column, "x"), swap(column, "y")
    along_x, along_y = after(along_x, *between), after(along_y, *between)
    far = (swap(along_y[:half], "x"), swap(along_x[half:], "y"))
    return (column, along_x, along_y) + far


def plane_first(shard):
    half = shard.shape[0] // 2
    along_x, along_y = swap(shard, "x"), swap(shard, "y")
    far_low, far_high = swap(along_y[:half], "x"), swap(along_x[half:], "y")
    return jnp.concatenate([shard, along_x, along_y, far_low, far_high])


def column_last(plane):
    parts = [plane]
    for _ in range(1, lax.axis_size("z")):
        parts.append(shift(parts[-1], 1))
    return parts


def column_first_spots(depth):
    half = depth // 2
    spots = [(0, (k,), 0, (k, 0, 0)) for k in range(depth)]
    spots += [(1, (k,), 0, (k, 0, 1)) for k in range(depth)]
    spots += [(2, (k,), 0, (k, 1, 0)) for k in range(depth)]
    spots += [(3, (k,), 0, (k, 1, 1)) for k in range(half)]
    return spots + [(4, (k - half,), 0, (k, 1, 1)) for k in range(half, depth)]


def plane_first_spots(depth, rows):
    return [(k, (), p * rows, (k, p // 2, p % 2)) for k in range(depth) for p in range(4)]


def first_hop(send_x, keep_x, send_y, keep_y, before=()):
    return keep_x, swap(after(send_x, *before), "x"), keep_y, swap(after(send_y, *before), "y")


def later_hops(keep_x, got_x, keep_y, got_y, between=(), last=()):
    depth, rows, cols = keep_x.shape[1:]

    def second_hop(kx, gx, ky, gy, to_y, to_x):
        to_y[...] = (kx[1].astype(WIDE) + gx[1].astype(WIDE)).astype(LOW)
        to_x[...] = (ky[1].astype(WIDE) + gy[1].astype(WIDE)).astype(LOW)

    outs = [((depth, rows, cols), LOW)] * 2
    to_y, to_x = run(second_hop, outs, keep_x, got_x, keep_y, got_y, scalars=False, deps=between)
    on_y, on_x = swap(to_y, "y"), swap(to_x, "x")
    hop = (on_x, on_y)

    def third_hop(kx, gx, ky, gy, ony, onx, own, *sends):
        for k in range(depth):
            one = kx[0, k].astype(WIDE) + gx[0, k].astype(WIDE) + ony[k].astype(WIDE)
            two = ky[0, k].astype(WIDE) + gy[0, k].astype(WIDE) + onx[k].astype(WIDE)
            out = sends[k - 1] if k else own
            out[:rows, :] = one.astype(out.dtype)
            out[rows:, :] = two.astype(out.dtype)

    outs = [((2 * rows, cols), WIDE if k == 0 else LOW) for k in range(depth)]
    own, *sends = run(third_hop, outs, keep_x, got_x, keep_y, got_y, on_y, on_x, scalars=False, deps=last)
    return [own] + [shift(part, k + 1) for k, part in enumerate(sends)], hop


def sum_of(refs):
    total = refs[0][...]
    for ref in refs[1:]:
        total = total + ref[...].astype(WIDE)
    return total


def spread(value):
    return jnp.broadcast_to(value, (8, LANES))


def total_squares(value):
    return jnp.sum(jnp.sum(value * value, axis=1, keepdims=True), axis=0, keepdims=True)


def finish_down(parts):
    def kernel(*refs):
        total = sum_of(refs[: len(parts)])
        refs[-2][...] = total
        refs[-1][...] = spread(total_squares(total))

    return run(kernel, [(parts[0].shape, WIDE), ((8, LANES), WIDE)], *parts, scalars=False)


def finish_up(parts, squares, rows, half_ff):
    half_d = parts[0].shape[1] - half_ff
    small = rows // 2

    def kernel(coords, squares_ref, *refs):
        own_ref, mate_ref, out_ref, total_ref, all_ref = refs[len(parts) :]
        total = sum_of(refs[: len(parts)])
        all_ref[...] = total
        core = coords[3]
        own_ref[...] = all_ref[pl.ds(pl.multiple_of(core * rows, 8), rows), :half_ff]
        mate_ref[...] = all_ref[pl.ds(pl.multiple_of((1 - core) * rows, 8), rows), :half_ff]
        for p in range(2):
            for h in range(2):
                block = total[h * rows + p * small : h * rows + (p + 1) * small, half_ff:]
                out_ref[h * small : (h + 1) * small, p * half_d : (p + 1) * half_d] = block
        total_ref[...] = squares_ref[...] + spread(total_squares(total))

    outs = [((rows, half_ff), WIDE)] * 2 + [((rows, 2 * half_d), WIDE), ((8, LANES), WIDE)]
    scratch = [pltpu.VMEM(parts[0].shape, WIDE)]
    return run(kernel, outs, squares, *parts, scratch=scratch)


def finish_qkv(parts, squares, rows, half_qkv, deps=()):
    def kernel(coords, squares_ref, *refs):
        own_ref, mate_ref, small_ref, all_ref = refs[len(parts) :]
        total = sum_of(refs[: len(parts)])
        all_ref[...] = total
        core = coords[3]
        own_ref[...] = all_ref[pl.ds(pl.multiple_of(core * rows, 8), rows), :half_qkv]
        mate_ref[...] = all_ref[pl.ds(pl.multiple_of((1 - core) * rows, 8), rows), :half_qkv]
        small_ref[: 2 * rows, :] = total[:, half_qkv:]
        small_ref[2 * rows :, :] = squares_ref[...] + spread(total_squares(total[:, :half_qkv]))

    outs = [((rows, half_qkv), WIDE)] * 2 + [((2 * rows + 8, LANES), WIDE)]
    scratch = [pltpu.VMEM(parts[0].shape, WIDE)]
    return run(kernel, outs, squares, *parts, scratch=scratch, deps=deps)


def chip_squares(small, got):
    rows = small.shape[0] - 8

    def kernel(small_ref, got_ref, total_ref, norm_ref):
        total = small_ref[...] + got_ref[...]
        norm_ref[...] = total[:rows]
        total_ref[...] = total[rows:] + spread(total_squares(total[:rows]))

    outs = [((8, LANES), WIDE), ((rows, LANES), WIDE)]
    return run(kernel, outs, small, got, scalars=False)


def sum_chips(value):
    across = lax.ppermute(value, ("y", "x"), [(i, 3 - i) for i in range(4)])
    value = value + swap(value, "y") + (swap(value, "x") + across)
    size, near = lax.axis_size("z"), 1
    while near < size // 2:
        value = value + lax.ppermute(value, "z", [(i, i ^ near) for i in range(size)])
        near *= 2
    return [value, lax.ppermute(value, "z", [(i, i ^ near) for i in range(size)])]


def interleave(first, own, mate, blocks):
    size = own.shape[1] // blocks
    pieces = []
    for j in range(blocks):
        at = slice(j * size, (j + 1) * size)
        pieces += [jnp.where(first, own[:, at], mate[:, at]), jnp.where(first, mate[:, at], own[:, at])]
    return jnp.concatenate(pieces, axis=1)


def update_all(grads, totals, masters, firsts, seconds, rates, decays, blocks):
    steps = 4
    n, m = len(grads), len(totals)

    def tile(array):
        rows, cols = array.shape
        return pl.BlockSpec((rows // steps, cols), lambda i: (i, 0))

    def whole(array):
        return pl.BlockSpec(array.shape, lambda i: (0, 0))

    def kernel(coords, *refs):
        first = coords[3] == 0
        g, t, old, new = refs[:n], refs[n : n + m], refs[n + m : n + m + 15], refs[n + m + 15 :]
        total = sum_of(t)[0:1, 0:1]
        norm = jnp.sqrt(total)
        clip = jnp.minimum(1.0, CLIP_LIMIT / (norm + 1e-06))
        qkv = interleave(first, g[0][...], g[1][...], blocks[0])
        up = interleave(first, g[3][...], g[4][...], blocks[1])
        for k, grad in enumerate((qkv, g[2][...], up, g[5][...], g[6][...])):
            news = adam_update(old[k][...], old[5 + k][...], old[10 + k][...], clip * grad, rates[k], decays[k])
            for part in range(3):
                new[5 * part + k][...] = news[part]
        new[15][...] = norm

    state = (*masters, *firsts, *seconds)
    specs = [whole(a) if k % 5 == 4 else tile(a) for k, a in enumerate(state)]
    norm_out = jax.ShapeDtypeStruct((1, 1), WIDE)
    return pl.pallas_call(
        kernel,
        grid=(steps,),
        out_shape=[jax.ShapeDtypeStruct(a.shape, WIDE) for a in state] + [norm_out],
        in_specs=[pl.BlockSpec(memory_space=pltpu.SMEM)]
        + [tile(a) for a in grads[:-1]]
        + [whole(grads[-1])]
        + [whole(a) for a in totals]
        + specs,
        out_specs=specs + [whole(norm_out)],
        compiler_params=FULL,
    )(coordinates(), *grads, *totals, *state)


def coordinates():
    return jnp.stack([lax.axis_index(name) for name in ("z", "y", "x", "c")]).astype(jnp.int32)


def chip_of(coords, rel, depth, back):
    dz, dy, dx = rel
    z, y, x = coords[0], coords[1], coords[2]
    zz = lax.rem(z + (depth - dz if back else dz), depth)
    yy = 1 - y if dy else y
    xx = 1 - x if dx else x
    return zz, yy * 2 + xx


def window(row, rows, col, cols):
    rows_at = pl.ds(row if isinstance(row, int) else pl.multiple_of(row, 16), rows)
    return rows_at, pl.ds(col, cols)


VMEM = pl.BlockSpec(memory_space=pltpu.VMEM)
ROOM_MB = 16
ROOM = pltpu.CompilerParams(vmem_limit_bytes=ROOM_MB * 1024 * 1024)
FULL = pltpu.CompilerParams(vmem_limit_bytes=56 * 1024 * 1024)


def place(parts, depth, outs, spots, moves, deps=()):
    def kernel(coords, *refs):
        ins, out_refs = refs[: len(parts)], refs[len(parts) + len(deps) :]
        for array, lead, base, rel in spots:
            zz, plane = chip_of(coords, rel, depth, True)
            for o, sr, sc, rows, cols, tr, tc in moves(zz, plane):
                out_refs[o][window(tr, rows, tc, cols)] = ins[array][(*lead, *window(base + sr, rows, sc, cols))]

    return pl.pallas_call(
        kernel,
        out_shape=[jax.ShapeDtypeStruct(s, LOW) for s in outs],
        in_specs=[pl.BlockSpec(memory_space=pltpu.SMEM)]
        + [VMEM] * len(parts)
        + [pl.BlockSpec(memory_space=pl.ANY)] * len(deps),
        out_specs=[VMEM] * len(outs),
        compiler_params=ROOM,
    )(coordinates(), *parts, *deps)


def unplace(grads, depth, rows_cols, moves):
    spots = []
    for dz in range(depth):
        for d in range(2):
            spots += [(0, d, dz, (dz, d, 1), 0), (1, d, dz, (dz, d, 0), 0)]
            spots += [(2, d, dz, (dz, 1, d), 1), (3, d, dz, (dz, 0, d), 1)]

    def kernel(coords, *refs):
        ins, out_refs = refs[: len(grads)], refs[len(grads) :]
        for array, d, dz, rel, half in spots:
            zz, plane = chip_of(coords, rel, depth, False)
            for i, sr, sc, rows, cols, tr, tc in moves(zz, plane, half):
                out_refs[array][(d, dz, *window(tr, rows, tc, cols))] = ins[i][window(sr, rows, sc, cols)]

    return pl.pallas_call(
        kernel,
        out_shape=[jax.ShapeDtypeStruct((2, depth) + rows_cols, LOW)] * 4,
        in_specs=[pl.BlockSpec(memory_space=pltpu.SMEM)] + [VMEM] * len(grads),
        out_specs=[VMEM] * 4,
        compiler_params=ROOM,
    )(coordinates(), *grads)


def cast_qkv(qkv, norm, halves):
    rows, cols = qkv.shape
    wide = cols // 2 + LANES
    block = cols // (2 * halves)

    def kernel(coords, qkv_ref, norm_ref, own_ref, mate_ref, tall):
        first = coords[3] == 0
        for j in range(halves):
            a = qkv_ref[:, 2 * j * block : (2 * j + 1) * block]
            b = qkv_ref[:, (2 * j + 1) * block : (2 * j + 2) * block]
            own_ref[:, j * block : (j + 1) * block] = jnp.where(first, a, b).astype(LOW)
            mate_ref[:, j * block : (j + 1) * block] = jnp.where(first, b, a).astype(LOW)
        tall[...] = jnp.zeros_like(tall)
        tall[0:4, :] = norm_ref[...].astype(LOW).astype(WIDE)
        i = lax.broadcasted_iota(jnp.int32, (rows, rows), 0)
        j = lax.broadcasted_iota(jnp.int32, (rows, rows), 1)
        columns = dot_cols((i == j).astype(LOW), tall[...].astype(LOW)).astype(LOW)
        own_ref[:, cols // 2 :] = columns
        mate_ref[:, cols // 2 :] = columns

    return pl.pallas_call(
        kernel,
        out_shape=[jax.ShapeDtypeStruct((rows, wide), LOW)] * 2,
        in_specs=[pl.BlockSpec(memory_space=pltpu.SMEM), VMEM, VMEM],
        out_specs=[VMEM] * 2,
        scratch_shapes=[pltpu.VMEM((LANES, rows), WIDE)],
        compiler_params=ROOM,
    )(coordinates(), qkv, norm)


def cast_rest(up, out, down, halves):
    rows, cols = up.shape
    block, width = cols // (2 * halves), out.shape[1]

    def kernel(coords, up_ref, out_ref, down_ref, own_ref, mate_ref, part_ref, low_ref):
        first = coords[3] == 0
        for j in range(halves):
            a = up_ref[:, 2 * j * block : (2 * j + 1) * block]
            b = up_ref[:, (2 * j + 1) * block : (2 * j + 2) * block]
            own_ref[:, j * block : (j + 1) * block] = jnp.where(first, a, b).astype(LOW)
            mate_ref[:, j * block : (j + 1) * block] = jnp.where(first, b, a).astype(LOW)
        part_ref[:rows, :] = out_ref[:, : width // 2].astype(LOW)
        part_ref[rows:, :] = out_ref[:, width // 2 :].astype(LOW)
        low_ref[...] = down_ref[...].astype(LOW)

    return pl.pallas_call(
        kernel,
        out_shape=[jax.ShapeDtypeStruct((rows, cols // 2), LOW)] * 2
        + [jax.ShapeDtypeStruct((2 * rows, width // 2), LOW), jax.ShapeDtypeStruct(down.shape, LOW)],
        in_specs=[pl.BlockSpec(memory_space=pltpu.SMEM), VMEM, VMEM, VMEM],
        out_specs=[VMEM] * 4,
        compiler_params=ROOM,
    )(coordinates(), up, out, down)


def join_rows(own, mate, side=None):
    rows, cols = own.shape
    wide = cols + (side.shape[1] if side is not None else 0)

    def kernel(coords, own_ref, mate_ref, *refs):
        out_ref = refs[-1]
        core = coords[3]
        out_ref[pl.ds(pl.multiple_of(core * rows, 16), rows), :cols] = own_ref[...]
        out_ref[pl.ds(pl.multiple_of((1 - core) * rows, 16), rows), :cols] = mate_ref[...]
        if side is not None:
            out_ref[:, cols:] = refs[0][...]

    ins = [own, mate] + ([side] if side is not None else [])
    return pl.pallas_call(
        kernel,
        out_shape=jax.ShapeDtypeStruct((2 * rows, wide), LOW),
        in_specs=[pl.BlockSpec(memory_space=pltpu.SMEM)] + [VMEM] * len(ins),
        out_specs=VMEM,
        compiler_params=ROOM,
    )(coordinates(), *ins)


def run(kernel, outs, *ins, scalars=True, scratch=(), flops=0, room=ROOM_MB, deps=()):
    first = len(ins) + scalars

    def body_of(*refs):
        return kernel(*refs[:first], *refs[first + len(deps) :])

    out_shape = [jax.ShapeDtypeStruct(shape, kind) for shape, kind in outs]
    return pl.pallas_call(
        body_of,
        out_shape=out_shape,
        in_specs=([pl.BlockSpec(memory_space=pltpu.SMEM)] if scalars else [])
        + [VMEM] * len(ins)
        + [pl.BlockSpec(memory_space=pl.ANY)] * len(deps),
        out_specs=[VMEM] * len(outs),
        scratch_shapes=list(scratch),
        compiler_params=pltpu.CompilerParams(vmem_limit_bytes=room * 1024 * 1024),
        cost_estimate=pl.CostEstimate(flops=flops, bytes_accessed=0, transcendentals=0),
    )(*([coordinates()] if scalars else []), *ins, *deps)


def dot(left, right):
    return jnp.dot(left, right, preferred_element_type=WIDE)


def dot_rows(left, right):
    return lax.dot_general(left, right, (((0,), (0,)), ((), ())), preferred_element_type=WIDE)


def dot_cols(left, right):
    return lax.dot_general(left, right, (((1,), (1,)), ((), ())), preferred_element_type=WIDE)


def eye(rows, cols):
    i = lax.broadcasted_iota(jnp.int32, (rows, cols), 0)
    return (i == lax.broadcasted_iota(jnp.int32, (rows, cols), 1)).astype(LOW)


def normalise(values):
    center = values - jnp.mean(values, axis=-1, keepdims=True)
    rate = lax.rsqrt(jnp.mean(center * center, axis=-1, keepdims=True) + NORM_EPS)
    return center * rate, rate


def norm_back(normed, rate, grad, gain):
    scaled = grad * gain
    shared = jnp.mean(scaled, axis=-1, keepdims=True)
    along = jnp.mean(scaled * normed, axis=-1, keepdims=True)
    return rate * (scaled - shared - normed * along)


def low_lanes(rows):
    return lax.broadcasted_iota(jnp.int32, (rows, LANES), 1) < HEAD_DIM


def by_head(pair):
    wide = pair.astype(WIDE)
    first = low_lanes(pair.shape[0])
    return jnp.where(first, wide, 0.0).astype(LOW), jnp.where(first, 0.0, wide).astype(LOW)


def pack_state(square):
    first = low_lanes(HEAD_DIM)
    return jnp.where(first, square[:HEAD_DIM], square[HEAD_DIM:])


def open_state(packed):
    first = low_lanes(HEAD_DIM)
    return jnp.concatenate([jnp.where(first, packed, 0.0), jnp.where(first, 0.0, packed)])


def feature(values):
    return jnp.where(values > 0.0, values + 1.0, jnp.exp(jnp.minimum(values, 0.0)))


def project(x, norm_w, qkv_w):
    tokens, width = x.shape
    half = qkv_w.shape[1] // 3
    pairs = half // LANES
    step = tokens // 2

    def kernel(x_ref, norm_ref, w_ref, rows_ref, normed_ref, qk_ref, q_ref, k_ref, v_ref, state_ref, sums):
        rows_ref[...] = dot_cols(eye(8, LANES), norm_ref[...])
        gain, bias = rows_ref[0:1, :], rows_ref[1:2, :]
        @pl.loop(0, 2)
        def _(i):
            at = at_block(i, step)
            normed = normalise(x_ref[at, :].astype(WIDE))[0]
            normed_ref[at, :] = (normed * gain + bias).astype(LOW)
            low = normed_ref[at, :]
            for j, out in enumerate((q_ref, k_ref)):
                part = dot(low, w_ref[:, j * half : (j + 1) * half])
                qk_ref[at, j * half : (j + 1) * half] = part
                out[at, :] = feature(part).astype(LOW)
            v_ref[at, :] = dot(low, w_ref[:, 2 * half :]).astype(LOW)
        total = dot_rows(jnp.ones((tokens, 8), LOW), k_ref[...])
        sums[...] = jnp.zeros_like(sums)
        for p in range(pairs):
            lanes = slice(p * LANES, (p + 1) * LANES)
            packed = pack_state(dot_rows(k_ref[:, lanes], v_ref[:, lanes]))
            state_ref[p * HEAD_DIM : (p + 1) * HEAD_DIM, :] = packed.astype(LOW)
            sums[p : p + 1, :] = total[0:1, lanes]
        state_ref[pairs * HEAD_DIM :, :] = sums[...].astype(LOW)

    outs = [((8, width), WIDE), ((tokens, width), LOW), ((tokens, 2 * half), WIDE)] + [((tokens, half), LOW)] * 3
    outs += [((pairs * HEAD_DIM + 16, LANES), LOW)]
    scratch = [pltpu.VMEM((16, LANES), WIDE)]
    return run(kernel, outs, x, norm_w, qkv_w, scalars=False, scratch=scratch)


def at_block(index, size):
    return pl.ds(pl.multiple_of(index * size, size), size)


def total_state(refs):
    total = refs[0][...].astype(WIDE)
    for ref in refs[1:]:
        total = total + ref[...].astype(WIDE)
    return total


def causal_mask(step):
    i = lax.broadcasted_iota(jnp.int32, (step, step), 0)
    return i >= lax.broadcasted_iota(jnp.int32, (step, step), 1)


def attend(query, key, value, parts, deps=()):
    tokens, half = query.shape
    pairs, step = half // LANES, tokens // 2

    def kernel(q_ref, k_ref, v_ref, *refs):
        mixed_ref, low_ref, denom_ref, state_ref, token_ref = refs[len(parts) :]
        token_ref[...] = jnp.zeros_like(token_ref)
        state_ref[...] = total_state(refs[: len(parts)])
        lower = causal_mask(step)
        first = low_lanes(step)
        top = low_lanes(HEAD_DIM)
        diagonal = eye(LANES, LANES).astype(WIDE)
        @pl.loop(0, pairs)
        def _(p):
            lanes = at_block(p, LANES)
            packed = state_ref[at_block(p, HEAD_DIM), :]
            sums = state_ref[pl.ds(pairs * HEAD_DIM + p, 1), :]
            column = jnp.sum(diagonal * sums, axis=1, keepdims=True)
            zero = jnp.zeros((HEAD_DIM, LANES), WIDE)
            ext = (
                jnp.concatenate([jnp.where(top, packed, column[:HEAD_DIM]), zero]).astype(LOW),
                jnp.concatenate([zero, jnp.where(top, column[HEAD_DIM:], packed)]).astype(LOW),
            )
            wide = v_ref[:, lanes].astype(WIDE)
            full = low_lanes(tokens)
            value_ext = (jnp.where(full, wide, 1.0).astype(LOW), jnp.where(full, 1.0, wide).astype(LOW))
            queries = by_head(q_ref[:, lanes])
            for i in range(2):
                at = slice(i * step, (i + 1) * step)
                got = []
                for h in range(2):
                    rows = queries[h][at]
                    total = dot(rows, ext[h])
                    for j in range(i + 1):
                        to = slice(j * step, (j + 1) * step)
                        scores = dot_cols(rows, k_ref[to, lanes])
                        if j == i:
                            scores = jnp.where(lower, scores, 0.0)
                        total = total + dot(scores.astype(LOW), value_ext[h][to])
                    got.append(total)
                denom = pltpu.roll(jnp.where(first, got[1], got[0]), HEAD_DIM, 1)
                mixed = jnp.where(first, got[0], got[1]) / denom
                mixed_ref[at, lanes] = mixed
                low_ref[at, lanes] = mixed.astype(LOW)
                denom_ref[at, lanes] = denom

    outs = [((tokens, half), WIDE), ((tokens, half), LOW), ((tokens, half), WIDE), (parts[0].shape, WIDE)]
    outs += [((8, LANES), WIDE)]
    return run(kernel, outs, query, key, value, *parts, scalars=False, deps=deps)


def out_project(mixed, out_w):
    def kernel(mixed_ref, w_ref, part_ref, low_ref):
        part = dot(mixed_ref[...], w_ref[...])
        part_ref[...] = part
        low_ref[...] = part.astype(LOW)

    shape = (mixed.shape[0], out_w.shape[1])
    return run(kernel, [(shape, WIDE), (shape, LOW)], mixed, out_w, scalars=False)


def feed(x, part, got, rows, up_w):
    tokens, width = x.shape
    units, step, cut = up_w.shape[1], tokens // 2, 512

    def kernel(x_ref, part_ref, got_ref, rows_ref, w_ref, resid_ref, normed_ref, act_ref, slope_ref):
        @pl.loop(0, 2)
        def _(i):
            at = at_block(i, step)
            resid = x_ref[at, :].astype(WIDE) + part_ref[at, :] + got_ref[at, :].astype(WIDE)
            resid_ref[at, :] = resid
            normed_ref[at, :] = (normalise(resid)[0] * rows_ref[2:3, :] + rows_ref[3:4, :]).astype(LOW)

        @pl.loop(0, units // cut)
        def _(j):
            to = at_block(j, cut)
            v = dot(normed_ref[...], w_ref[:, to])
            root = (2.0 / 3.141592653589793) ** 0.5
            square = v * v
            bend = jnp.tanh(root * v * (1.0 + 0.044715 * square))
            cdf = 0.5 * (1.0 + bend)
            act_ref[:, to] = (v * cdf).astype(LOW)
            slope_ref[:, to] = cdf + 0.5 * v * (1.0 - bend * bend) * (root * (1.0 + 3.0 * 0.044715 * square))

    outs = [((tokens, width), WIDE), ((tokens, width), LOW), ((tokens, units), LOW), ((tokens, units), WIDE)]
    return run(kernel, outs, x, part, got, rows, up_w, scalars=False)


def feed_back(grad_out, down_w, slope, up_w):
    tokens, width = grad_out.shape
    units, cut = up_w.shape[1], 512

    def kernel(g_ref, down_ref, slope_ref, up_ref, hidden_ref, part_ref, low_ref):
        @pl.loop(0, units // cut)
        def _(j):
            to = at_block(j, cut)
            hidden_ref[:, to] = (dot_cols(g_ref[...], down_ref[to, :]) * slope_ref[:, to]).astype(LOW)

        @pl.loop(0, width // cut)
        def _(j):
            to = at_block(j, cut)
            part = dot_cols(hidden_ref[...], up_ref[to, :])
            part_ref[:, to] = part
            low_ref[:, to] = part.astype(LOW)

    outs = [((tokens, units), LOW), ((tokens, width), WIDE), ((tokens, width), LOW)]
    return run(kernel, outs, grad_out, down_w, slope, up_w, scalars=False)


def down_project(activated, down_w, resid, deps):
    tokens, width = resid.shape
    group, cut = tokens // 2, width // 2

    def kernel(coords, act_ref, w_ref, resid_ref, own_ref, give_ref):
        own = pl.ds(pl.multiple_of(coords[3] * group, 16), group)
        mate = pl.ds(pl.multiple_of((1 - coords[3]) * group, 16), group)

        @pl.loop(0, 2)
        def _(j):
            to = at_block(j, cut)
            own_ref[:, to] = resid_ref[own, to] + dot(act_ref[own, :], w_ref[:, to])
            give_ref[:, to] = dot(act_ref[mate, :], w_ref[:, to]).astype(LOW)

    outs = [((group, width), WIDE), ((group, width), LOW)]
    return run(kernel, outs, activated, down_w, resid, deps=deps)


def weight_grad(rows, grad, deps=()):
    tokens, width = rows.shape
    units, cut = grad.shape[1], 512

    def kernel(rows_ref, grad_ref, out_ref):
        @pl.loop(0, units // cut)
        def _(j):
            to = at_block(j, cut)
            out_ref[:, to] = dot_rows(rows_ref[...], grad_ref[:, to]).astype(LOW)

    return run(kernel, [((width, units), LOW)], rows, grad, scalars=False, deps=deps)[0]


def attend_turn(part, got, resid, rows, grad_out, out_w, mixed, denom, query):
    tokens, width = resid.shape
    half = mixed.shape[1]
    pairs, step = half // LANES, tokens // 2

    def kernel(
        part_ref, got_ref, resid_ref, rows_ref, g_ref, w_ref, mixed_ref, denom_ref, q_ref,
        grad_ref, low_ref, a_ref, b_ref, state_ref, norm_ref, sums,
    ):
        gain = rows_ref[2:3, :]
        first = low_lanes(step)
        norm_ref[...] = jnp.zeros_like(norm_ref)

        @pl.loop(0, 2)
        def _(i):
            at = at_block(i, step)
            normed, rate = normalise(resid_ref[at, :])
            own = part_ref[at, :]
            norm_ref[0:1, :] += jnp.sum(own * normed, axis=0, keepdims=True)
            norm_ref[1:2, :] += jnp.sum(own, axis=0, keepdims=True)
            grad = g_ref[at, :].astype(WIDE) + norm_back(normed, rate, own + got_ref[at, :].astype(WIDE), gain)
            grad_ref[at, :] = grad
            low_ref[at, :] = grad.astype(LOW)
            turned = dot_cols(low_ref[at, :], w_ref[...]) / denom_ref[at, :]
            a_ref[at, :] = turned.astype(LOW)
            along = turned * mixed_ref[at, :]
            for p in range(pairs):
                lanes = slice(p * LANES, (p + 1) * LANES)
                piece = along[:, lanes]
                low = jnp.sum(jnp.where(first, piece, 0.0), axis=1, keepdims=True)
                high = jnp.sum(jnp.where(first, 0.0, piece), axis=1, keepdims=True)
                b_ref[at, lanes] = -jnp.where(first, low, high)
        sums[...] = jnp.zeros_like(sums)
        for p in range(pairs):
            lanes = slice(p * LANES, (p + 1) * LANES)
            packed = pack_state(dot_rows(q_ref[:, lanes], a_ref[:, lanes]))
            state_ref[p * HEAD_DIM : (p + 1) * HEAD_DIM, :] = packed.astype(LOW)
            sums[p : p + 1, :] = jnp.sum(q_ref[:, lanes].astype(WIDE) * b_ref[:, lanes], axis=0, keepdims=True)
        state_ref[pairs * HEAD_DIM :, :] = sums[...].astype(LOW)

    outs = [((tokens, width), WIDE), ((tokens, width), LOW), ((tokens, half), LOW), ((tokens, half), WIDE)]
    outs += [((pairs * HEAD_DIM + 16, LANES), LOW), ((2, width), WIDE)]
    ins = (part, got, resid, rows, grad_out, out_w, mixed, denom, query)
    scratch = [pltpu.VMEM((16, LANES), WIDE)]
    return run(kernel, outs, *ins, scalars=False, scratch=scratch)


def attend_back(query, key, value, qk, a_low, b_rows, state, parts, deps=()):
    tokens, half = query.shape
    pairs, step = half // LANES, tokens // 2

    def kernel(q_ref, k_ref, v_ref, qk_ref, a_ref, b_ref, state_ref, *refs):
        out_ref, later = refs[len(parts) :]
        later[...] = total_state(refs[: len(parts)])
        lower = causal_mask(step)
        @pl.loop(0, pairs)
        def _(p):
            lanes, rows = at_block(p, LANES), at_block(p, HEAD_DIM)
            sums = pl.ds(pairs * HEAD_DIM + p, 1)
            before, after_it = open_state(state_ref[rows, :]).astype(LOW), open_state(later[rows, :]).astype(LOW)
            queries, keys, pulls = by_head(q_ref[:, lanes]), by_head(k_ref[:, lanes]), by_head(a_ref[:, lanes])
            cuts = [slice(i * step, (i + 1) * step) for i in range(2)]
            grad_q = [dot_cols(a_ref[c, lanes], before) + b_ref[c, lanes] * state_ref[sums, :] for c in cuts]
            grad_k = [dot_cols(v_ref[c, lanes], after_it) + later[sums, :] for c in cuts]
            shifts = b_ref[:, lanes]
            grad_v = [dot(k_ref[c, lanes], after_it) for c in cuts]
            for i in range(2):
                for j in range(i + 1):
                    for h in range(2):
                        q, a = queries[h][cuts[i]], pulls[h][cuts[i]]
                        b = shifts[cuts[i], h * HEAD_DIM : h * HEAD_DIM + 1]
                        scores = dot_cols(q, k_ref[cuts[j], lanes])
                        pull = dot_cols(a, v_ref[cuts[j], lanes]) + b
                        if j == i:
                            scores, pull = jnp.where(lower, scores, 0.0), jnp.where(lower, pull, 0.0)
                        scores, pull = scores.astype(LOW), pull.astype(LOW)
                        grad_q[i] = grad_q[i] + dot(pull, keys[h][cuts[j]])
                        grad_k[j] = grad_k[j] + dot_rows(pull, q)
                        grad_v[j] = grad_v[j] + dot_rows(scores, a)
            for i, c in enumerate(cuts):
                for n, grad in enumerate((grad_q[i], grad_k[i])):
                    at = at_block(n * pairs + p, LANES)
                    raw = qk_ref[c, at]
                    out_ref[c, at] = (grad * jnp.where(raw > 0.0, 1.0, jnp.exp(jnp.minimum(raw, 0.0)))).astype(LOW)
                out_ref[c, at_block(2 * pairs + p, LANES)] = grad_v[i].astype(LOW)

    ins = (query, key, value, qk, a_low, b_rows, state, *parts)
    scratch = [pltpu.VMEM(parts[0].shape, WIDE)]
    return run(kernel, [((tokens, 3 * half), LOW)], *ins, scalars=False, scratch=scratch, deps=deps)[0]


def project_back(grad, qkv_w, x, norm_two):
    tokens, width = x.shape
    step = tokens // 2

    def kernel(grad_ref, w_ref, x_ref, two_ref, part_ref, low_ref, cols_ref, rows):
        rows[...] = jnp.zeros_like(rows)

        @pl.loop(0, 2)
        def _(i):
            at = at_block(i, step)
            part = dot_cols(grad_ref[at, :], w_ref[...])
            part_ref[at, :] = part
            low_ref[at, :] = part.astype(LOW)
            rows[0:1, :] += jnp.sum(part * normalise(x_ref[at, :].astype(WIDE))[0], axis=0, keepdims=True)
            rows[1:2, :] += jnp.sum(part, axis=0, keepdims=True)

        rows[2:4, :] = two_ref[...]
        cols_ref[...] = dot_rows(rows[...].astype(LOW), eye(8, LANES)).astype(LOW)

    outs = [((tokens, width), WIDE), ((tokens, width), LOW), ((width, LANES), LOW)]
    scratch = [pltpu.VMEM((8, width), WIDE)]
    return run(kernel, outs, grad, qkv_w, x, norm_two, scalars=False, scratch=scratch)


def input_back(part, got, grad_resid, own_x, rows):
    group, width = own_x.shape

    def kernel(coords, part_ref, got_ref, resid_ref, x_ref, rows_ref, out_ref):
        at = pl.ds(pl.multiple_of(coords[3] * group, 16), group)
        normed, rate = normalise(x_ref[...].astype(WIDE))
        grad = part_ref[at, :] + got_ref[...].astype(WIDE)
        out_ref[...] = (resid_ref[at, :] + norm_back(normed, rate, grad, rows_ref[0:1, :])).astype(LOW)

    return run(kernel, [((group, width), LOW)], part, got, grad_resid, own_x, rows)[0]


def adam_update(weight, first, second, grad, rate, decay):
    first_new = BETA_ONE * first + (1.0 - BETA_ONE) * grad
    second_new = BETA_TWO * second + (1.0 - BETA_TWO) * grad * grad
    first_hat = first_new / (1.0 - BETA_ONE**STEP)
    second_hat = second_new / (1.0 - BETA_TWO**STEP)
    weight_new = weight - rate * (first_hat / (jnp.sqrt(second_hat) + ADAM_EPS) + decay * weight)
    return (weight_new, first_new, second_new)


def from_others(low, step):
    if lax.axis_size("z") == 4:
        near = shift(low, step, wrap=False)
        pair = (low.astype(WIDE) + near.astype(WIDE)).astype(LOW)
        return [near, shift(pair, 2 * step, wrap=False)]
    return [shift(low, step * k, wrap=False) for k in range(1, lax.axis_size("z"))]


def body(
    images,
    cotangent,
    qkv_weight,
    out_weight,
    up_weight,
    down_weight,
    norm_params,
    qkv_first,
    out_first,
    up_first,
    down_first,
    norm_first,
    qkv_second,
    out_second,
    up_second,
    down_second,
    norm_second,
):
    depth, core = lax.axis_size("z"), lax.axis_index("c")
    count, group, width = images.shape
    hidden_units = up_weight.shape[1]
    own_rows = qkv_weight.shape[0]
    own_units = down_weight.shape[0]
    chips = lax.axis_size("y") * lax.axis_size("x")
    block, ff_block = width // (2 * depth), hidden_units // (2 * depth)
    half_qkv, half_ff, half_d = 3 * width // 2, hidden_units // 2, width // 2
    ring = lax.axis_size("y") == 2 and lax.axis_size("x") == 2 and depth == 4 and own_rows % 32 == 0
    heads = half_d // HEAD_DIM
    tokens = 2 * group

    own_x, own_g = images.reshape(group, width), cotangent.reshape(group, width)
    split_qkv = lambda w: jnp.moveaxis(w.reshape(-1, 3 * depth, 2, block), 2, 0).reshape(2, -1, half_qkv)
    split_up = lambda w: jnp.moveaxis(w.reshape(-1, depth, 2, ff_block), 2, 0).reshape(2, -1, half_ff)

    thin, small = own_units // 2, own_rows // 2
    if ring:
        qkv_mine, qkv_give = cast_qkv(qkv_weight, norm_params, 3 * depth)
        qkv_part = join_rows(qkv_mine, swap(qkv_give, "c"))
        up_mine, up_give, out_part, down_low = cast_rest(
            after(up_weight, qkv_part), out_weight, down_weight, depth
        )
        inputs = join_rows(own_x, swap(own_x, "c"))
        up_part = join_rows(up_mine, swap(up_give, "c"), out_part)
        qkv_column = column_first(qkv_part)
        down_plane = plane_first(after(down_low, qkv_part))
        qkv_column = [after(part, down_plane, up_part, inputs) for part in qkv_column]
        up_column = column_first(after(up_part, *qkv_column))
        qkv_parts = plane_last(jnp.stack(qkv_column))
        g_mate = swap(after(own_g, *up_column), "c")
        down_parts = [down_plane, shift(after(down_plane, *up_column), 1)]

        def qkv_moves(zz, plane):
            row = lambda h: ((zz * 2 + h) * chips + plane) * own_rows
            moves = [(0, h * own_rows, 0, own_rows, half_qkv, row(h), 0) for h in (0, 1)]
            return moves + [(1, h * own_rows, half_qkv, own_rows, LANES, row(h), 0) for h in (0, 1)]

        def up_moves(zz, plane):
            row = lambda h: ((zz * 2 + h) * chips + plane) * own_rows
            moves = [(0, h * own_rows, 0, own_rows, half_ff, row(h), 0) for h in (0, 1)]
            to = zz * block + plane * own_rows
            return moves + [(1, h * own_rows, half_ff, own_rows, half_d, to, h * half_d) for h in (0, 1)]

        def down_moves(zz, plane):
            return [(0, 0, 0, own_units, width, zz * ff_block + plane * own_units, 0)]

        spots = column_first_spots(depth)
        qkv_w, norm_w = place(qkv_parts, depth, [(width, half_qkv), (width, LANES)], spots, qkv_moves)
    else:
        qkv_low, out_low = qkv_weight.astype(LOW), out_weight.astype(LOW)
        up_low, down_low = up_weight.astype(LOW), down_weight.astype(LOW)
        norm_low = norm_params.astype(LOW)
        x_mate, g_mate = swap(own_x, "c"), swap(own_g, "c")
        whole = lambda w, axis=0: lax.all_gather(w, ALL, axis=axis, tiled=True)
        qkv_w, up_w = mine(split_qkv(whole(qkv_low))), mine(split_up(whole(up_low)))
        rows_half = lambda w, b: mine(jnp.moveaxis(w.reshape(depth, 2, b, width), 1, 0)).reshape(-1, width)
        out_w, down_w = rows_half(whole(out_low), block), rows_half(whole(down_low), ff_block)
        norm_w = jnp.pad(whole(norm_low, 1).T, ((0, 0), (0, LANES - 4)))

        inputs = join_rows(own_x, x_mate)
    grad_out = join_rows(own_g, g_mate)
    halves = lambda a: a.reshape(2, group, -1)
    rows, normed_one, qk, query, key, value, state = project(inputs, norm_w, qkv_w)
    earlier = from_others(state, 1)
    mixed, mixed_low, denom, state_in, attended = attend(query, key, value, earlier, (grad_out,))
    if ring:
        up_parts = plane_last(after(jnp.stack(up_column), *qkv_parts[3:]), tuple(earlier))
        down_parts.append(shift(after(down_parts[-1], *earlier), 1))
        for _ in range(3, depth):
            down_parts.append(shift(down_parts[-1], 1))
        up_w, out_w = place(
            up_parts, depth, [(width, half_ff), (half_d, width)], spots, up_moves, down_parts[2:3]
        )
    out_part, out_low = out_project(mixed_low, out_w)
    out_got = swap(out_low, "c")
    resid, normed_two, activated, slope = feed(inputs, out_part, out_got, rows, up_w)
    down_grad = dot_rows(activated, grad_out).astype(LOW)
    if ring:
        def down_cuts(zz, plane, half):
            return [(0, zz * ff_block + plane * own_units + half * thin, 0, thin, width, 0, 0)]

        down_cut = unplace([down_grad], depth, (thin, width), down_cuts)
        down_hop = first_hop(*down_cut)
        spots = plane_first_spots(depth, own_units)
        (down_w,) = place(down_parts, depth, [(half_ff, width)], spots, down_moves, (down_cut[0],))

    grad_hidden, two_part, two_low = feed_back(grad_out, down_w, slope, up_w)
    down_own, down_give = down_project(activated, down_w, resid, (two_low,))
    down_got = swap(down_give, "c")
    activations = (down_own + down_got.astype(WIDE)).astype(LOW)
    up_grad = weight_grad(normed_two, grad_hidden, down_hop[1::2] if ring else ())
    two_got = after(swap(two_low, "c"), up_grad)
    grad_resid, grad_resid_low, a_low, b_rows, state_grad, norm_two = attend_turn(
        two_part, two_got, resid, rows, grad_out, out_w, mixed, denom, query
    )
    later = from_others(state_grad, -1)
    out_grad = dot_rows(mixed_low, grad_resid_low).astype(LOW)
    deps = ()
    if ring:

        def up_cuts(zz, plane, half):
            cuts = [(0, ((zz * 2 + half) * chips + plane) * own_rows, 0, own_rows, half_ff, 0, 0)]
            row = zz * block + plane * own_rows + half * small
            return cuts + [(1, row, p * half_d, small, half_d, p * small, half_ff) for p in (0, 1)]

        up_cut = unplace([up_grad, out_grad], depth, (own_rows, half_ff + half_d), up_cuts)
        deps = (up_cut[0],)
    grad_projected = attend_back(query, key, value, qk, a_low, b_rows, state_in, later, deps)
    qkv_grad = dot_rows(normed_one, grad_projected).astype(LOW)
    one_part, one_low, norm_cols = project_back(grad_projected, qkv_w, inputs, norm_two)
    input_grad = input_back(one_part, swap(other(halves(one_low)), "c"), grad_resid, own_x, rows)

    out_fan = max(1, width * 64 // (tokens * depth))
    rates = (3.0 * width**-0.5, 3.0 * out_fan**-0.5, 3.0 * width**-0.5, 3.0 * hidden_units**-0.5, 1.5)
    decays = (WEIGHT_DECAY, WEIGHT_DECAY, WEIGHT_DECAY, WEIGHT_DECAY, 0.0)
    masters = (qkv_weight, out_weight, up_weight, down_weight, norm_params)
    firsts = (qkv_first, out_first, up_first, down_first, norm_first)
    seconds = (qkv_second, out_second, up_second, down_second, norm_second)
    if ring:

        def qkv_cuts(zz, plane, half):
            row = ((zz * 2 + half) * chips + plane) * own_rows
            return [(0, row, 0, own_rows, half_qkv, 0, 0), (1, row, 0, own_rows, LANES, 0, half_qkv)]

        down_sum, hop = later_hops(*down_hop)
        up_sum, hop = later_hops(*first_hop(*up_cut, (*hop, *later)), (*down_sum[1:], grad_projected))
        qkv_cut = unplace([qkv_grad, norm_cols], depth, (own_rows, half_qkv + LANES), qkv_cuts)
        qkv_sum, hop = later_hops(*first_hop(*qkv_cut, hop), (), up_sum[1:])
        down_red, squares = finish_down(down_sum)
        up_mine, up_give, out_red, squares = finish_up(up_sum, squares, own_rows, half_ff)
        up_mate = swap(up_give, "c")
        deps = (input_grad, activations, up_mate)
        qkv_mine, qkv_give, small_mine = finish_qkv(qkv_sum, squares, own_rows, half_qkv, deps)
        small_mate, qkv_mate = swap(small_mine, "c"), swap(qkv_give, "c")
        squares, norm_sum = chip_squares(small_mine, small_mate)
        norm_red = mine(norm_sum.reshape(2, own_rows, LANES))[:, :4].T
        grads = (qkv_mine, qkv_mate, out_red, up_mine, up_mate, down_red, norm_red)
        *news, grad_norm = update_all(
            grads, sum_chips(squares), masters, firsts, seconds, rates, decays, (3 * depth, depth)
        )
        return (
            activations.reshape(count, group, width),
            input_grad.reshape(count, group, width),
            grad_norm.reshape(()),
            *news,
        )
    scatter = lambda g: lax.psum_scatter(g, ALL, scatter_dimension=0, tiled=True)
    both = lambda a, axis: jnp.stack([jnp.where(core == k, a, 0.0) for k in (0, 1)], axis)
    to_all = lambda a: a.astype(WIDE)
    qkv_red = scatter(both(to_all(qkv_grad).reshape(width, 3 * depth, block), 2).reshape(width, -1))
    up_red = scatter(both(to_all(up_grad).reshape(width, depth, ff_block), 2).reshape(width, -1))
    out_red = scatter(both(to_all(out_grad).reshape(depth, block, width), 1).reshape(width, width))
    down_red = scatter(both(to_all(down_grad).reshape(depth, ff_block, width), 1).reshape(hidden_units, width))
    norm_red = scatter(norm_cols.astype(WIDE))[:, :4].T

    reduced = (qkv_red, out_red, up_red, down_red, norm_red)
    local_squares = sum(jnp.sum(grad * grad) for grad in reduced)
    grad_norm = jnp.sqrt(lax.psum(local_squares, ALL))
    clip = jnp.minimum(1.0, CLIP_LIMIT / (grad_norm + 1e-06))
    news = [
        adam_update(masters[k], firsts[k], seconds[k], clip * reduced[k], rates[k], decays[k]) for k in range(5)
    ]
    return (
        activations.reshape(count, group, width),
        input_grad.reshape(count, group, width),
        grad_norm,
        *[new[0] for new in news],
        *[new[1] for new in news],
        *[new[2] for new in news],
    )


def solution(mesh):
    depth, planes = mesh.shape["seq"] // 2, mesh.shape["img"]
    across = max(k for k in range(1, planes + 1) if planes % k == 0 and k * k <= planes)
    grid = jax.sharding.Mesh(mesh.devices.reshape(depth, 2, planes // across, across), ALL)
    tokens = P(("y", "x"), ("z", "c"), None)
    matrix, norm = P(ALL, None), P(None, ALL)
    state = (matrix, matrix, matrix, matrix, norm)
    return jax.shard_map(
        body,
        mesh=grid,
        in_specs=(tokens, tokens) + state * 3,
        out_specs=(tokens, tokens, P()) + state * 3,
        check_vma=False,
    )
```

profile of v0, /device:TPU:0, one launch (start us, length us, event | category | flops | bytes accessed | tf_op | source)
XLA Modules:
  0.0 311.9 jit_solution(8014422556373394731)
XLA Ops:
  13.7 3.6 %collective-permute-start.9 = (bf16[64,1664]{1,0:T(8,128)(2,1)S(1)}, bf16[64,1664]{1,0:T(8,128)(2,1)S(1)}, u32[]{:S(2)}, u32[]{:S(2)}) collective-permute-start(bf16[64,1664]{1,0:T(8,128)(2,1)S(1)} %shard_map.306), channel_id=1, source_target_pairs={{0,24},{8,0},{16,8},{24,16},{1,25},{9,1},{17,9},{25,17},{2,26},{10... | collective-permute-start | bytes 638984 | tf_op jit(solution)/shard_map/ppermute | solution.py:33
  25.8 9.7 %collective-permute-done.8 = bf16[64,1664]{1,0:T(8,128)(2,1)S(1)} collective-permute-done((bf16[64,1664]{1,0:T(8,128)(2,1)S(1)}, bf16[64,1664]{1,0:T(8,128)(2,1)S(1)}, u32[]{:S(2)}, u32[]{:S(2)}) %collective-permute-start.8) | collective-permute-done | bytes 213024 | tf_op jit(solution)/shard_map/ppermute | solution.py:33
  36.8 3.7 %collective-permute-start.18 = (bf16[64,2560]{1,0:T(8,128)(2,1)S(1)}, bf16[64,2560]{1,0:T(8,128)(2,1)S(1)}, u32[]{:S(2)}, u32[]{:S(2)}) collective-permute-start(bf16[64,2560]{1,0:T(8,128)(2,1)S(1)} %shard_map.308), channel_id=1, source_target_pairs={{0,24},{8,0},{16,8},{24,16},{1,25},{9,1},{17,9},{25,17},{2,26},{10... | collective-permute-start | bytes 983048 | tf_op jit(solution)/shard_map/ppermute | solution.py:33
  42.3 13.4 %collective-permute-done.11.refs_2_ = bf16[4,64,1664]{2,1,0:T(8,128)(2,1)S(1)} collective-permute-done((bf16[4,64,1664]{2,1,0:T(8,128)(2,1)S(1)}, bf16[4,64,1664]{2,1,0:T(8,128)(2,1)S(1)}, u32[]{:S(2)}, u32[]{:S(2)}) %collective-permute-start.11) | collective-permute-done | bytes 852000 | tf_op jit(solution)/shard_map/ppermute | solution.py:27
  57.8 10.9 %collective-permute-done.17 = bf16[64,2560]{1,0:T(8,128)(2,1)S(1)} collective-permute-done((bf16[64,2560]{1,0:T(8,128)(2,1)S(1)}, bf16[64,2560]{1,0:T(8,128)(2,1)S(1)}, u32[]{:S(2)}, u32[]{:S(2)}) %collective-permute-start.17) | collective-permute-done | bytes 327712 | tf_op jit(solution)/shard_map/ppermute | solution.py:33
  78.3 14.6 %collective-permute-done.14.refs_3_ = bf16[272,128]{1,0:T(8,128)(2,1)S(1)} collective-permute-done((bf16[272,128]{1,0:T(8,128)(2,1)S(1)}, bf16[272,128]{1,0:T(8,128)(2,1)S(1)}, u32[]{:S(2)}, u32[]{:S(2)}) %collective-permute-start.14) | collective-permute-done | bytes 69664 | tf_op jit(solution)/shard_map/ppermute | solution.py:33
  92.9 6.3 %collective-permute-start.15 = (bf16[272,128]{1,0:T(8,128)(2,1)S(1)}, bf16[272,128]{1,0:T(8,128)(2,1)S(1)}, u32[]{:S(2)}, u32[]{:S(2)}) collective-permute-start(bf16[272,128]{1,0:T(8,128)(2,1)S(1)} %add_convert_fusion.2), channel_id=1, source_target_pairs={{0,16},{8,24},{1,17},{9,25},{2,18},{10,26},{3,19},{11,27},{4,20},{... | collective-permute-start | bytes 208904 | tf_op jit(solution)/shard_map/ppermute | solution.py:33
  105.2 4.8 %shard_map.312 = (f32[512,512]{1,0:T(8,128)S(1)}, bf16[512,512]{1,0:T(8,128)(2,1)S(1)}, f32[512,512]{1,0:T(8,128)S(1)}, f32[272,128]{1,0:T(8,128)S(1)}, f32[8,128]{1,0:T(8,128)}) custom-call(bf16[512,512]{1,0:T(8,128)(2,1)S(1)} %get-tuple-element.148.refs_0_.refs_8_, bf16[512,512]{1,0:T(8,128)(2,1)S(1)} %get-tuple-element.149.refs_1_, ...), custom_call_target="tpu_custom_call" | custom-call | tf_op jit(solution)/shard_map/pallas_call | solution.py:406
  110.0 16.3 %collective-permute-done.25.refs_5_.refs_2_ = bf16[512,1024]{1,0:T(8,128)(2,1)S(1)} collective-permute-done((bf16[512,1024]{1,0:T(8,128)(2,1)S(1)}, bf16[512,1024]{1,0:T(8,128)(2,1)S(1)}, u32[]{:S(2)}, u32[]{:S(2)}) %collective-permute-start.25) | collective-permute-done | bytes 1048608 | tf_op jit(solution)/shard_map/ppermute | solution.py:33
  130.7 5.7 %shard_map.315 = (f32[512,1024]{1,0:T(8,128)S(1)}, bf16[512,1024]{1,0:T(8,128)(2,1)S(1)}, bf16[512,2048]{1,0:T(8,128)(2,1)S(1)}, f32[512,2048]{1,0:T(8,128)S(1)}) custom-call(bf16[512,1024]{1,0:T(8,128)(2,1)S(1)} %shard_map.304.refs_0_.refs_2_, f32[512,1024]{1,0:T(8,128)S(1)} %get-tuple-element.161.refs_1_, ...), custom_call_target="tpu_custom_call" | custom-call | tf_op jit(solution)/shard_map/pallas_call | solution.py:406
  141.4 14.0 %collective-permute-done.27.refs_3_ = bf16[512,1024]{1,0:T(8,128)(2,1)S(1)} collective-permute-done((bf16[512,1024]{1,0:T(8,128)(2,1)S(1)}, bf16[512,1024]{1,0:T(8,128)(2,1)S(1)}, u32[]{:S(2)}, u32[]{:S(2)}) %collective-permute-start.27) | collective-permute-done | bytes 1048608 | tf_op jit(solution)/shard_map/ppermute | solution.py:33
  156.3 5.6 %shard_map.318 = (bf16[512,2048]{1,0:T(8,128)(2,1)S(1)}, f32[512,1024]{1,0:T(8,128)S(1)}, bf16[512,1024]{1,0:T(8,128)(2,1)S(1)}) custom-call(bf16[512,1024]{1,0:T(8,128)(2,1)S(1)} %shard_map.311.refs_5_.refs_0_.refs_4_, bf16[2048,1024]{1,0:T(8,128)(2,1)S(1)} %shard_map.317.refs_1_.refs_2_, f32[512,2048]{1,0:T(8,128)S(1)} %get-tuple-element.168.refs_2_, ...), custom_call_target="tpu_custom_call" | custom-call | tf_op jit(solution)/shard_map/pallas_call | solution.py:406
  161.9 4.0 %collective-permute-done.29.refs_2_.refs_1_ = bf16[2,4,64,1024]{3,2,1,0:T(8,128)(2,1)S(1)} collective-permute-done((bf16[2,4,64,1024]{3,2,1,0:T(8,128)(2,1)S(1)}, bf16[2,4,64,1024]{3,2,1,0:T(8,128)(2,1)S(1)}, u32[]{:S(2)}, u32[]{:S(2)}) %collective-permute-start.29) | collective-permute-done | bytes 1048608 | tf_op jit(solution)/shard_map/ppermute | solution.py:27
  181.8 4.5 %collective-permute-done.33.refs_8_ = bf16[272,128]{1,0:T(8,128)(2,1)S(1)} collective-permute-done((bf16[272,128]{1,0:T(8,128)(2,1)S(1)}, bf16[272,128]{1,0:T(8,128)(2,1)S(1)}, u32[]{:S(2)}, u32[]{:S(2)}) %collective-permute-start.33) | collective-permute-done | bytes 69664 | tf_op jit(solution)/shard_map/ppermute | solution.py:33
  195.7 8.9 %shard_map.323.refs_0_.refs_7_ = bf16[512,1536]{1,0:T(8,128)(2,1)S(1)} custom-call(bf16[512,512]{1,0:T(8,128)(2,1)S(1)} %get-tuple-element.148.refs_0_.refs_8_, bf16[512,512]{1,0:T(8,128)(2,1)S(1)} %get-tuple-element.149.refs_1_, bf16[512,512]{1,0:T(8,128)(2,1)S(1)} %get-tuple-element.150.refs_2_, f32[512,1024]{1,0:T(8,128)S(1)} %get-tuple-element.172.refs_3_, ...), custom_call_target="tpu_custom_call" | custom-call | tf_op jit(solution)/shard_map/pallas_call | solution.py:406
  204.7 4.8 %collective-permute-done.38.refs_2_.refs_5_ = bf16[128,1024]{1,0:T(8,128)(2,1)S(1)} collective-permute-done((bf16[128,1024]{1,0:T(8,128)(2,1)S(1)}, bf16[128,1024]{1,0:T(8,128)(2,1)S(1)}, u32[]{:S(2)}, u32[]{:S(2)}) %collective-permute-start.38) | collective-permute-done | bytes 262176 | tf_op jit(solution)/shard_map/ppermute | solution.py:33
  209.5 6.7 %collective-permute-done.40.refs_1_ = bf16[2,4,32,2560]{3,2,1,0:T(8,128)(2,1)S(1)} collective-permute-done((bf16[2,4,32,2560]{3,2,1,0:T(8,128)(2,1)S(1)}, bf16[2,4,32,2560]{3,2,1,0:T(8,128)(2,1)S(1)}, u32[]{:S(2)}, u32[]{:S(2)}) %collective-permute-start.40) | collective-permute-done | bytes 1310752 | tf_op jit(solution)/shard_map/ppermute | solution.py:27
  226.4 4.8 %collective-permute-done.42.refs_4_ = bf16[4,32,2560]{2,1,0:T(8,128)(2,1)S(1)} collective-permute-done((bf16[4,32,2560]{2,1,0:T(8,128)(2,1)S(1)}, bf16[4,32,2560]{2,1,0:T(8,128)(2,1)S(1)}, u32[]{:S(2)}, u32[]{:S(2)}) %collective-permute-start.42) | collective-permute-done | bytes 655392 | tf_op jit(solution)/shard_map/ppermute | solution.py:27
  239.7 3.9 %shard_map.319 = (f32[256,1024]{1,0:T(8,128)S(1)}, bf16[256,1024]{1,0:T(8,128)(2,1)}) custom-call(s32[4]{0:T(128)S(1)} %pad_add_fusion.coords.refs_0_, bf16[512,2048]{1,0:T(8,128)(2,1)S(1)} %copy-done.3, bf16[2048,1024]{1,0:T(8,128)(2,1)S(1)} %shard_map.317.refs_1_.refs_2_, f32[512,1024]{1,0:T(8,128)S(1)} %get-tuple-element.167.refs_3_.refs_2_, ...), custom_call_target="tpu_custom_call" | custom-call | tf_op jit(solution)/shard_map/pallas_call | solution.py:406
  244.6 5.6 %collective-permute-done.47.refs_1_ = bf16[2,4,32,1664]{3,2,1,0:T(8,128)(2,1)S(1)} collective-permute-done((bf16[2,4,32,1664]{3,2,1,0:T(8,128)(2,1)}, bf16[2,4,32,1664]{3,2,1,0:T(8,128)(2,1)S(1)}, u32[]{:S(2)}, u32[]{:S(2)}) %collective-permute-start.47) | collective-permute-done | bytes 852000 | tf_op jit(solution)/shard_map/ppermute | solution.py:27
  257.4 4.5 %collective-permute-done.46.refs_5_.refs_8_ = bf16[64,2560]{1,0:T(8,128)(2,1)S(1)} collective-permute-done((bf16[64,2560]{1,0:T(8,128)(2,1)}, bf16[64,2560]{1,0:T(8,128)(2,1)S(1)}, u32[]{:S(2)}, u32[]{:S(2)}) %collective-permute-start.46) | collective-permute-done | bytes 327712 | tf_op jit(solution)/shard_map/ppermute | solution.py:33
  275.1 8.6 %collective-permute-done.52.refs_4_ = bf16[64,1664]{1,0:T(8,128)(2,1)S(1)} collective-permute-done((bf16[64,1664]{1,0:T(8,128)(2,1)S(1)}, bf16[64,1664]{1,0:T(8,128)(2,1)S(1)}, u32[]{:S(2)}, u32[]{:S(2)}) %collective-permute-start.52) | collective-permute-done | bytes 213024 | tf_op jit(solution)/shard_map/ppermute | solution.py:33
  293.9 5.1 %collective-permute-start.60 = (f32[8,128]{1,0:T(8,128)S(1)}, f32[8,128]{1,0:T(8,128)S(1)}, u32[]{:S(2)}, u32[]{:S(2)}) collective-permute-start(f32[8,128]{1,0:T(8,128)S(1)} %add_add_fusion), channel_id=1, source_target_pairs={{0,8},{8,0},{16,24},{24,16},{1,9},{9,1},{17,25},{25,17},{2,10},{10... | collective-permute-start | bytes 12296 | tf_op jit(solution)/shard_map/ppermute | solution.py:200
  305.7 6.0 %shard_map.337 = (f32[32,3072]{1,0:T(8,128)}, f32[32,1024]{1,0:T(8,128)}, f32[32,4096]{1,0:T(8,128)}, f32[128,1024]{1,0:T(8,128)}, f32[4,32]{1,0:T(4,128)}, /*in...) custom-call(s32[4]{0:T(128)} %copy-done.39, ...), custom_call_target="tpu_custom_call" | custom-call | tf_op jit(solution)/shard_map/pallas_call | solution.py:242
  (256 shorter events, 134.1 us)
Async XLA Ops:
  17.3 18.2 %collective-permute-start.8 = (bf16[64,1664]{1,0:T(8,128)(2,1)S(1)}, bf16[64,1664]{1,0:T(8,128)(2,1)S(1)}, u32[]{:S(2)}, u32[]{:S(2)}) collective-permute-start(bf16[64,1664]{1,0:T(8,128)(2,1)S(1)} %shard_map.306), channel_id=1, source_target_pairs={{0,16},{8,24},{16,0},{24,8},{1,17},{9,25},{17,1},{25,9},{2,18},{10... | collective-permute-start | bytes 638984 | tf_op jit(solution)/shard_map/ppermute | solution.py:33
  35.7 20.1 %collective-permute-start.11 = (bf16[4,64,1664]{2,1,0:T(8,128)(2,1)S(1)}, bf16[4,64,1664]{2,1,0:T(8,128)(2,1)S(1)}, u32[]{:S(2)}, u32[]{:S(2)}) collective-permute-start(bf16[4,64,1664]{2,1,0:T(8,128)(2,1)S(1)} %pad_maximum_fusion.1.refs_0_), channel_id=1, source_target_pairs={{0,2},{2,0},{1,3},{3,1},{4,6},{6,4},{5,7},{7,5},{8,10},{10,8},{9,1... | collective-permute-start | bytes 2555912 | tf_op jit(solution)/shard_map/ppermute | solution.py:27
  36.3 20.1 %collective-permute-start.10 = (bf16[4,64,1664]{2,1,0:T(8,128)(2,1)S(1)}, bf16[4,64,1664]{2,1,0:T(8,128)(2,1)S(1)}, u32[]{:S(2)}, u32[]{:S(2)}) collective-permute-start(bf16[4,64,1664]{2,1,0:T(8,128)(2,1)S(1)} %pad_maximum_fusion.1.refs_0_), channel_id=1, source_target_pairs={{0,1},{1,0},{2,3},{3,2},{4,5},{5,4},{6,7},{7,6},{8,9},{9,8},{10,11... | collective-permute-start | bytes 2555912 | tf_op jit(solution)/shard_map/ppermute | solution.py:27
  36.8 21.1 %collective-permute-start.18 = (bf16[64,2560]{1,0:T(8,128)(2,1)S(1)}, bf16[64,2560]{1,0:T(8,128)(2,1)S(1)}, u32[]{:S(2)}, u32[]{:S(2)}) collective-permute-start(bf16[64,2560]{1,0:T(8,128)(2,1)S(1)} %shard_map.308), channel_id=1, source_target_pairs={{0,24},{8,0},{16,8},{24,16},{1,25},{9,1},{17,9},{25,17},{2,26},{10... | collective-permute-start | bytes 983048 | tf_op jit(solution)/shard_map/ppermute | solution.py:33
  40.4 28.3 %collective-permute-start.17 = (bf16[64,2560]{1,0:T(8,128)(2,1)S(1)}, bf16[64,2560]{1,0:T(8,128)(2,1)S(1)}, u32[]{:S(2)}, u32[]{:S(2)}) collective-permute-start(bf16[64,2560]{1,0:T(8,128)(2,1)S(1)} %shard_map.308), channel_id=1, source_target_pairs={{0,16},{8,24},{16,0},{24,8},{1,17},{9,25},{17,1},{25,9},{2,18},{10... | collective-permute-start | bytes 983048 | tf_op jit(solution)/shard_map/ppermute | solution.py:33
  40.4 28.3 %collective-permute-start.16 = (bf16[64,2560]{1,0:T(8,128)(2,1)S(1)}, bf16[64,2560]{1,0:T(8,128)(2,1)S(1)}, u32[]{:S(2)}, u32[]{:S(2)}) collective-permute-start(bf16[64,2560]{1,0:T(8,128)(2,1)S(1)} %shard_map.308), channel_id=1, source_target_pairs={{0,8},{8,16},{16,24},{24,0},{1,9},{9,17},{17,25},{25,1},{2,10},{10... | collective-permute-start | bytes 983048 | tf_op jit(solution)/shard_map/ppermute | solution.py:33
  68.7 30.5 %collective-permute-start.24 = (bf16[512,1024]{1,0:T(8,128)(2,1)S(1)}, bf16[512,1024]{1,0:T(8,128)(2,1)S(1)}, u32[]{:S(2)}, u32[]{:S(2)}) collective-permute-start(bf16[512,1024]{1,0:T(8,128)(2,1)S(1)} %constant_dynamic-update-slice_fusion.refs_0_), channel_id=1, source_target_pairs={{0,8},{8,16},{16,24},{24,0},{1,9},{9,17},{17,25},{25,1},{2,10},{10... | collective-permute-start | bytes 3145736 | tf_op jit(solution)/shard_map/ppermute | solution.py:33
  69.0 32.8 %collective-permute-start.21 = (bf16[4,64,2560]{2,1,0:T(8,128)(2,1)S(1)}, bf16[4,64,2560]{2,1,0:T(8,128)(2,1)S(1)}, u32[]{:S(2)}, u32[]{:S(2)}) collective-permute-start(bf16[4,64,2560]{2,1,0:T(8,128)(2,1)S(1)} %pad_maximum_fusion.refs_0_), channel_id=1, source_target_pairs={{0,2},{2,0},{1,3},{3,1},{4,6},{6,4},{5,7},{7,5},{8,10},{10,8},{9,1... | collective-permute-start | bytes 3932168 | tf_op jit(solution)/shard_map/ppermute | solution.py:27
  70.5 31.3 %collective-permute-start.20 = (bf16[4,64,2560]{2,1,0:T(8,128)(2,1)S(1)}, bf16[4,64,2560]{2,1,0:T(8,128)(2,1)S(1)}, u32[]{:S(2)}, u32[]{:S(2)}) collective-permute-start(bf16[4,64,2560]{2,1,0:T(8,128)(2,1)S(1)} %pad_maximum_fusion.refs_0_), channel_id=1, source_target_pairs={{0,1},{1,0},{2,3},{3,2},{4,5},{5,4},{6,7},{7,6},{8,9},{9,8},{10,11... | collective-permute-start | bytes 3932168 | tf_op jit(solution)/shard_map/ppermute | solution.py:27
  76.0 16.9 %collective-permute-start.14 = (bf16[272,128]{1,0:T(8,128)(2,1)S(1)}, bf16[272,128]{1,0:T(8,128)(2,1)S(1)}, u32[]{:S(2)}, u32[]{:S(2)}) collective-permute-start(bf16[272,128]{1,0:T(8,128)(2,1)S(1)} %get-tuple-element.151), channel_id=1, source_target_pairs={{0,8},{8,16},{16,24},{1,9},{9,17},{17,25},{2,10},{10,18},{18,26},{... | collective-permute-start | bytes 208904 | tf_op jit(solution)/shard_map/ppermute | solution.py:33
  101.8 24.6 %collective-permute-start.25 = (bf16[512,1024]{1,0:T(8,128)(2,1)S(1)}, bf16[512,1024]{1,0:T(8,128)(2,1)S(1)}, u32[]{:S(2)}, u32[]{:S(2)}) collective-permute-start(bf16[512,1024]{1,0:T(8,128)(2,1)S(1)} %collective-permute-done.24.refs_1_), channel_id=1, source_target_pairs={{0,8},{8,16},{16,24},{24,0},{1,9},{9,17},{17,25},{25,1},{2,10},{10... | collective-permute-start | bytes 3145736 | tf_op jit(solution)/shard_map/ppermute | solution.py:33
  101.9 24.4 %collective-permute-start.22 = (bf16[2,64,2560]{2,1,0:T(8,128)(2,1)S(1)}, bf16[2,64,2560]{2,1,0:T(8,128)(2,1)S(1)}, u32[]{:S(2)}, u32[]{:S(2)}) collective-permute-start(bf16[2,64,2560]{2,1,0:T(8,128)(2,1)S(1)} %slice.41), channel_id=1, source_target_pairs={{0,1},{1,0},{2,3},{3,2},{4,5},{5,4},{6,7},{7,6},{8,9},{9,8},{10,11... | collective-permute-start | bytes 1966088 | tf_op jit(solution)/shard_map/ppermute | solution.py:27
  102.3 24.1 %collective-permute-start.23 = (bf16[2,64,2560]{2,1,0:T(8,128)(2,1)S(1)}, bf16[2,64,2560]{2,1,0:T(8,128)(2,1)S(1)}, u32[]{:S(2)}, u32[]{:S(2)}) collective-permute-start(bf16[2,64,2560]{2,1,0:T(8,128)(2,1)S(1)} %slice.42), channel_id=1, source_target_pairs={{0,2},{2,0},{1,3},{3,1},{4,6},{6,4},{5,7},{7,5},{8,10},{10,8},{9,1... | collective-permute-start | bytes 1966088 | tf_op jit(solution)/shard_map/ppermute | solution.py:27
  128.1 27.4 %collective-permute-start.27 = (bf16[512,1024]{1,0:T(8,128)(2,1)S(1)}, bf16[512,1024]{1,0:T(8,128)(2,1)S(1)}, u32[]{:S(2)}, u32[]{:S(2)}) collective-permute-start(bf16[512,1024]{1,0:T(8,128)(2,1)S(1)} %collective-permute-done.25.refs_5_.refs_2_), channel_id=1, source_target_pairs={{0,8},{8,16},{16,24},{24,0},{1,9},{9,17},{17,25},{25,1},{2,10},{10... | collective-permute-start | bytes 3145736 | tf_op jit(solution)/shard_map/ppermute | solution.py:33
  140.7 25.3 %collective-permute-start.29 = (bf16[2,4,64,1024]{3,2,1,0:T(8,128)(2,1)S(1)}, bf16[2,4,64,1024]{3,2,1,0:T(8,128)(2,1)S(1)}, u32[]{:S(2)}, u32[]{:S(2)}) collective-permute-start(bf16[2,4,64,1024]{3,2,1,0:T(8,128)(2,1)S(1)} %get-tuple-element.166.refs_4_), channel_id=1, source_target_pairs={{0,1},{1,0},{2,3},{3,2},{4,5},{5,4},{6,7},{7,6},{8,9},{9,8},{10,11... | collective-permute-start | bytes 3145736 | tf_op jit(solution)/shard_map/ppermute | solution.py:27
  141.0 25.0 %collective-permute-start.30 = (bf16[2,4,64,1024]{3,2,1,0:T(8,128)(2,1)S(1)}, bf16[2,4,64,1024]{3,2,1,0:T(8,128)(2,1)S(1)}, u32[]{:S(2)}, u32[]{:S(2)}) collective-permute-start(bf16[2,4,64,1024]{3,2,1,0:T(8,128)(2,1)S(1)} %get-tuple-element.176), channel_id=1, source_target_pairs={{0,2},{2,0},{1,3},{3,1},{4,6},{6,4},{5,7},{7,5},{8,10},{10,8},{9,1... | collective-permute-start | bytes 3145736 | tf_op jit(solution)/shard_map/ppermute | solution.py:27
  187.4 28.9 %collective-permute-start.40 = (bf16[2,4,32,2560]{3,2,1,0:T(8,128)(2,1)S(1)}, bf16[2,4,32,2560]{3,2,1,0:T(8,128)(2,1)S(1)}, u32[]{:S(2)}, u32[]{:S(2)}) collective-permute-start(bf16[2,4,32,2560]{3,2,1,0:T(8,128)(2,1)S(1)} %get-tuple-element.200.refs_9_), channel_id=1, source_target_pairs={{0,1},{1,0},{2,3},{3,2},{4,5},{5,4},{6,7},{7,6},{8,9},{9,8},{10,11... | collective-permute-start | bytes 3932168 | tf_op jit(solution)/shard_map/ppermute | solution.py:27
  188.8 28.5 %collective-permute-start.41 = (bf16[2,4,32,2560]{3,2,1,0:T(8,128)(2,1)S(1)}, bf16[2,4,32,2560]{3,2,1,0:T(8,128)(2,1)S(1)}, u32[]{:S(2)}, u32[]{:S(2)}) collective-permute-start(bf16[2,4,32,2560]{3,2,1,0:T(8,128)(2,1)S(1)} %get-tuple-element.203), channel_id=1, source_target_pairs={{0,2},{2,0},{1,3},{3,1},{4,6},{6,4},{5,7},{7,5},{8,10},{10,8},{9,1... | collective-permute-start | bytes 3932168 | tf_op jit(solution)/shard_map/ppermute | solution.py:27
  193.2 16.3 %collective-permute-start.38 = (bf16[128,1024]{1,0:T(8,128)(2,1)S(1)}, bf16[128,1024]{1,0:T(8,128)(2,1)S(1)}, u32[]{:S(2)}, u32[]{:S(2)}) collective-permute-start(bf16[128,1024]{1,0:T(8,128)(2,1)S(1)} %get-tuple-element.196), channel_id=1, source_target_pairs={{0,16},{8,24},{16,0},{24,8},{1,17},{9,25},{17,1},{25,9},{2,18},{10... | collective-permute-start | bytes 786440 | tf_op jit(solution)/shard_map/ppermute | solution.py:33
  234.7 18.5 %collective-permute-start.48 = (bf16[2,4,32,1664]{3,2,1,0:T(8,128)(2,1)}, bf16[2,4,32,1664]{3,2,1,0:T(8,128)(2,1)S(1)}, u32[]{:S(2)}, u32[]{:S(2)}) collective-permute-start(bf16[2,4,32,1664]{3,2,1,0:T(8,128)(2,1)} %get-tuple-element.218), channel_id=1, source_target_pairs={{0,2},{2,0},{1,3},{3,1},{4,6},{6,4},{5,7},{7,5},{8,10},{10,8},{9,1... | collective-permute-start | bytes 2555912 | tf_op jit(solution)/shard_map/ppermute | solution.py:27
  236.5 18.2 %collective-permute-start.44 = (bf16[64,2560]{1,0:T(8,128)(2,1)}, bf16[64,2560]{1,0:T(8,128)(2,1)}, u32[]{:S(2)}, u32[]{:S(2)}) collective-permute-start(bf16[64,2560]{1,0:T(8,128)(2,1)} %get-tuple-element.207), channel_id=1, source_target_pairs={{0,8},{8,16},{16,24},{24,0},{1,9},{9,17},{17,25},{25,1},{2,10},{10... | collective-permute-start | bytes 983048 | tf_op jit(solution)/shard_map/ppermute | solution.py:33
  238.4 17.9 %collective-permute-start.45 = (bf16[64,2560]{1,0:T(8,128)(2,1)}, bf16[64,2560]{1,0:T(8,128)(2,1)}, u32[]{:S(2)}, u32[]{:S(2)}) collective-permute-start(bf16[64,2560]{1,0:T(8,128)(2,1)} %get-tuple-element.208), channel_id=1, source_target_pairs={{0,16},{8,24},{16,0},{24,8},{1,17},{9,25},{17,1},{25,9},{2,18},{10... | collective-permute-start | bytes 983048 | tf_op jit(solution)/shard_map/ppermute | solution.py:33
  244.6 24.9 %collective-permute-start.28 = (bf16[256,1024]{1,0:T(8,128)(2,1)}, bf16[256,1024]{1,0:T(8,128)(2,1)}, u32[]{:S(2)}, u32[]{:S(2)}) collective-permute-start(bf16[256,1024]{1,0:T(8,128)(2,1)} %get-tuple-element.171), channel_id=1, source_target_pairs={{0,4},{4,0},{1,5},{5,1},{2,6},{6,2},{3,7},{7,3},{8,12},{12,8},{9,1... | collective-permute-start | bytes 1572872 | tf_op jit(solution)/shard_map/ppermute | solution.py:27
  266.9 16.8 %collective-permute-start.52 = (bf16[64,1664]{1,0:T(8,128)(2,1)S(1)}, bf16[64,1664]{1,0:T(8,128)(2,1)S(1)}, u32[]{:S(2)}, u32[]{:S(2)}) collective-permute-start(bf16[64,1664]{1,0:T(8,128)(2,1)S(1)} %get-tuple-element.223), channel_id=1, source_target_pairs={{0,16},{8,24},{16,0},{24,8},{1,17},{9,25},{17,1},{25,9},{2,18},{10... | collective-permute-start | bytes 638984 | tf_op jit(solution)/shard_map/ppermute | solution.py:33
  (86 other events, 922.4 us)
where the time goes:
time: 312 us
  waiting for transfers between devices  151 us (48%)
  starting transfers between devices  75.1 us (24%)
  Pallas kernels  65 us (21%)
  local copies, waits for them, and re-layouts  11.8 us (4%)
  matrix products  4.98 us (2%)
    ppermute x22, waiting for transfers between devices, shift(): return lax.ppermute(value, 'z', pairs)  95.9 us
    ppermute x37, waiting for transfers between devices, swap(): return lax.ppermute(value, axis, SWAP)  49.9 us
    pallas_call x21, Pallas kernels, run(): pl.pallas_call(body_of, out_shape=out_shape, in_specs=([pl.BlockSpec(memo...  49.1 us
    ppermute x22, starting transfers between devices, shift(): return lax.ppermute(value, 'z', pairs)  37.9 us
    ppermute x37, starting transfers between devices, swap(): return lax.ppermute(value, axis, SWAP)  30.2 us
    unnamed x100, local copies, waits for them, and re-layouts  11.4 us
  transfers between devices with their start and end apart: 62, of which 33 were waited for; matrix products, arithmetic and copies ran while one was open for 2% of the time, Pallas kernels for 16%

commit v1 on v0

--- a/solution.py
+++ b/solution.py
@@ -63,10 +63,8 @@
 
 
 def plane_first(shard):
-    half = shard.shape[0] // 2
-    along_x, along_y = swap(shard, "x"), swap(shard, "y")
-    far_low, far_high = swap(along_y[:half], "x"), swap(along_x[half:], "y")
-    return jnp.concatenate([shard, along_x, along_y, far_low, far_high])
+    far = lax.ppermute(shard, ("y", "x"), [(i, 3 - i) for i in range(4)])
+    return jnp.concatenate([shard, swap(shard, "x"), swap(shard, "y"), far])
 
 
 def column_last(plane):
@@ -78,22 +76,22 @@
 
 def column_first_spots(depth):
     half = depth // 2
-    spots = [(0, (k,), 0, (k, 0, 0)) for k in range(depth)]
-    spots += [(1, (k,), 0, (k, 0, 1)) for k in range(depth)]
-    spots += [(2, (k,), 0, (k, 1, 0)) for k in range(depth)]
-    spots += [(3, (k,), 0, (k, 1, 1)) for k in range(half)]
-    return spots + [(4, (k - half,), 0, (k, 1, 1)) for k in range(half, depth)]
-
-
-def plane_first_spots(depth, rows):
-    return [(k, (), p * rows, (k, p // 2, p % 2)) for k in range(depth) for p in range(4)]
+    spots = [(0, (k,), 0, (k, 0, 0), 0) for k in range(depth)]
+    spots += [(1, (k,), 0, (k, 0, 1), 0) for k in range(depth)]
+    spots += [(2, (k,), 0, (k, 1, 0), 0) for k in range(depth)]
+    spots += [(3, (k,), 0, (k, 1, 1), 0) for k in range(half)]
+    return spots + [(4, (k - half,), 0, (k, 1, 1), 0) for k in range(half, depth)]
+
+
+def plane_first_spots(depth, rows, base):
+    return [(base + k, (), p * rows, (k, p // 2, p % 2), 1) for k in range(depth) for p in range(4)]
 
 
 def first_hop(send_x, keep_x, send_y, keep_y, before=()):
     return keep_x, swap(after(send_x, *before), "x"), keep_y, swap(after(send_y, *before), "y")
 
 
-def later_hops(keep_x, got_x, keep_y, got_y, between=(), last=()):
+def second_hop_of(keep_x, got_x, keep_y, got_y, deps=()):
     depth, rows, cols = keep_x.shape[1:]
 
     def second_hop(kx, gx, ky, gy, to_y, to_x):
@@ -101,9 +99,11 @@
         to_x[...] = (ky[1].astype(WIDE) + gy[1].astype(WIDE)).astype(LOW)
 
     outs = [((depth, rows, cols), LOW)] * 2
-    to_y, to_x = run(second_hop, outs, keep_x, got_x, keep_y, got_y, scalars=False, deps=between)
-    on_y, on_x = swap(to_y, "y"), swap(to_x, "x")
-    hop = (on_x, on_y)
+    return run(second_hop, outs, keep_x, got_x, keep_y, got_y, scalars=False, deps=deps)
+
+
+def third_hop_of(keep_x, got_x, keep_y, got_y, on_y, on_x, deps=()):
+    depth, rows, cols = keep_x.shape[1:]
 
     def third_hop(kx, gx, ky, gy, ony, onx, own, *sends):
         for k in range(depth):
@@ -114,8 +114,8 @@
             out[rows:, :] = two.astype(out.dtype)
 
     outs = [((2 * rows, cols), WIDE if k == 0 else LOW) for k in range(depth)]
-    own, *sends = run(third_hop, outs, keep_x, got_x, keep_y, got_y, on_y, on_x, scalars=False, deps=last)
-    return [own] + [shift(part, k + 1) for k, part in enumerate(sends)], hop
+    own, *sends = run(third_hop, outs, keep_x, got_x, keep_y, got_y, on_y, on_x, scalars=False, deps=deps)
+    return [own] + [shift(part, k + 1) for k, part in enumerate(sends)]
 
 
 def sum_of(refs):
@@ -280,9 +280,9 @@
 def place(parts, depth, outs, spots, moves, deps=()):
     def kernel(coords, *refs):
         ins, out_refs = refs[: len(parts)], refs[len(parts) + len(deps) :]
-        for array, lead, base, rel in spots:
+        for array, lead, base, rel, piece in spots:
             zz, plane = chip_of(coords, rel, depth, True)
-            for o, sr, sc, rows, cols, tr, tc in moves(zz, plane):
+            for o, sr, sc, rows, cols, tr, tc in moves(zz, plane, piece):
                 out_refs[o][window(tr, rows, tc, cols)] = ins[array][(*lead, *window(base + sr, rows, sc, cols))]
 
     return pl.pallas_call(
@@ -349,11 +349,27 @@
     )(coordinates(), qkv, norm)
 
 
-def cast_rest(up, out, down, halves):
+def cast_down(down):
+    half = down.shape[0] // 2
+
+    def kernel(down_ref, one_ref, two_ref):
+        one_ref[...] = down_ref[:half, :].astype(LOW)
+        two_ref[...] = down_ref[half:, :].astype(LOW)
+
+    return pl.pallas_call(
+        kernel,
+        out_shape=[jax.ShapeDtypeStruct((half, down.shape[1]), LOW)] * 2,
+        in_specs=[VMEM],
+        out_specs=[VMEM] * 2,
+        compiler_params=ROOM,
+    )(down)
+
+
+def cast_rest(up, out, halves):
     rows, cols = up.shape
     block, width = cols // (2 * halves), out.shape[1]
 
-    def kernel(coords, up_ref, out_ref, down_ref, own_ref, mate_ref, part_ref, low_ref):
+    def kernel(coords, up_ref, out_ref, own_ref, mate_ref, part_ref):
         first = coords[3] == 0
         for j in range(halves):
             a = up_ref[:, 2 * j * block : (2 * j + 1) * block]
@@ -362,16 +378,15 @@
             mate_ref[:, j * block : (j + 1) * block] = jnp.where(first, b, a).astype(LOW)
         part_ref[:rows, :] = out_ref[:, : width // 2].astype(LOW)
         part_ref[rows:, :] = out_ref[:, width // 2 :].astype(LOW)
-        low_ref[...] = down_ref[...].astype(LOW)
 
     return pl.pallas_call(
         kernel,
         out_shape=[jax.ShapeDtypeStruct((rows, cols // 2), LOW)] * 2
-        + [jax.ShapeDtypeStruct((2 * rows, width // 2), LOW), jax.ShapeDtypeStruct(down.shape, LOW)],
-        in_specs=[pl.BlockSpec(memory_space=pltpu.SMEM), VMEM, VMEM, VMEM],
-        out_specs=[VMEM] * 4,
+        + [jax.ShapeDtypeStruct((2 * rows, width // 2), LOW)],
+        in_specs=[pl.BlockSpec(memory_space=pltpu.SMEM), VMEM, VMEM],
+        out_specs=[VMEM] * 3,
         compiler_params=ROOM,
-    )(coordinates(), up, out, down)
+    )(coordinates(), up, out)
 
 
 def join_rows(own, mate, side=None):
@@ -661,7 +676,7 @@
     return run(kernel, [((width, units), LOW)], rows, grad, scalars=False, deps=deps)[0]
 
 
-def attend_turn(part, got, resid, rows, grad_out, out_w, mixed, denom, query):
+def attend_turn(part, got, resid, rows, grad_out, out_w, mixed, denom, query, deps):
     tokens, width = resid.shape
     half = mixed.shape[1]
     pairs, step = half // LANES, tokens // 2
@@ -705,7 +720,7 @@
     outs += [((pairs * HEAD_DIM + 16, LANES), LOW), ((2, width), WIDE)]
     ins = (part, got, resid, rows, grad_out, out_w, mixed, denom, query)
     scratch = [pltpu.VMEM((16, LANES), WIDE)]
-    return run(kernel, outs, *ins, scalars=False, scratch=scratch)
+    return run(kernel, outs, *ins, scalars=False, scratch=scratch, deps=deps)
 
 
 def attend_back(query, key, value, qk, a_low, b_rows, state, parts, deps=()):
@@ -844,32 +859,32 @@
     if ring:
         qkv_mine, qkv_give = cast_qkv(qkv_weight, norm_params, 3 * depth)
         qkv_part = join_rows(qkv_mine, swap(qkv_give, "c"))
-        up_mine, up_give, out_part, down_low = cast_rest(
-            after(up_weight, qkv_part), out_weight, down_weight, depth
-        )
+        down_one, down_two = cast_down(down_weight)
+        up_mine, up_give, out_part = cast_rest(after(up_weight, qkv_part), out_weight, depth)
         inputs = join_rows(own_x, swap(own_x, "c"))
         up_part = join_rows(up_mine, swap(up_give, "c"), out_part)
         qkv_column = column_first(qkv_part)
-        down_plane = plane_first(after(down_low, qkv_part))
-        qkv_column = [after(part, down_plane, up_part, inputs) for part in qkv_column]
+        two_plane = plane_first(after(down_two, qkv_part))
+        qkv_column = [after(part, two_plane, up_part, inputs) for part in qkv_column]
         up_column = column_first(after(up_part, *qkv_column))
         qkv_parts = plane_last(jnp.stack(qkv_column))
         g_mate = swap(after(own_g, *up_column), "c")
-        down_parts = [down_plane, shift(after(down_plane, *up_column), 1)]
-
-        def qkv_moves(zz, plane):
+        two_parts = [two_plane, shift(after(two_plane, *up_column), 1)]
+        one_column = column_first(after(down_one, two_parts[1]))
+
+        def qkv_moves(zz, plane, piece):
             row = lambda h: ((zz * 2 + h) * chips + plane) * own_rows
             moves = [(0, h * own_rows, 0, own_rows, half_qkv, row(h), 0) for h in (0, 1)]
             return moves + [(1, h * own_rows, half_qkv, own_rows, LANES, row(h), 0) for h in (0, 1)]
 
-        def up_moves(zz, plane):
+        def up_moves(zz, plane, piece):
             row = lambda h: ((zz * 2 + h) * chips + plane) * own_rows
             moves = [(0, h * own_rows, 0, own_rows, half_ff, row(h), 0) for h in (0, 1)]
             to = zz * block + plane * own_rows
             return moves + [(1, h * own_rows, half_ff, own_rows, half_d, to, h * half_d) for h in (0, 1)]
 
-        def down_moves(zz, plane):
-            return [(0, 0, 0, own_units, width, zz * ff_block + plane * own_units, 0)]
+        def down_moves(zz, plane, piece):
+            return [(0, 0, 0, thin, width, zz * ff_block + plane * own_units + piece * thin, 0)]
 
         spots = column_first_spots(depth)
         qkv_w, norm_w = place(qkv_parts, depth, [(width, half_qkv), (width, LANES)], spots, qkv_moves)
@@ -891,12 +906,13 @@
     earlier = from_others(state, 1)
     mixed, mixed_low, denom, state_in, attended = attend(query, key, value, earlier, (grad_out,))
     if ring:
-        up_parts = plane_last(after(jnp.stack(up_column), *qkv_parts[3:]), tuple(earlier))
-        down_parts.append(shift(after(down_parts[-1], *earlier), 1))
+        gate = (*earlier, *one_column[1:])
+        up_parts = plane_last(after(jnp.stack(up_column), *qkv_parts[3:]), gate)
+        two_parts.append(shift(after(two_parts[-1], *gate), 1))
         for _ in range(3, depth):
-            down_parts.append(shift(down_parts[-1], 1))
+            two_parts.append(shift(two_parts[-1], 1))
         up_w, out_w = place(
-            up_parts, depth, [(width, half_ff), (half_d, width)], spots, up_moves, down_parts[2:3]
+            up_parts, depth, [(width, half_ff), (half_d, width)], spots, up_moves, two_parts[2:3]
         )
     out_part, out_low = out_project(mixed_low, out_w)
     out_got = swap(out_low, "c")
@@ -908,17 +924,23 @@
 
         down_cut = unplace([down_grad], depth, (thin, width), down_cuts)
         down_hop = first_hop(*down_cut)
-        spots = plane_first_spots(depth, own_units)
+        one_parts = plane_last(after(jnp.stack(one_column), *up_parts[3:]), (down_cut[0][0, 0, :16, :LANES],))
+        spots = spots + plane_first_spots(depth, thin, 5)
+        down_parts = [*one_parts, *two_parts]
         (down_w,) = place(down_parts, depth, [(half_ff, width)], spots, down_moves, (down_cut[0],))
 
     grad_hidden, two_part, two_low = feed_back(grad_out, down_w, slope, up_w)
     down_own, down_give = down_project(activated, down_w, resid, (two_low,))
     down_got = swap(down_give, "c")
     activations = (down_own + down_got.astype(WIDE)).astype(LOW)
-    up_grad = weight_grad(normed_two, grad_hidden, down_hop[1::2] if ring else ())
-    two_got = after(swap(two_low, "c"), up_grad)
+    up_grad = weight_grad(normed_two, grad_hidden)
+    two_got = swap(two_low, "c")
+    deps = (up_grad,)
+    if ring:
+        down_turn = second_hop_of(*down_hop)
+        deps = (up_grad, down_turn[0])
     grad_resid, grad_resid_low, a_low, b_rows, state_grad, norm_two = attend_turn(
-        two_part, two_got, resid, rows, grad_out, out_w, mixed, denom, query
+        two_part, two_got, resid, rows, grad_out, out_w, mixed, denom, query, deps
     )
     later = from_others(state_grad, -1)
     out_grad = dot_rows(mixed_low, grad_resid_low).astype(LOW)
@@ -949,10 +971,17 @@
             row = ((zz * 2 + half) * chips + plane) * own_rows
             return [(0, row, 0, own_rows, half_qkv, 0, 0), (1, row, 0, own_rows, LANES, 0, half_qkv)]
 
-        down_sum, hop = later_hops(*down_hop)
-        up_sum, hop = later_hops(*first_hop(*up_cut, (*hop, *later)), (*down_sum[1:], grad_projected))
+        hop = swap(down_turn[0], "y"), swap(down_turn[1], "x")
+        down_sum = third_hop_of(*down_hop, *hop)
+        up_hop = first_hop(*up_cut, (*hop, *later))
+        turn = second_hop_of(*up_hop, (*down_sum[1:], grad_projected))
+        hop = swap(turn[0], "y"), swap(turn[1], "x")
+        up_sum = third_hop_of(*up_hop, *hop)
         qkv_cut = unplace([qkv_grad, norm_cols], depth, (own_rows, half_qkv + LANES), qkv_cuts)
-        qkv_sum, hop = later_hops(*first_hop(*qkv_cut, hop), (), up_sum[1:])
+        qkv_hop = first_hop(*qkv_cut, hop)
+        turn = second_hop_of(*qkv_hop)
+        hop = swap(turn[0], "y"), swap(turn[1], "x")
+        qkv_sum = third_hop_of(*qkv_hop, *hop, up_sum[1:])
         down_red, squares = finish_down(down_sum)
         up_mine, up_give, out_red, squares = finish_up(up_sum, squares, own_rows, half_ff)
         up_mate = swap(up_give, "c")

time: 312 us -> 304 us (0.974)
  waiting for transfers between devices: 151 us -> 131 us
  starting transfers between devices: 75.1 us -> 83.6 us
  local copies, waits for them, and re-layouts: 11.8 us -> 15.3 us
    ppermute x22 -> x25, waiting for transfers between devices: 95.9 us -> 62.3 us  [shift(): return lax.ppermute(value, 'z', pairs)]
    ppermute x37 -> x39, waiting for transfers between devices: 49.9 us -> 60.1 us  [swap(): return lax.ppermute(value, axis, SWAP)]
    ppermute x22 -> x25, starting transfers between devices: 37.9 us -> 43 us  [shift(): return lax.ppermute(value, 'z', pairs)]
    unnamed x100 -> x95, local copies, waits for them, and re-layouts: 11.4 us -> 14.9 us
    ppermute x0 -> x1, waiting for transfers between devices: none -> 3.34 us  [plane_first(): far = lax.ppermute(shard, ('y', 'x'), [(i, 3 - i) for i in range(4)])]
    ppermute x37 -> x39, starting transfers between devices: 30.2 us -> 32.6 us  [swap(): return lax.ppermute(value, axis, SWAP)]
  transfers between devices with their start and end apart: 62 -> 68, of which waited for: 33 -> 36; matrix products, arithmetic and copies ran while one was open for 2% -> 2% of each run, Pallas kernels for 16% -> 17%
where the time goes in v1:
time: 304 us
  waiting for transfers between devices  131 us (43%)
  starting transfers between devices  83.6 us (28%)
  Pallas kernels  65 us (21%)
  local copies, waits for them, and re-layouts  15.3 us (5%)
  matrix products  4.97 us (2%)
    ppermute x25, waiting for transfers between devices, shift(): return lax.ppermute(value, 'z', pairs)  62.3 us
    ppermute x39, waiting for transfers between devices, swap(): return lax.ppermute(value, axis, SWAP)  60.1 us
    pallas_call x21, Pallas kernels, run(): pl.pallas_call(body_of, out_shape=out_shape, in_specs=([pl.BlockSpec(memo...  49.1 us
    ppermute x25, starting transfers between devices, shift(): return lax.ppermute(value, 'z', pairs)  43 us
    ppermute x39, starting transfers between devices, swap(): return lax.ppermute(value, axis, SWAP)  32.6 us
    unnamed x95, local copies, waits for them, and re-layouts  14.9 us
  transfers between devices with their start and end apart: 68, of which 36 were waited for; matrix products, arithmetic and copies ran while one was open for 2% of the time, Pallas kernels for 17%

profile of v1, /device:TPU:0, one launch (start us, length us, event | category | flops | bytes accessed | tf_op | source)
XLA Modules:
  0.0 303.9 jit_solution(16273416509062976968)
XLA Ops:
  8.4 3.6 %collective-permute-start.8 = (bf16[64,1664]{1,0:T(8,128)(2,1)S(1)}, bf16[64,1664]{1,0:T(8,128)(2,1)S(1)}, u32[]{:S(2)}, u32[]{:S(2)}) collective-permute-start(bf16[64,1664]{1,0:T(8,128)(2,1)S(1)} %shard_map.306), channel_id=1, source_target_pairs={{0,24},{8,0},{16,8},{24,16},{1,25},{9,1},{17,9},{25,17},{2,26},{10... | collective-permute-start | bytes 638984 | tf_op jit(solution)/shard_map/ppermute | solution.py:33
  19.7 3.3 %collective-permute-done.4 = bf16[64,1024]{1,0:T(8,128)(2,1)S(1)} collective-permute-done((bf16[64,1024]{1,0:T(8,128)(2,1)S(1)}, bf16[64,1024]{1,0:T(8,128)(2,1)S(1)}, u32[]{:S(2)}, u32[]{:S(2)}) %collective-permute-start.4) | collective-permute-done | bytes 131104 | tf_op jit(solution)/shard_map/ppermute | solution.py:66
  23.7 9.0 %collective-permute-done.7 = bf16[64,1664]{1,0:T(8,128)(2,1)S(1)} collective-permute-done((bf16[64,1664]{1,0:T(8,128)(2,1)S(1)}, bf16[64,1664]{1,0:T(8,128)(2,1)S(1)}, u32[]{:S(2)}, u32[]{:S(2)}) %collective-permute-start.7) | collective-permute-done | bytes 213024 | tf_op jit(solution)/shard_map/ppermute | solution.py:33
  39.0 14.7 %collective-permute-done.10.refs_2_ = bf16[4,64,1664]{2,1,0:T(8,128)(2,1)S(1)} collective-permute-done((bf16[4,64,1664]{2,1,0:T(8,128)(2,1)S(1)}, bf16[4,64,1664]{2,1,0:T(8,128)(2,1)S(1)}, u32[]{:S(2)}, u32[]{:S(2)}) %collective-permute-start.10) | collective-permute-done | bytes 852000 | tf_op jit(solution)/shard_map/ppermute | solution.py:27
  56.4 8.4 %collective-permute-done.16 = bf16[64,2560]{1,0:T(8,128)(2,1)S(1)} collective-permute-done((bf16[64,2560]{1,0:T(8,128)(2,1)S(1)}, bf16[64,2560]{1,0:T(8,128)(2,1)S(1)}, u32[]{:S(2)}, u32[]{:S(2)}) %collective-permute-start.16) | collective-permute-done | bytes 327712 | tf_op jit(solution)/shard_map/ppermute | solution.py:33
  71.5 3.6 %collective-permute-start.13 = (bf16[272,128]{1,0:T(8,128)(2,1)S(1)}, bf16[272,128]{1,0:T(8,128)(2,1)S(1)}, u32[]{:S(2)}, u32[]{:S(2)}) collective-permute-start(bf16[272,128]{1,0:T(8,128)(2,1)S(1)} %get-tuple-element.155), channel_id=1, source_target_pairs={{0,8},{8,16},{16,24},{1,9},{9,17},{17,25},{2,10},{10,18},{18,26},{... | collective-permute-start | bytes 208904 | tf_op jit(solution)/shard_map/ppermute | solution.py:33
  75.2 5.5 %collective-permute-done.19.refs_6_ = bf16[256,1024]{1,0:T(8,128)(2,1)S(1)} collective-permute-done((bf16[256,1024]{1,0:T(8,128)(2,1)S(1)}, bf16[256,1024]{1,0:T(8,128)(2,1)S(1)}, u32[]{:S(2)}, u32[]{:S(2)}) %collective-permute-start.19) | collective-permute-done | bytes 524320 | tf_op jit(solution)/shard_map/ppermute | solution.py:33
  87.1 6.4 %collective-permute-start.14 = (bf16[272,128]{1,0:T(8,128)(2,1)S(1)}, bf16[272,128]{1,0:T(8,128)(2,1)S(1)}, u32[]{:S(2)}, u32[]{:S(2)}) collective-permute-start(bf16[272,128]{1,0:T(8,128)(2,1)S(1)} %add_convert_fusion.2), channel_id=1, source_target_pairs={{0,16},{8,24},{1,17},{9,25},{2,18},{10,26},{3,19},{11,27},{4,20},{... | collective-permute-start | bytes 208904 | tf_op jit(solution)/shard_map/ppermute | solution.py:33
  100.5 4.8 %shard_map.313 = (f32[512,512]{1,0:T(8,128)S(1)}, bf16[512,512]{1,0:T(8,128)(2,1)S(1)}, f32[512,512]{1,0:T(8,128)S(1)}, f32[272,128]{1,0:T(8,128)S(1)}, f32[8,128]{1,0:T(8,128)}) custom-call(bf16[512,512]{1,0:T(8,128)(2,1)S(1)} %get-tuple-element.152.refs_0_.refs_8_, bf16[512,512]{1,0:T(8,128)(2,1)S(1)} %get-tuple-element.153.refs_1_, ...), custom_call_target="tpu_custom_call" | custom-call | tf_op jit(solution)/shard_map/pallas_call | solution.py:421
  106.3 7.8 %collective-permute-done.27.refs_5_.refs_7_ = bf16[256,1024]{1,0:T(8,128)(2,1)S(1)} collective-permute-done((bf16[256,1024]{1,0:T(8,128)(2,1)S(1)}, bf16[256,1024]{1,0:T(8,128)(2,1)S(1)}, u32[]{:S(2)}, u32[]{:S(2)}) %collective-permute-start.27) | collective-permute-done | bytes 524320 | tf_op jit(solution)/shard_map/ppermute | solution.py:33
  118.5 5.8 %shard_map.316 = (f32[512,1024]{1,0:T(8,128)S(1)}, bf16[512,1024]{1,0:T(8,128)(2,1)S(1)}, bf16[512,2048]{1,0:T(8,128)(2,1)S(1)}, f32[512,2048]{1,0:T(8,128)S(1)}) custom-call(bf16[512,1024]{1,0:T(8,128)(2,1)S(1)} %shard_map.304.refs_0_.refs_2_, f32[512,1024]{1,0:T(8,128)S(1)} %get-tuple-element.167.refs_1_, ...), custom_call_target="tpu_custom_call" | custom-call | tf_op jit(solution)/shard_map/pallas_call | solution.py:421
  134.9 5.2 %collective-permute-done.31.refs_3_ = bf16[2,64,1024]{2,1,0:T(8,128)(2,1)S(1)} collective-permute-done((bf16[2,64,1024]{2,1,0:T(8,128)(2,1)S(1)}, bf16[2,64,1024]{2,1,0:T(8,128)(2,1)S(1)}, u32[]{:S(2)}, u32[]{:S(2)}) %collective-permute-start.31) | collective-permute-done | bytes 262176 | tf_op jit(solution)/shard_map/ppermute | solution.py:27
  142.5 5.6 %shard_map.319 = (bf16[512,2048]{1,0:T(8,128)(2,1)S(1)}, f32[512,1024]{1,0:T(8,128)S(1)}, bf16[512,1024]{1,0:T(8,128)(2,1)S(1)}) custom-call(bf16[512,1024]{1,0:T(8,128)(2,1)S(1)} %shard_map.312.refs_5_.refs_0_.refs_4_, bf16[2048,1024]{1,0:T(8,128)(2,1)S(1)} %shard_map.318.refs_1_.refs_2_, f32[512,2048]{1,0:T(8,128)S(1)} %get-tuple-element.177.refs_2_, ...), custom_call_target="tpu_custom_call" | custom-call | tf_op jit(solution)/shard_map/pallas_call | solution.py:421
  151.2 9.9 %collective-permute-done.36.refs_1_ = bf16[2,4,64,1024]{3,2,1,0:T(8,128)(2,1)S(1)} collective-permute-done((bf16[2,4,64,1024]{3,2,1,0:T(8,128)(2,1)S(1)}, bf16[2,4,64,1024]{3,2,1,0:T(8,128)(2,1)S(1)}, u32[]{:S(2)}, u32[]{:S(2)}) %collective-permute-start.36) | collective-permute-done | bytes 1048608 | tf_op jit(solution)/shard_map/ppermute | solution.py:27
  163.7 3.5 %shard_map.323 = (f32[512,1024]{1,0:T(8,128)S(1)}, bf16[512,1024]{1,0:T(8,128)(2,1)S(1)}, bf16[512,512]{1,0:T(8,128)(2,1)S(1)}, f32[512,512]{1,0:T(8,128)S(1)}, ...) custom-call(f32[512,1024]{1,0:T(8,128)S(1)} %get-tuple-element.182.refs_0_, ...), custom_call_target="tpu_custom_call" | custom-call | tf_op jit(solution)/shard_map/pallas_call | solution.py:421
  176.4 4.9 %collective-permute-done.39.refs_8_ = bf16[272,128]{1,0:T(8,128)(2,1)S(1)} collective-permute-done((bf16[272,128]{1,0:T(8,128)(2,1)S(1)}, bf16[272,128]{1,0:T(8,128)(2,1)S(1)}, u32[]{:S(2)}, u32[]{:S(2)}) %collective-permute-start.39) | collective-permute-done | bytes 69664 | tf_op jit(solution)/shard_map/ppermute | solution.py:33
  189.6 8.9 %shard_map.325.refs_0_.refs_7_ = bf16[512,1536]{1,0:T(8,128)(2,1)S(1)} custom-call(bf16[512,512]{1,0:T(8,128)(2,1)S(1)} %get-tuple-element.152.refs_0_.refs_8_, bf16[512,512]{1,0:T(8,128)(2,1)S(1)} %get-tuple-element.153.refs_1_, bf16[512,512]{1,0:T(8,128)(2,1)S(1)} %get-tuple-element.154.refs_2_, f32[512,1024]{1,0:T(8,128)S(1)} %get-tuple-element.181.refs_3_, ...), custom_call_target="tpu_custom_call" | custom-call | tf_op jit(solution)/shard_map/pallas_call | solution.py:421
  201.4 7.4 %collective-permute-done.46.refs_1_ = bf16[2,4,32,2560]{3,2,1,0:T(8,128)(2,1)S(1)} collective-permute-done((bf16[2,4,32,2560]{3,2,1,0:T(8,128)(2,1)S(1)}, bf16[2,4,32,2560]{3,2,1,0:T(8,128)(2,1)S(1)}, u32[]{:S(2)}, u32[]{:S(2)}) %collective-permute-start.46) | collective-permute-done | bytes 1310752 | tf_op jit(solution)/shard_map/ppermute | solution.py:27
  221.1 4.5 %collective-permute-done.48.refs_4_ = bf16[4,32,2560]{2,1,0:T(8,128)(2,1)S(1)} collective-permute-done((bf16[4,32,2560]{2,1,0:T(8,128)(2,1)S(1)}, bf16[4,32,2560]{2,1,0:T(8,128)(2,1)S(1)}, u32[]{:S(2)}, u32[]{:S(2)}) %collective-permute-start.48) | collective-permute-done | bytes 655392 | tf_op jit(solution)/shard_map/ppermute | solution.py:27
  232.5 3.9 %shard_map.320 = (f32[256,1024]{1,0:T(8,128)S(1)}, bf16[256,1024]{1,0:T(8,128)(2,1)}) custom-call(s32[4]{0:T(128)S(1)} %pad_add_fusion.coords.refs_0_, bf16[512,2048]{1,0:T(8,128)(2,1)S(1)} %get-tuple-element.171.refs_1_, bf16[2048,1024]{1,0:T(8,128)(2,1)S(1)} %shard_map.318.refs_1_.refs_2_, f32[512,1024]{1,0:T(8,128)S(1)} %get-tuple-element.176.refs_3_.refs_2_, ...), custom_call_target="tpu_custom_call" | custom-call | tf_op jit(solution)/shard_map/pallas_call | solution.py:421
  237.4 4.0 %collective-permute-done.53.refs_1_ = bf16[2,4,32,1664]{3,2,1,0:T(8,128)(2,1)S(1)} collective-permute-done((bf16[2,4,32,1664]{3,2,1,0:T(8,128)(2,1)}, bf16[2,4,32,1664]{3,2,1,0:T(8,128)(2,1)S(1)}, u32[]{:S(2)}, u32[]{:S(2)}) %collective-permute-start.53) | collective-permute-done | bytes 852000 | tf_op jit(solution)/shard_map/ppermute | solution.py:27
  267.2 8.5 %collective-permute-done.58.refs_4_ = bf16[64,1664]{1,0:T(8,128)(2,1)S(1)} collective-permute-done((bf16[64,1664]{1,0:T(8,128)(2,1)S(1)}, bf16[64,1664]{1,0:T(8,128)(2,1)S(1)}, u32[]{:S(2)}, u32[]{:S(2)}) %collective-permute-start.58) | collective-permute-done | bytes 213024 | tf_op jit(solution)/shard_map/ppermute | solution.py:33
  285.9 5.0 %collective-permute-start.66 = (f32[8,128]{1,0:T(8,128)S(1)}, f32[8,128]{1,0:T(8,128)S(1)}, u32[]{:S(2)}, u32[]{:S(2)}) collective-permute-start(f32[8,128]{1,0:T(8,128)S(1)} %add_add_fusion), channel_id=1, source_target_pairs={{0,8},{8,0},{16,24},{24,16},{1,9},{9,1},{17,25},{25,17},{2,10},{10... | collective-permute-start | bytes 12296 | tf_op jit(solution)/shard_map/ppermute | solution.py:200
  297.7 6.0 %shard_map.338 = (f32[32,3072]{1,0:T(8,128)}, f32[32,1024]{1,0:T(8,128)}, f32[32,4096]{1,0:T(8,128)}, f32[128,1024]{1,0:T(8,128)}, f32[4,32]{1,0:T(4,128)}, /*in...) custom-call(s32[4]{0:T(128)} %copy-done.37, ...), custom_call_target="tpu_custom_call" | custom-call | tf_op jit(solution)/shard_map/pallas_call | solution.py:242
  (265 shorter events, 152.1 us)
Async XLA Ops:
  3.7 19.4 %collective-permute-start = (bf16[256,1024]{1,0:T(8,128)(2,1)}, bf16[256,1024]{1,0:T(8,128)(2,1)S(1)}, u32[]{:S(2)}, u32[]{:S(2)}) collective-permute-start(bf16[256,1024]{1,0:T(8,128)(2,1)} %bitcast.31), channel_id=1, source_target_pairs={{0,4},{4,0},{1,5},{5,1},{2,6},{6,2},{3,7},{7,3},{8,12},{12,8},{9,1... | collective-permute-start | bytes 1572872 | tf_op jit(solution)/shard_map/ppermute | solution.py:27
  8.4 15.3 %collective-permute-start.8 = (bf16[64,1664]{1,0:T(8,128)(2,1)S(1)}, bf16[64,1664]{1,0:T(8,128)(2,1)S(1)}, u32[]{:S(2)}, u32[]{:S(2)}) collective-permute-start(bf16[64,1664]{1,0:T(8,128)(2,1)S(1)} %shard_map.306), channel_id=1, source_target_pairs={{0,24},{8,0},{16,8},{24,16},{1,25},{9,1},{17,9},{25,17},{2,26},{10... | collective-permute-start | bytes 638984 | tf_op jit(solution)/shard_map/ppermute | solution.py:33
  32.8 21.0 %collective-permute-start.10 = (bf16[4,64,1664]{2,1,0:T(8,128)(2,1)S(1)}, bf16[4,64,1664]{2,1,0:T(8,128)(2,1)S(1)}, u32[]{:S(2)}, u32[]{:S(2)}) collective-permute-start(bf16[4,64,1664]{2,1,0:T(8,128)(2,1)S(1)} %pad_maximum_fusion.1.refs_0_), channel_id=1, source_target_pairs={{0,2},{2,0},{1,3},{3,1},{4,6},{6,4},{5,7},{7,5},{8,10},{10,8},{9,1... | collective-permute-start | bytes 2555912 | tf_op jit(solution)/shard_map/ppermute | solution.py:27
  33.8 21.0 %collective-permute-start.9 = (bf16[4,64,1664]{2,1,0:T(8,128)(2,1)S(1)}, bf16[4,64,1664]{2,1,0:T(8,128)(2,1)S(1)}, u32[]{:S(2)}, u32[]{:S(2)}) collective-permute-start(bf16[4,64,1664]{2,1,0:T(8,128)(2,1)S(1)} %pad_maximum_fusion.1.refs_0_), channel_id=1, source_target_pairs={{0,1},{1,0},{2,3},{3,2},{4,5},{5,4},{6,7},{7,6},{8,9},{9,8},{10,11... | collective-permute-start | bytes 2555912 | tf_op jit(solution)/shard_map/ppermute | solution.py:27
  35.2 21.1 %collective-permute-start.17 = (bf16[64,2560]{1,0:T(8,128)(2,1)S(1)}, bf16[64,2560]{1,0:T(8,128)(2,1)S(1)}, u32[]{:S(2)}, u32[]{:S(2)}) collective-permute-start(bf16[64,2560]{1,0:T(8,128)(2,1)S(1)} %shard_map.309), channel_id=1, source_target_pairs={{0,24},{8,0},{16,8},{24,16},{1,25},{9,1},{17,9},{25,17},{2,26},{10... | collective-permute-start | bytes 983048 | tf_op jit(solution)/shard_map/ppermute | solution.py:33
  35.3 29.5 %collective-permute-start.16 = (bf16[64,2560]{1,0:T(8,128)(2,1)S(1)}, bf16[64,2560]{1,0:T(8,128)(2,1)S(1)}, u32[]{:S(2)}, u32[]{:S(2)}) collective-permute-start(bf16[64,2560]{1,0:T(8,128)(2,1)S(1)} %shard_map.309), channel_id=1, source_target_pairs={{0,16},{8,24},{16,0},{24,8},{1,17},{9,25},{17,1},{25,9},{2,18},{10... | collective-permute-start | bytes 983048 | tf_op jit(solution)/shard_map/ppermute | solution.py:33
  37.0 27.8 %collective-permute-start.15 = (bf16[64,2560]{1,0:T(8,128)(2,1)S(1)}, bf16[64,2560]{1,0:T(8,128)(2,1)S(1)}, u32[]{:S(2)}, u32[]{:S(2)}) collective-permute-start(bf16[64,2560]{1,0:T(8,128)(2,1)S(1)} %shard_map.309), channel_id=1, source_target_pairs={{0,8},{8,16},{16,24},{24,0},{1,9},{9,17},{17,25},{25,1},{2,10},{10... | collective-permute-start | bytes 983048 | tf_op jit(solution)/shard_map/ppermute | solution.py:33
  65.5 29.9 %collective-permute-start.24 = (bf16[4,64,2560]{2,1,0:T(8,128)(2,1)S(1)}, bf16[4,64,2560]{2,1,0:T(8,128)(2,1)S(1)}, u32[]{:S(2)}, u32[]{:S(2)}) collective-permute-start(bf16[4,64,2560]{2,1,0:T(8,128)(2,1)S(1)} %pad_maximum_fusion.refs_0_), channel_id=1, source_target_pairs={{0,2},{2,0},{1,3},{3,1},{4,6},{6,4},{5,7},{7,5},{8,10},{10,8},{9,1... | collective-permute-start | bytes 3932168 | tf_op jit(solution)/shard_map/ppermute | solution.py:27
  67.0 28.8 %collective-permute-start.23 = (bf16[4,64,2560]{2,1,0:T(8,128)(2,1)S(1)}, bf16[4,64,2560]{2,1,0:T(8,128)(2,1)S(1)}, u32[]{:S(2)}, u32[]{:S(2)}) collective-permute-start(bf16[4,64,2560]{2,1,0:T(8,128)(2,1)S(1)} %pad_maximum_fusion.refs_0_), channel_id=1, source_target_pairs={{0,1},{1,0},{2,3},{3,2},{4,5},{5,4},{6,7},{7,6},{8,9},{9,8},{10,11... | collective-permute-start | bytes 3932168 | tf_op jit(solution)/shard_map/ppermute | solution.py:27
  95.9 18.3 %collective-permute-start.25 = (bf16[2,64,2560]{2,1,0:T(8,128)(2,1)S(1)}, bf16[2,64,2560]{2,1,0:T(8,128)(2,1)S(1)}, u32[]{:S(2)}, u32[]{:S(2)}) collective-permute-start(bf16[2,64,2560]{2,1,0:T(8,128)(2,1)S(1)} %slice.42), channel_id=1, source_target_pairs={{0,1},{1,0},{2,3},{3,2},{4,5},{5,4},{6,7},{7,6},{8,9},{9,8},{10,11... | collective-permute-start | bytes 1966088 | tf_op jit(solution)/shard_map/ppermute | solution.py:27
  96.5 17.7 %collective-permute-start.26 = (bf16[2,64,2560]{2,1,0:T(8,128)(2,1)S(1)}, bf16[2,64,2560]{2,1,0:T(8,128)(2,1)S(1)}, u32[]{:S(2)}, u32[]{:S(2)}) collective-permute-start(bf16[2,64,2560]{2,1,0:T(8,128)(2,1)S(1)} %slice.43), channel_id=1, source_target_pairs={{0,2},{2,0},{1,3},{3,1},{4,6},{6,4},{5,7},{7,5},{8,10},{10,8},{9,1... | collective-permute-start | bytes 1966088 | tf_op jit(solution)/shard_map/ppermute | solution.py:27
  98.0 16.1 %collective-permute-start.27 = (bf16[256,1024]{1,0:T(8,128)(2,1)S(1)}, bf16[256,1024]{1,0:T(8,128)(2,1)S(1)}, u32[]{:S(2)}, u32[]{:S(2)}) collective-permute-start(bf16[256,1024]{1,0:T(8,128)(2,1)S(1)} %collective-permute-done.19.refs_6_), channel_id=1, source_target_pairs={{0,8},{8,16},{16,24},{24,0},{1,9},{9,17},{17,25},{25,1},{2,10},{10... | collective-permute-start | bytes 1572872 | tf_op jit(solution)/shard_map/ppermute | solution.py:33
  115.9 19.0 %collective-permute-start.33 = (bf16[256,1024]{1,0:T(8,128)(2,1)S(1)}, bf16[256,1024]{1,0:T(8,128)(2,1)S(1)}, u32[]{:S(2)}, u32[]{:S(2)}) collective-permute-start(bf16[256,1024]{1,0:T(8,128)(2,1)S(1)} %collective-permute-done.27.refs_5_.refs_7_), channel_id=1, source_target_pairs={{0,8},{8,16},{16,24},{24,0},{1,9},{9,17},{17,25},{25,1},{2,10},{10... | collective-permute-start | bytes 1572872 | tf_op jit(solution)/shard_map/ppermute | solution.py:33
  132.9 28.1 %collective-permute-start.36 = (bf16[2,4,64,1024]{3,2,1,0:T(8,128)(2,1)S(1)}, bf16[2,4,64,1024]{3,2,1,0:T(8,128)(2,1)S(1)}, u32[]{:S(2)}, u32[]{:S(2)}) collective-permute-start(bf16[2,4,64,1024]{3,2,1,0:T(8,128)(2,1)S(1)} %get-tuple-element.173.refs_9_), channel_id=1, source_target_pairs={{0,1},{1,0},{2,3},{3,2},{4,5},{5,4},{6,7},{7,6},{8,9},{9,8},{10,11... | collective-permute-start | bytes 3145736 | tf_op jit(solution)/shard_map/ppermute | solution.py:27
  134.4 27.7 %collective-permute-start.37 = (bf16[2,4,64,1024]{3,2,1,0:T(8,128)(2,1)S(1)}, bf16[2,4,64,1024]{3,2,1,0:T(8,128)(2,1)S(1)}, u32[]{:S(2)}, u32[]{:S(2)}) collective-permute-start(bf16[2,4,64,1024]{3,2,1,0:T(8,128)(2,1)S(1)} %get-tuple-element.189), channel_id=1, source_target_pairs={{0,2},{2,0},{1,3},{3,1},{4,6},{6,4},{5,7},{7,5},{8,10},{10,8},{9,1... | collective-permute-start | bytes 3145736 | tf_op jit(solution)/shard_map/ppermute | solution.py:27
  181.3 27.5 %collective-permute-start.46 = (bf16[2,4,32,2560]{3,2,1,0:T(8,128)(2,1)S(1)}, bf16[2,4,32,2560]{3,2,1,0:T(8,128)(2,1)S(1)}, u32[]{:S(2)}, u32[]{:S(2)}) collective-permute-start(bf16[2,4,32,2560]{3,2,1,0:T(8,128)(2,1)S(1)} %get-tuple-element.208.refs_9_), channel_id=1, source_target_pairs={{0,1},{1,0},{2,3},{3,2},{4,5},{5,4},{6,7},{7,6},{8,9},{9,8},{10,11... | collective-permute-start | bytes 3932168 | tf_op jit(solution)/shard_map/ppermute | solution.py:27
  182.4 28.5 %collective-permute-start.47 = (bf16[2,4,32,2560]{3,2,1,0:T(8,128)(2,1)S(1)}, bf16[2,4,32,2560]{3,2,1,0:T(8,128)(2,1)S(1)}, u32[]{:S(2)}, u32[]{:S(2)}) collective-permute-start(bf16[2,4,32,2560]{3,2,1,0:T(8,128)(2,1)S(1)} %get-tuple-element.211), channel_id=1, source_target_pairs={{0,2},{2,0},{1,3},{3,1},{4,6},{6,4},{5,7},{7,5},{8,10},{10,8},{9,1... | collective-permute-start | bytes 3932168 | tf_op jit(solution)/shard_map/ppermute | solution.py:27
  185.9 15.5 %collective-permute-start.44 = (bf16[128,1024]{1,0:T(8,128)(2,1)S(1)}, bf16[128,1024]{1,0:T(8,128)(2,1)S(1)}, u32[]{:S(2)}, u32[]{:S(2)}) collective-permute-start(bf16[128,1024]{1,0:T(8,128)(2,1)S(1)} %get-tuple-element.204), channel_id=1, source_target_pairs={{0,16},{8,24},{16,0},{24,8},{1,17},{9,25},{17,1},{25,9},{2,18},{10... | collective-permute-start | bytes 786440 | tf_op jit(solution)/shard_map/ppermute | solution.py:33
  225.6 15.7 %collective-permute-start.53 = (bf16[2,4,32,1664]{3,2,1,0:T(8,128)(2,1)}, bf16[2,4,32,1664]{3,2,1,0:T(8,128)(2,1)S(1)}, u32[]{:S(2)}, u32[]{:S(2)}) collective-permute-start(bf16[2,4,32,1664]{3,2,1,0:T(8,128)(2,1)} %get-tuple-element.223), channel_id=1, source_target_pairs={{0,1},{1,0},{2,3},{3,2},{4,5},{5,4},{6,7},{7,6},{8,9},{9,8},{10,11... | collective-permute-start | bytes 2555912 | tf_op jit(solution)/shard_map/ppermute | solution.py:27
  226.5 17.7 %collective-permute-start.54 = (bf16[2,4,32,1664]{3,2,1,0:T(8,128)(2,1)}, bf16[2,4,32,1664]{3,2,1,0:T(8,128)(2,1)S(1)}, u32[]{:S(2)}, u32[]{:S(2)}) collective-permute-start(bf16[2,4,32,1664]{3,2,1,0:T(8,128)(2,1)} %get-tuple-element.226), channel_id=1, source_target_pairs={{0,2},{2,0},{1,3},{3,1},{4,6},{6,4},{5,7},{7,5},{8,10},{10,8},{9,1... | collective-permute-start | bytes 2555912 | tf_op jit(solution)/shard_map/ppermute | solution.py:27
  229.7 15.8 %collective-permute-start.50 = (bf16[64,2560]{1,0:T(8,128)(2,1)}, bf16[64,2560]{1,0:T(8,128)(2,1)}, u32[]{:S(2)}, u32[]{:S(2)}) collective-permute-start(bf16[64,2560]{1,0:T(8,128)(2,1)} %get-tuple-element.215), channel_id=1, source_target_pairs={{0,8},{8,16},{16,24},{24,0},{1,9},{9,17},{17,25},{25,1},{2,10},{10... | collective-permute-start | bytes 983048 | tf_op jit(solution)/shard_map/ppermute | solution.py:33
  232.0 17.6 %collective-permute-start.51 = (bf16[64,2560]{1,0:T(8,128)(2,1)}, bf16[64,2560]{1,0:T(8,128)(2,1)}, u32[]{:S(2)}, u32[]{:S(2)}) collective-permute-start(bf16[64,2560]{1,0:T(8,128)(2,1)} %get-tuple-element.216), channel_id=1, source_target_pairs={{0,16},{8,24},{16,0},{24,8},{1,17},{9,25},{17,1},{25,9},{2,18},{10... | collective-permute-start | bytes 983048 | tf_op jit(solution)/shard_map/ppermute | solution.py:33
  237.4 24.2 %collective-permute-start.34 = (bf16[256,1024]{1,0:T(8,128)(2,1)}, bf16[256,1024]{1,0:T(8,128)(2,1)}, u32[]{:S(2)}, u32[]{:S(2)}) collective-permute-start(bf16[256,1024]{1,0:T(8,128)(2,1)} %get-tuple-element.180), channel_id=1, source_target_pairs={{0,4},{4,0},{1,5},{5,1},{2,6},{6,2},{3,7},{7,3},{8,12},{12,8},{9,1... | collective-permute-start | bytes 1572872 | tf_op jit(solution)/shard_map/ppermute | solution.py:27
  258.8 16.9 %collective-permute-start.58 = (bf16[64,1664]{1,0:T(8,128)(2,1)S(1)}, bf16[64,1664]{1,0:T(8,128)(2,1)S(1)}, u32[]{:S(2)}, u32[]{:S(2)}) collective-permute-start(bf16[64,1664]{1,0:T(8,128)(2,1)S(1)} %get-tuple-element.231), channel_id=1, source_target_pairs={{0,16},{8,24},{16,0},{24,8},{1,17},{9,25},{17,1},{25,9},{2,18},{10... | collective-permute-start | bytes 638984 | tf_op jit(solution)/shard_map/ppermute | solution.py:33
  (90 other events, 968.4 us)

commit v2 on v1

--- a/solution.py
+++ b/solution.py
@@ -212,7 +212,7 @@
 
 
 def update_all(grads, totals, masters, firsts, seconds, rates, decays, blocks):
-    steps = 4
+    steps = 2
     n, m = len(grads), len(totals)
 
     def tile(array):
@@ -813,7 +813,7 @@
 
 
 def from_others(low, step):
-    if lax.axis_size("z") == 4:
+    if lax.axis_size("z") == 4 and step == 1:
         near = shift(low, step, wrap=False)
         pair = (low.astype(WIDE) + near.astype(WIDE)).astype(LOW)
         return [near, shift(pair, 2 * step, wrap=False)]
@@ -937,7 +937,7 @@
     two_got = swap(two_low, "c")
     deps = (up_grad,)
     if ring:
-        down_turn = second_hop_of(*down_hop)
+        down_turn = second_hop_of(*down_hop, (up_grad,))
         deps = (up_grad, down_turn[0])
     grad_resid, grad_resid_low, a_low, b_rows, state_grad, norm_two = attend_turn(
         two_part, two_got, resid, rows, grad_out, out_w, mixed, denom, query, deps

time: 304 us -> 300 us (0.987)
  waiting for transfers between devices: 131 us -> 123 us
  starting transfers between devices: 83.6 us -> 87.4 us
    ppermute x25 -> x26, waiting for transfers between devices: 62.3 us -> 55 us  [shift(): return lax.ppermute(value, 'z', pairs)]
    ppermute x25 -> x26, starting transfers between devices: 43 us -> 46.4 us  [shift(): return lax.ppermute(value, 'z', pairs)]
  transfers between devices with their start and end apart: 68 -> 69, of which waited for: 36 -> 37; matrix products, arithmetic and copies ran while one was open for 2% -> 2% of each run, Pallas kernels for 17% -> 19%
where the time goes in v2:
time: 300 us
  waiting for transfers between devices  123 us (41%)
  starting transfers between devices  87.4 us (29%)
  Pallas kernels  64.3 us (21%)
  local copies, waits for them, and re-layouts  16.1 us (5%)
  matrix products  5.01 us (2%)
    ppermute x39, waiting for transfers between devices, swap(): return lax.ppermute(value, axis, SWAP)  59.3 us
    ppermute x26, waiting for transfers between devices, shift(): return lax.ppermute(value, 'z', pairs)  55 us
    pallas_call x21, Pallas kernels, run(): pl.pallas_call(body_of, out_shape=out_shape, in_specs=([pl.BlockSpec(memo...  49.1 us
    ppermute x26, starting transfers between devices, shift(): return lax.ppermute(value, 'z', pairs)  46.4 us
    ppermute x39, starting transfers between devices, swap(): return lax.ppermute(value, axis, SWAP)  33 us
    unnamed x95, local copies, waits for them, and re-layouts  15.7 us
    ppermute x2, starting transfers between devices, sum_chips(): lax.ppermute(value, 'z', [(i, i ^ near) for i in range(size)])  6.04 us
  transfers between devices with their start and end apart: 69, of which 37 were waited for; matrix products, arithmetic and copies ran while one was open for 2% of the time, Pallas kernels for 19%

profile of v2, /device:TPU:0, one launch (start us, length us, event | category | flops | bytes accessed | tf_op | source)
XLA Modules:
  0.0 299.9 jit_solution(15896066056632173477)
XLA Ops:
  8.4 3.6 %collective-permute-start.8 = (bf16[64,1664]{1,0:T(8,128)(2,1)S(1)}, bf16[64,1664]{1,0:T(8,128)(2,1)S(1)}, u32[]{:S(2)}, u32[]{:S(2)}) collective-permute-start(bf16[64,1664]{1,0:T(8,128)(2,1)S(1)} %shard_map.306), channel_id=1, source_target_pairs={{0,24},{8,0},{16,8},{24,16},{1,25},{9,1},{17,9},{25,17},{2,26},{10... | collective-permute-start | bytes 638984 | tf_op jit(solution)/shard_map/ppermute | solution.py:33
  19.7 3.3 %collective-permute-done.4 = bf16[64,1024]{1,0:T(8,128)(2,1)S(1)} collective-permute-done((bf16[64,1024]{1,0:T(8,128)(2,1)S(1)}, bf16[64,1024]{1,0:T(8,128)(2,1)S(1)}, u32[]{:S(2)}, u32[]{:S(2)}) %collective-permute-start.4) | collective-permute-done | bytes 131104 | tf_op jit(solution)/shard_map/ppermute | solution.py:66
  23.7 9.0 %collective-permute-done.7 = bf16[64,1664]{1,0:T(8,128)(2,1)S(1)} collective-permute-done((bf16[64,1664]{1,0:T(8,128)(2,1)S(1)}, bf16[64,1664]{1,0:T(8,128)(2,1)S(1)}, u32[]{:S(2)}, u32[]{:S(2)}) %collective-permute-start.7) | collective-permute-done | bytes 213024 | tf_op jit(solution)/shard_map/ppermute | solution.py:33
  39.0 14.7 %collective-permute-done.10.refs_2_ = bf16[4,64,1664]{2,1,0:T(8,128)(2,1)S(1)} collective-permute-done((bf16[4,64,1664]{2,1,0:T(8,128)(2,1)S(1)}, bf16[4,64,1664]{2,1,0:T(8,128)(2,1)S(1)}, u32[]{:S(2)}, u32[]{:S(2)}) %collective-permute-start.10) | collective-permute-done | bytes 852000 | tf_op jit(solution)/shard_map/ppermute | solution.py:27
  56.4 8.4 %collective-permute-done.16 = bf16[64,2560]{1,0:T(8,128)(2,1)S(1)} collective-permute-done((bf16[64,2560]{1,0:T(8,128)(2,1)S(1)}, bf16[64,2560]{1,0:T(8,128)(2,1)S(1)}, u32[]{:S(2)}, u32[]{:S(2)}) %collective-permute-start.16) | collective-permute-done | bytes 327712 | tf_op jit(solution)/shard_map/ppermute | solution.py:33
  72.6 3.6 %collective-permute-start.13 = (bf16[272,128]{1,0:T(8,128)(2,1)S(1)}, bf16[272,128]{1,0:T(8,128)(2,1)S(1)}, u32[]{:S(2)}, u32[]{:S(2)}) collective-permute-start(bf16[272,128]{1,0:T(8,128)(2,1)S(1)} %get-tuple-element.155), channel_id=1, source_target_pairs={{0,8},{8,16},{16,24},{1,9},{9,17},{17,25},{2,10},{10,18},{18,26},{... | collective-permute-start | bytes 208904 | tf_op jit(solution)/shard_map/ppermute | solution.py:33
  76.2 4.5 %collective-permute-done.19.refs_6_ = bf16[256,1024]{1,0:T(8,128)(2,1)S(1)} collective-permute-done((bf16[256,1024]{1,0:T(8,128)(2,1)S(1)}, bf16[256,1024]{1,0:T(8,128)(2,1)S(1)}, u32[]{:S(2)}, u32[]{:S(2)}) %collective-permute-start.19) | collective-permute-done | bytes 524320 | tf_op jit(solution)/shard_map/ppermute | solution.py:33
  87.1 6.4 %collective-permute-start.14 = (bf16[272,128]{1,0:T(8,128)(2,1)S(1)}, bf16[272,128]{1,0:T(8,128)(2,1)S(1)}, u32[]{:S(2)}, u32[]{:S(2)}) collective-permute-start(bf16[272,128]{1,0:T(8,128)(2,1)S(1)} %add_convert_fusion.1), channel_id=1, source_target_pairs={{0,16},{8,24},{1,17},{9,25},{2,18},{10,26},{3,19},{11,27},{4,20},{... | collective-permute-start | bytes 208904 | tf_op jit(solution)/shard_map/ppermute | solution.py:33
  100.5 4.8 %shard_map.313 = (f32[512,512]{1,0:T(8,128)S(1)}, bf16[512,512]{1,0:T(8,128)(2,1)S(1)}, f32[512,512]{1,0:T(8,128)S(1)}, f32[272,128]{1,0:T(8,128)S(1)}, f32[8,128]{1,0:T(8,128)}) custom-call(bf16[512,512]{1,0:T(8,128)(2,1)S(1)} %get-tuple-element.152.refs_0_.refs_8_, bf16[512,512]{1,0:T(8,128)(2,1)S(1)} %get-tuple-element.153.refs_1_, ...), custom_call_target="tpu_custom_call" | custom-call | tf_op jit(solution)/shard_map/pallas_call | solution.py:421
  106.3 7.8 %collective-permute-done.27.refs_5_.refs_7_ = bf16[256,1024]{1,0:T(8,128)(2,1)S(1)} collective-permute-done((bf16[256,1024]{1,0:T(8,128)(2,1)S(1)}, bf16[256,1024]{1,0:T(8,128)(2,1)S(1)}, u32[]{:S(2)}, u32[]{:S(2)}) %collective-permute-start.27) | collective-permute-done | bytes 524320 | tf_op jit(solution)/shard_map/ppermute | solution.py:33
  118.5 5.7 %shard_map.316 = (f32[512,1024]{1,0:T(8,128)S(1)}, bf16[512,1024]{1,0:T(8,128)(2,1)S(1)}, bf16[512,2048]{1,0:T(8,128)(2,1)S(1)}, f32[512,2048]{1,0:T(8,128)S(1)}) custom-call(bf16[512,1024]{1,0:T(8,128)(2,1)S(1)} %shard_map.304.refs_0_.refs_2_, f32[512,1024]{1,0:T(8,128)S(1)} %get-tuple-element.167.refs_1_, ...), custom_call_target="tpu_custom_call" | custom-call | tf_op jit(solution)/shard_map/pallas_call | solution.py:421
  134.9 5.2 %collective-permute-done.31.refs_3_ = bf16[2,64,1024]{2,1,0:T(8,128)(2,1)S(1)} collective-permute-done((bf16[2,64,1024]{2,1,0:T(8,128)(2,1)S(1)}, bf16[2,64,1024]{2,1,0:T(8,128)(2,1)S(1)}, u32[]{:S(2)}, u32[]{:S(2)}) %collective-permute-start.31) | collective-permute-done | bytes 262176 | tf_op jit(solution)/shard_map/ppermute | solution.py:27
  142.5 5.6 %shard_map.319 = (bf16[512,2048]{1,0:T(8,128)(2,1)S(1)}, f32[512,1024]{1,0:T(8,128)S(1)}, bf16[512,1024]{1,0:T(8,128)(2,1)S(1)}) custom-call(bf16[512,1024]{1,0:T(8,128)(2,1)S(1)} %shard_map.312.refs_5_.refs_0_.refs_4_, bf16[2048,1024]{1,0:T(8,128)(2,1)S(1)} %shard_map.318.refs_1_.refs_2_, f32[512,2048]{1,0:T(8,128)S(1)} %get-tuple-element.177.refs_2_, ...), custom_call_target="tpu_custom_call" | custom-call | tf_op jit(solution)/shard_map/pallas_call | solution.py:421
  151.2 9.9 %collective-permute-done.36.refs_1_ = bf16[2,4,64,1024]{3,2,1,0:T(8,128)(2,1)S(1)} collective-permute-done((bf16[2,4,64,1024]{3,2,1,0:T(8,128)(2,1)S(1)}, bf16[2,4,64,1024]{3,2,1,0:T(8,128)(2,1)S(1)}, u32[]{:S(2)}, u32[]{:S(2)}) %collective-permute-start.36) | collective-permute-done | bytes 1048608 | tf_op jit(solution)/shard_map/ppermute | solution.py:27
  164.5 3.5 %shard_map.323 = (f32[512,1024]{1,0:T(8,128)S(1)}, bf16[512,1024]{1,0:T(8,128)(2,1)S(1)}, bf16[512,512]{1,0:T(8,128)(2,1)S(1)}, f32[512,512]{1,0:T(8,128)S(1)}, ...) custom-call(f32[512,1024]{1,0:T(8,128)S(1)} %get-tuple-element.182.refs_0_, ...), custom_call_target="tpu_custom_call" | custom-call | tf_op jit(solution)/shard_map/pallas_call | solution.py:421
  185.8 8.9 %shard_map.325.refs_0_.refs_7_ = bf16[512,1536]{1,0:T(8,128)(2,1)S(1)} custom-call(bf16[512,512]{1,0:T(8,128)(2,1)S(1)} %get-tuple-element.152.refs_0_.refs_8_, bf16[512,512]{1,0:T(8,128)(2,1)S(1)} %get-tuple-element.153.refs_1_, bf16[512,512]{1,0:T(8,128)(2,1)S(1)} %get-tuple-element.154.refs_2_, f32[512,1024]{1,0:T(8,128)S(1)} %get-tuple-element.181.refs_3_, ...), custom_call_target="tpu_custom_call" | custom-call | tf_op jit(solution)/shard_map/pallas_call | solution.py:421
  197.6 7.5 %collective-permute-done.47.refs_1_ = bf16[2,4,32,2560]{3,2,1,0:T(8,128)(2,1)S(1)} collective-permute-done((bf16[2,4,32,2560]{3,2,1,0:T(8,128)(2,1)S(1)}, bf16[2,4,32,2560]{3,2,1,0:T(8,128)(2,1)S(1)}, u32[]{:S(2)}, u32[]{:S(2)}) %collective-permute-start.47) | collective-permute-done | bytes 1310752 | tf_op jit(solution)/shard_map/ppermute | solution.py:27
  228.6 3.9 %shard_map.320 = (f32[256,1024]{1,0:T(8,128)S(1)}, bf16[256,1024]{1,0:T(8,128)(2,1)}) custom-call(s32[4]{0:T(128)S(1)} %pad_add_fusion.coords.refs_0_, bf16[512,2048]{1,0:T(8,128)(2,1)S(1)} %get-tuple-element.171.refs_1_, bf16[2048,1024]{1,0:T(8,128)(2,1)S(1)} %shard_map.318.refs_1_.refs_2_, f32[512,1024]{1,0:T(8,128)S(1)} %get-tuple-element.176.refs_3_.refs_2_, ...), custom_call_target="tpu_custom_call" | custom-call | tf_op jit(solution)/shard_map/pallas_call | solution.py:421
  233.5 4.1 %collective-permute-done.54.refs_1_ = bf16[2,4,32,1664]{3,2,1,0:T(8,128)(2,1)S(1)} collective-permute-done((bf16[2,4,32,1664]{3,2,1,0:T(8,128)(2,1)}, bf16[2,4,32,1664]{3,2,1,0:T(8,128)(2,1)S(1)}, u32[]{:S(2)}, u32[]{:S(2)}) %collective-permute-start.54) | collective-permute-done | bytes 852000 | tf_op jit(solution)/shard_map/ppermute | solution.py:27
  242.4 3.4 %collective-permute-done.52.refs_4_.refs_7_ = bf16[64,2560]{1,0:T(8,128)(2,1)} collective-permute-done((bf16[64,2560]{1,0:T(8,128)(2,1)}, bf16[64,2560]{1,0:T(8,128)(2,1)}, u32[]{:S(2)}, u32[]{:S(2)}) %collective-permute-start.52) | collective-permute-done | bytes 327712 | tf_op jit(solution)/shard_map/ppermute | solution.py:33
  254.7 3.4 %collective-permute-start.59 = (bf16[64,1664]{1,0:T(8,128)(2,1)S(1)}, bf16[64,1664]{1,0:T(8,128)(2,1)S(1)}, u32[]{:S(2)}, u32[]{:S(2)}) collective-permute-start(bf16[64,1664]{1,0:T(8,128)(2,1)S(1)} %get-tuple-element.231), channel_id=1, source_target_pairs={{0,16},{8,24},{16,0},{24,8},{1,17},{9,25},{17,1},{25,9},{2,18},{10... | collective-permute-start | bytes 638984 | tf_op jit(solution)/shard_map/ppermute | solution.py:33
  263.8 8.5 %collective-permute-done.59.refs_4_ = bf16[64,1664]{1,0:T(8,128)(2,1)S(1)} collective-permute-done((bf16[64,1664]{1,0:T(8,128)(2,1)S(1)}, bf16[64,1664]{1,0:T(8,128)(2,1)S(1)}, u32[]{:S(2)}, u32[]{:S(2)}) %collective-permute-start.59) | collective-permute-done | bytes 213024 | tf_op jit(solution)/shard_map/ppermute | solution.py:33
  282.5 5.0 %collective-permute-start.67 = (f32[8,128]{1,0:T(8,128)S(1)}, f32[8,128]{1,0:T(8,128)S(1)}, u32[]{:S(2)}, u32[]{:S(2)}) collective-permute-start(f32[8,128]{1,0:T(8,128)S(1)} %add_add_fusion), channel_id=1, source_target_pairs={{0,8},{8,0},{16,24},{24,16},{1,9},{9,1},{17,25},{25,17},{2,10},{10... | collective-permute-start | bytes 12296 | tf_op jit(solution)/shard_map/ppermute | solution.py:200
  294.4 5.3 %shard_map.338 = (f32[32,3072]{1,0:T(8,128)}, f32[32,1024]{1,0:T(8,128)}, f32[32,4096]{1,0:T(8,128)}, f32[128,1024]{1,0:T(8,128)}, f32[4,32]{1,0:T(4,128)}, /*in...) custom-call(s32[4]{0:T(128)} %copy-done.37, ...), custom_call_target="tpu_custom_call" | custom-call | tf_op jit(solution)/shard_map/pallas_call | solution.py:242
  (266 shorter events, 152.2 us)
Async XLA Ops:
  3.7 19.4 %collective-permute-start = (bf16[256,1024]{1,0:T(8,128)(2,1)}, bf16[256,1024]{1,0:T(8,128)(2,1)S(1)}, u32[]{:S(2)}, u32[]{:S(2)}) collective-permute-start(bf16[256,1024]{1,0:T(8,128)(2,1)} %bitcast.31), channel_id=1, source_target_pairs={{0,4},{4,0},{1,5},{5,1},{2,6},{6,2},{3,7},{7,3},{8,12},{12,8},{9,1... | collective-permute-start | bytes 1572872 | tf_op jit(solution)/shard_map/ppermute | solution.py:27
  32.8 21.0 %collective-permute-start.10 = (bf16[4,64,1664]{2,1,0:T(8,128)(2,1)S(1)}, bf16[4,64,1664]{2,1,0:T(8,128)(2,1)S(1)}, u32[]{:S(2)}, u32[]{:S(2)}) collective-permute-start(bf16[4,64,1664]{2,1,0:T(8,128)(2,1)S(1)} %pad_maximum_fusion.1.refs_0_), channel_id=1, source_target_pairs={{0,2},{2,0},{1,3},{3,1},{4,6},{6,4},{5,7},{7,5},{8,10},{10,8},{9,1... | collective-permute-start | bytes 2555912 | tf_op jit(solution)/shard_map/ppermute | solution.py:27
  33.8 21.0 %collective-permute-start.9 = (bf16[4,64,1664]{2,1,0:T(8,128)(2,1)S(1)}, bf16[4,64,1664]{2,1,0:T(8,128)(2,1)S(1)}, u32[]{:S(2)}, u32[]{:S(2)}) collective-permute-start(bf16[4,64,1664]{2,1,0:T(8,128)(2,1)S(1)} %pad_maximum_fusion.1.refs_0_), channel_id=1, source_target_pairs={{0,1},{1,0},{2,3},{3,2},{4,5},{5,4},{6,7},{7,6},{8,9},{9,8},{10,11... | collective-permute-start | bytes 2555912 | tf_op jit(solution)/shard_map/ppermute | solution.py:27
  35.2 21.1 %collective-permute-start.17 = (bf16[64,2560]{1,0:T(8,128)(2,1)S(1)}, bf16[64,2560]{1,0:T(8,128)(2,1)S(1)}, u32[]{:S(2)}, u32[]{:S(2)}) collective-permute-start(bf16[64,2560]{1,0:T(8,128)(2,1)S(1)} %shard_map.309), channel_id=1, source_target_pairs={{0,24},{8,0},{16,8},{24,16},{1,25},{9,1},{17,9},{25,17},{2,26},{10... | collective-permute-start | bytes 983048 | tf_op jit(solution)/shard_map/ppermute | solution.py:33
  35.3 29.5 %collective-permute-start.16 = (bf16[64,2560]{1,0:T(8,128)(2,1)S(1)}, bf16[64,2560]{1,0:T(8,128)(2,1)S(1)}, u32[]{:S(2)}, u32[]{:S(2)}) collective-permute-start(bf16[64,2560]{1,0:T(8,128)(2,1)S(1)} %shard_map.309), channel_id=1, source_target_pairs={{0,16},{8,24},{16,0},{24,8},{1,17},{9,25},{17,1},{25,9},{2,18},{10... | collective-permute-start | bytes 983048 | tf_op jit(solution)/shard_map/ppermute | solution.py:33
  37.0 27.8 %collective-permute-start.15 = (bf16[64,2560]{1,0:T(8,128)(2,1)S(1)}, bf16[64,2560]{1,0:T(8,128)(2,1)S(1)}, u32[]{:S(2)}, u32[]{:S(2)}) collective-permute-start(bf16[64,2560]{1,0:T(8,128)(2,1)S(1)} %shard_map.309), channel_id=1, source_target_pairs={{0,8},{8,16},{16,24},{24,0},{1,9},{9,17},{17,25},{25,1},{2,10},{10... | collective-permute-start | bytes 983048 | tf_op jit(solution)/shard_map/ppermute | solution.py:33
  65.5 29.9 %collective-permute-start.24 = (bf16[4,64,2560]{2,1,0:T(8,128)(2,1)S(1)}, bf16[4,64,2560]{2,1,0:T(8,128)(2,1)S(1)}, u32[]{:S(2)}, u32[]{:S(2)}) collective-permute-start(bf16[4,64,2560]{2,1,0:T(8,128)(2,1)S(1)} %pad_maximum_fusion.refs_0_), channel_id=1, source_target_pairs={{0,2},{2,0},{1,3},{3,1},{4,6},{6,4},{5,7},{7,5},{8,10},{10,8},{9,1... | collective-permute-start | bytes 3932168 | tf_op jit(solution)/shard_map/ppermute | solution.py:27
  67.0 28.8 %collective-permute-start.23 = (bf16[4,64,2560]{2,1,0:T(8,128)(2,1)S(1)}, bf16[4,64,2560]{2,1,0:T(8,128)(2,1)S(1)}, u32[]{:S(2)}, u32[]{:S(2)}) collective-permute-start(bf16[4,64,2560]{2,1,0:T(8,128)(2,1)S(1)} %pad_maximum_fusion.refs_0_), channel_id=1, source_target_pairs={{0,1},{1,0},{2,3},{3,2},{4,5},{5,4},{6,7},{7,6},{8,9},{9,8},{10,11... | collective-permute-start | bytes 3932168 | tf_op jit(solution)/shard_map/ppermute | solution.py:27
  95.9 18.3 %collective-permute-start.25 = (bf16[2,64,2560]{2,1,0:T(8,128)(2,1)S(1)}, bf16[2,64,2560]{2,1,0:T(8,128)(2,1)S(1)}, u32[]{:S(2)}, u32[]{:S(2)}) collective-permute-start(bf16[2,64,2560]{2,1,0:T(8,128)(2,1)S(1)} %slice.42), channel_id=1, source_target_pairs={{0,1},{1,0},{2,3},{3,2},{4,5},{5,4},{6,7},{7,6},{8,9},{9,8},{10,11... | collective-permute-start | bytes 1966088 | tf_op jit(solution)/shard_map/ppermute | solution.py:27
  96.5 17.7 %collective-permute-start.26 = (bf16[2,64,2560]{2,1,0:T(8,128)(2,1)S(1)}, bf16[2,64,2560]{2,1,0:T(8,128)(2,1)S(1)}, u32[]{:S(2)}, u32[]{:S(2)}) collective-permute-start(bf16[2,64,2560]{2,1,0:T(8,128)(2,1)S(1)} %slice.43), channel_id=1, source_target_pairs={{0,2},{2,0},{1,3},{3,1},{4,6},{6,4},{5,7},{7,5},{8,10},{10,8},{9,1... | collective-permute-start | bytes 1966088 | tf_op jit(solution)/shard_map/ppermute | solution.py:27
  98.0 16.1 %collective-permute-start.27 = (bf16[256,1024]{1,0:T(8,128)(2,1)S(1)}, bf16[256,1024]{1,0:T(8,128)(2,1)S(1)}, u32[]{:S(2)}, u32[]{:S(2)}) collective-permute-start(bf16[256,1024]{1,0:T(8,128)(2,1)S(1)} %collective-permute-done.19.refs_6_), channel_id=1, source_target_pairs={{0,8},{8,16},{16,24},{24,0},{1,9},{9,17},{17,25},{25,1},{2,10},{10... | collective-permute-start | bytes 1572872 | tf_op jit(solution)/shard_map/ppermute | solution.py:33
  115.9 19.0 %collective-permute-start.33 = (bf16[256,1024]{1,0:T(8,128)(2,1)S(1)}, bf16[256,1024]{1,0:T(8,128)(2,1)S(1)}, u32[]{:S(2)}, u32[]{:S(2)}) collective-permute-start(bf16[256,1024]{1,0:T(8,128)(2,1)S(1)} %collective-permute-done.27.refs_5_.refs_7_), channel_id=1, source_target_pairs={{0,8},{8,16},{16,24},{24,0},{1,9},{9,17},{17,25},{25,1},{2,10},{10... | collective-permute-start | bytes 1572872 | tf_op jit(solution)/shard_map/ppermute | solution.py:33
  132.9 28.1 %collective-permute-start.36 = (bf16[2,4,64,1024]{3,2,1,0:T(8,128)(2,1)S(1)}, bf16[2,4,64,1024]{3,2,1,0:T(8,128)(2,1)S(1)}, u32[]{:S(2)}, u32[]{:S(2)}) collective-permute-start(bf16[2,4,64,1024]{3,2,1,0:T(8,128)(2,1)S(1)} %get-tuple-element.173.refs_9_), channel_id=1, source_target_pairs={{0,1},{1,0},{2,3},{3,2},{4,5},{5,4},{6,7},{7,6},{8,9},{9,8},{10,11... | collective-permute-start | bytes 3145736 | tf_op jit(solution)/shard_map/ppermute | solution.py:27
  134.4 27.7 %collective-permute-start.37 = (bf16[2,4,64,1024]{3,2,1,0:T(8,128)(2,1)S(1)}, bf16[2,4,64,1024]{3,2,1,0:T(8,128)(2,1)S(1)}, u32[]{:S(2)}, u32[]{:S(2)}) collective-permute-start(bf16[2,4,64,1024]{3,2,1,0:T(8,128)(2,1)S(1)} %get-tuple-element.189), channel_id=1, source_target_pairs={{0,2},{2,0},{1,3},{3,1},{4,6},{6,4},{5,7},{7,5},{8,10},{10,8},{9,1... | collective-permute-start | bytes 3145736 | tf_op jit(solution)/shard_map/ppermute | solution.py:27
  148.0 16.5 %collective-permute-start.35 = (bf16[512,1024]{1,0:T(8,128)(2,1)S(1)}, bf16[512,1024]{1,0:T(8,128)(2,1)S(1)}, u32[]{:S(2)}, u32[]{:S(2)}) collective-permute-start(bf16[512,1024]{1,0:T(8,128)(2,1)S(1)} %get-tuple-element.178.refs_4_), channel_id=1, source_target_pairs={{0,4},{4,0},{1,5},{5,1},{2,6},{6,2},{3,7},{7,3},{8,12},{12,8},{9,1... | collective-permute-start | bytes 3145736 | tf_op jit(solution)/shard_map/ppermute | solution.py:27
  177.7 27.4 %collective-permute-start.47 = (bf16[2,4,32,2560]{3,2,1,0:T(8,128)(2,1)S(1)}, bf16[2,4,32,2560]{3,2,1,0:T(8,128)(2,1)S(1)}, u32[]{:S(2)}, u32[]{:S(2)}) collective-permute-start(bf16[2,4,32,2560]{3,2,1,0:T(8,128)(2,1)S(1)} %get-tuple-element.208.refs_10_), channel_id=1, source_target_pairs={{0,1},{1,0},{2,3},{3,2},{4,5},{5,4},{6,7},{7,6},{8,9},{9,8},{10,11... | collective-permute-start | bytes 3932168 | tf_op jit(solution)/shard_map/ppermute | solution.py:27
  178.3 28.5 %collective-permute-start.48 = (bf16[2,4,32,2560]{3,2,1,0:T(8,128)(2,1)S(1)}, bf16[2,4,32,2560]{3,2,1,0:T(8,128)(2,1)S(1)}, u32[]{:S(2)}, u32[]{:S(2)}) collective-permute-start(bf16[2,4,32,2560]{3,2,1,0:T(8,128)(2,1)S(1)} %get-tuple-element.211), channel_id=1, source_target_pairs={{0,2},{2,0},{1,3},{3,1},{4,6},{6,4},{5,7},{7,5},{8,10},{10,8},{9,1... | collective-permute-start | bytes 3932168 | tf_op jit(solution)/shard_map/ppermute | solution.py:27
  181.5 16.1 %collective-permute-start.45 = (bf16[128,1024]{1,0:T(8,128)(2,1)S(1)}, bf16[128,1024]{1,0:T(8,128)(2,1)S(1)}, u32[]{:S(2)}, u32[]{:S(2)}) collective-permute-start(bf16[128,1024]{1,0:T(8,128)(2,1)S(1)} %get-tuple-element.204), channel_id=1, source_target_pairs={{0,16},{8,24},{16,0},{24,8},{1,17},{9,25},{17,1},{25,9},{2,18},{10... | collective-permute-start | bytes 786440 | tf_op jit(solution)/shard_map/ppermute | solution.py:33
  221.8 15.8 %collective-permute-start.54 = (bf16[2,4,32,1664]{3,2,1,0:T(8,128)(2,1)}, bf16[2,4,32,1664]{3,2,1,0:T(8,128)(2,1)S(1)}, u32[]{:S(2)}, u32[]{:S(2)}) collective-permute-start(bf16[2,4,32,1664]{3,2,1,0:T(8,128)(2,1)} %get-tuple-element.223), channel_id=1, source_target_pairs={{0,1},{1,0},{2,3},{3,2},{4,5},{5,4},{6,7},{7,6},{8,9},{9,8},{10,11... | collective-permute-start | bytes 2555912 | tf_op jit(solution)/shard_map/ppermute | solution.py:27
  223.0 17.1 %collective-permute-start.55 = (bf16[2,4,32,1664]{3,2,1,0:T(8,128)(2,1)}, bf16[2,4,32,1664]{3,2,1,0:T(8,128)(2,1)S(1)}, u32[]{:S(2)}, u32[]{:S(2)}) collective-permute-start(bf16[2,4,32,1664]{3,2,1,0:T(8,128)(2,1)} %get-tuple-element.226), channel_id=1, source_target_pairs={{0,2},{2,0},{1,3},{3,1},{4,6},{6,4},{5,7},{7,5},{8,10},{10,8},{9,1... | collective-permute-start | bytes 2555912 | tf_op jit(solution)/shard_map/ppermute | solution.py:27
  226.9 18.9 %collective-permute-start.52 = (bf16[64,2560]{1,0:T(8,128)(2,1)}, bf16[64,2560]{1,0:T(8,128)(2,1)}, u32[]{:S(2)}, u32[]{:S(2)}) collective-permute-start(bf16[64,2560]{1,0:T(8,128)(2,1)} %get-tuple-element.216), channel_id=1, source_target_pairs={{0,16},{8,24},{16,0},{24,8},{1,17},{9,25},{17,1},{25,9},{2,18},{10... | collective-permute-start | bytes 983048 | tf_op jit(solution)/shard_map/ppermute | solution.py:33
  233.5 24.6 %collective-permute-start.34 = (bf16[256,1024]{1,0:T(8,128)(2,1)}, bf16[256,1024]{1,0:T(8,128)(2,1)}, u32[]{:S(2)}, u32[]{:S(2)}) collective-permute-start(bf16[256,1024]{1,0:T(8,128)(2,1)} %get-tuple-element.180), channel_id=1, source_target_pairs={{0,4},{4,0},{1,5},{5,1},{2,6},{6,2},{3,7},{7,3},{8,12},{12,8},{9,1... | collective-permute-start | bytes 1572872 | tf_op jit(solution)/shard_map/ppermute | solution.py:27
  245.8 15.3 %collective-permute-start.41 = (bf16[256,1024]{1,0:T(8,128)(2,1)S(1)}, bf16[256,1024]{1,0:T(8,128)(2,1)S(1)}, u32[]{:S(2)}, u32[]{:S(2)}) collective-permute-start(bf16[256,1024]{1,0:T(8,128)(2,1)S(1)} %slice_select_fusion), channel_id=1, source_target_pairs={{0,4},{4,0},{1,5},{5,1},{2,6},{6,2},{3,7},{7,3},{8,12},{12,8},{9,1... | collective-permute-start | bytes 1572872 | tf_op jit(solution)/shard_map/ppermute | solution.py:27
  254.7 17.5 %collective-permute-start.59 = (bf16[64,1664]{1,0:T(8,128)(2,1)S(1)}, bf16[64,1664]{1,0:T(8,128)(2,1)S(1)}, u32[]{:S(2)}, u32[]{:S(2)}) collective-permute-start(bf16[64,1664]{1,0:T(8,128)(2,1)S(1)} %get-tuple-element.231), channel_id=1, source_target_pairs={{0,16},{8,24},{16,0},{24,8},{1,17},{9,25},{17,1},{25,9},{2,18},{10... | collective-permute-start | bytes 638984 | tf_op jit(solution)/shard_map/ppermute | solution.py:33
  (91 other events, 962.4 us)

commit v3 on v2

--- a/solution.py
+++ b/solution.py
@@ -133,13 +133,13 @@
     return jnp.sum(jnp.sum(value * value, axis=1, keepdims=True), axis=0, keepdims=True)
 
 
-def finish_down(parts):
+def finish_down(parts, deps=()):
     def kernel(*refs):
         total = sum_of(refs[: len(parts)])
         refs[-2][...] = total
         refs[-1][...] = spread(total_squares(total))
 
-    return run(kernel, [(parts[0].shape, WIDE), ((8, LANES), WIDE)], *parts, scalars=False)
+    return run(kernel, [(parts[0].shape, WIDE), ((8, LANES), WIDE)], *parts, scalars=False, deps=deps)
 
 
 def finish_up(parts, squares, rows, half_ff):
@@ -349,16 +349,16 @@
     )(coordinates(), qkv, norm)
 
 
-def cast_down(down):
-    half = down.shape[0] // 2
+def cast_down(down, last):
+    rows, cols = down.shape
 
     def kernel(down_ref, one_ref, two_ref):
-        one_ref[...] = down_ref[:half, :].astype(LOW)
-        two_ref[...] = down_ref[half:, :].astype(LOW)
+        one_ref[...] = down_ref[:last, :].astype(LOW)
+        two_ref[...] = down_ref[last:, :].astype(LOW)
 
     return pl.pallas_call(
         kernel,
-        out_shape=[jax.ShapeDtypeStruct((half, down.shape[1]), LOW)] * 2,
+        out_shape=[jax.ShapeDtypeStruct((last, cols), LOW), jax.ShapeDtypeStruct((rows - last, cols), LOW)],
         in_specs=[VMEM],
         out_specs=[VMEM] * 2,
         compiler_params=ROOM,
@@ -855,11 +855,11 @@
     split_qkv = lambda w: jnp.moveaxis(w.reshape(-1, 3 * depth, 2, block), 2, 0).reshape(2, -1, half_qkv)
     split_up = lambda w: jnp.moveaxis(w.reshape(-1, depth, 2, ff_block), 2, 0).reshape(2, -1, half_ff)
 
-    thin, small = own_units // 2, own_rows // 2
+    thin, small, last = own_units // 2, own_rows // 2, 3 * own_units // 8
     if ring:
         qkv_mine, qkv_give = cast_qkv(qkv_weight, norm_params, 3 * depth)
         qkv_part = join_rows(qkv_mine, swap(qkv_give, "c"))
-        down_one, down_two = cast_down(down_weight)
+        down_one, down_two = cast_down(down_weight, last)
         up_mine, up_give, out_part = cast_rest(after(up_weight, qkv_part), out_weight, depth)
         inputs = join_rows(own_x, swap(own_x, "c"))
         up_part = join_rows(up_mine, swap(up_give, "c"), out_part)
@@ -884,7 +884,8 @@
             return moves + [(1, h * own_rows, half_ff, own_rows, half_d, to, h * half_d) for h in (0, 1)]
 
         def down_moves(zz, plane, piece):
-            return [(0, 0, 0, thin, width, zz * ff_block + plane * own_units + piece * thin, 0)]
+            rows = own_units - last if piece else last
+            return [(0, 0, 0, rows, width, zz * ff_block + plane * own_units + piece * last, 0)]
 
         spots = column_first_spots(depth)
         qkv_w, norm_w = place(qkv_parts, depth, [(width, half_qkv), (width, LANES)], spots, qkv_moves)
@@ -923,9 +924,9 @@
             return [(0, zz * ff_block + plane * own_units + half * thin, 0, thin, width, 0, 0)]
 
         down_cut = unplace([down_grad], depth, (thin, width), down_cuts)
-        down_hop = first_hop(*down_cut)
         one_parts = plane_last(after(jnp.stack(one_column), *up_parts[3:]), (down_cut[0][0, 0, :16, :LANES],))
-        spots = spots + plane_first_spots(depth, thin, 5)
+        down_hop = first_hop(*down_cut, one_parts[3:])
+        spots = spots + plane_first_spots(depth, own_units - last, 5)
         down_parts = [*one_parts, *two_parts]
         (down_w,) = place(down_parts, depth, [(half_ff, width)], spots, down_moves, (down_cut[0],))
 
@@ -982,7 +983,7 @@
         turn = second_hop_of(*qkv_hop)
         hop = swap(turn[0], "y"), swap(turn[1], "x")
         qkv_sum = third_hop_of(*qkv_hop, *hop, up_sum[1:])
-        down_red, squares = finish_down(down_sum)
+        down_red, squares = finish_down(down_sum, qkv_sum[:1])
         up_mine, up_give, out_red, squares = finish_up(up_sum, squares, own_rows, half_ff)
         up_mate = swap(up_give, "c")
         deps = (input_grad, activations, up_mate)

time: 300 us -> 292 us (0.973)
  starting transfers between devices: 87.4 us -> 78.3 us
  waiting for transfers between devices: 123 us -> 126 us
    ppermute x26, starting transfers between devices: 46.4 us -> 39.2 us  [shift(): return lax.ppermute(value, 'z', pairs)]
    ppermute x39, waiting for transfers between devices: 59.3 us -> 65.8 us  [swap(): return lax.ppermute(value, axis, SWAP)]
    ppermute x1, waiting for transfers between devices: 3.34 us -> 0.01 us  [plane_first(): far = lax.ppermute(shard, ('y', 'x'), [(i, 3 - i) for i in range(4)])]
    unnamed x95 -> x99, local copies, waits for them, and re-layouts: 15.7 us -> 13.5 us
  transfers between devices with their start and end apart: 69 -> 69, of which waited for: 37 -> 37; matrix products, arithmetic and copies ran while one was open for 2% -> 3% of each run, Pallas kernels for 19% -> 19%
where the time goes in v3:
time: 292 us
  waiting for transfers between devices  126 us (43%)
  starting transfers between devices  78.3 us (27%)
  Pallas kernels  64.5 us (22%)
  local copies, waits for them, and re-layouts  13.8 us (5%)
  matrix products  5.01 us (2%)
    ppermute x39, waiting for transfers between devices, swap(): return lax.ppermute(value, axis, SWAP)  65.8 us
    ppermute x26, waiting for transfers between devices, shift(): return lax.ppermute(value, 'z', pairs)  54.9 us
    pallas_call x21, Pallas kernels, run(): pl.pallas_call(body_of, out_shape=out_shape, in_specs=([pl.BlockSpec(memo...  49.3 us
    ppermute x26, starting transfers between devices, shift(): return lax.ppermute(value, 'z', pairs)  39.2 us
    ppermute x39, starting transfers between devices, swap(): return lax.ppermute(value, axis, SWAP)  30.1 us
    unnamed x99, local copies, waits for them, and re-layouts  13.5 us
    ppermute x2, starting transfers between devices, sum_chips(): lax.ppermute(value, 'z', [(i, i ^ near) for i in range(size)])  6.03 us
  transfers between devices with their start and end apart: 69, of which 37 were waited for; matrix products, arithmetic and copies ran while one was open for 3% of the time, Pallas kernels for 19%

profile of v3, /device:TPU:0, one launch (start us, length us, event | category | flops | bytes accessed | tf_op | source)
XLA Modules:
  0.0 291.8 jit_solution(13024125628274804761)
XLA Ops:
  11.0 3.7 %collective-permute-start.8 = (bf16[64,1664]{1,0:T(8,128)(2,1)S(1)}, bf16[64,1664]{1,0:T(8,128)(2,1)S(1)}, u32[]{:S(2)}, u32[]{:S(2)}) collective-permute-start(bf16[64,1664]{1,0:T(8,128)(2,1)S(1)} %shard_map.306), channel_id=1, source_target_pairs={{0,24},{8,0},{16,8},{24,16},{1,25},{9,1},{17,9},{25,17},{2,26},{10... | collective-permute-start | bytes 638984 | tf_op jit(solution)/shard_map/ppermute | solution.py:33
  17.4 7.0 %collective-permute-done.3 = bf16[80,1024]{1,0:T(8,128)(2,1)S(1)} collective-permute-done((bf16[80,1024]{1,0:T(8,128)(2,1)S(1)}, bf16[80,1024]{1,0:T(8,128)(2,1)S(1)}, u32[]{:S(2)}, u32[]{:S(2)}) %collective-permute-start.3) | collective-permute-done | bytes 163872 | tf_op jit(solution)/shard_map/ppermute | solution.py:27
  25.1 8.2 %collective-permute-done.7 = bf16[64,1664]{1,0:T(8,128)(2,1)S(1)} collective-permute-done((bf16[64,1664]{1,0:T(8,128)(2,1)S(1)}, bf16[64,1664]{1,0:T(8,128)(2,1)S(1)}, u32[]{:S(2)}, u32[]{:S(2)}) %collective-permute-start.7) | collective-permute-done | bytes 213024 | tf_op jit(solution)/shard_map/ppermute | solution.py:33
  41.2 12.7 %collective-permute-done.10.refs_2_ = bf16[4,64,1664]{2,1,0:T(8,128)(2,1)S(1)} collective-permute-done((bf16[4,64,1664]{2,1,0:T(8,128)(2,1)S(1)}, bf16[4,64,1664]{2,1,0:T(8,128)(2,1)S(1)}, u32[]{:S(2)}, u32[]{:S(2)}) %collective-permute-start.10) | collective-permute-done | bytes 852000 | tf_op jit(solution)/shard_map/ppermute | solution.py:27
  56.3 11.2 %collective-permute-done.16 = bf16[64,2560]{1,0:T(8,128)(2,1)S(1)} collective-permute-done((bf16[64,2560]{1,0:T(8,128)(2,1)S(1)}, bf16[64,2560]{1,0:T(8,128)(2,1)S(1)}, u32[]{:S(2)}, u32[]{:S(2)}) %collective-permute-start.16) | collective-permute-done | bytes 327712 | tf_op jit(solution)/shard_map/ppermute | solution.py:33
  71.2 3.2 %shard_map.311 = (f32[8,1024]{1,0:T(8,128)S(1)}, bf16[512,1024]{1,0:T(8,128)(2,1)S(1)}, f32[512,1024]{1,0:T(8,128)S(1)}, bf16[512,512]{1,0:T(8,128)(2,1)S(1)}, b...) custom-call(bf16[512,1024]{1,0:T(8,128)(2,1)S(1)} %shard_map.304.refs_0_.refs_2_, ...), custom_call_target="tpu_custom_call" | custom-call | tf_op jit(solution)/shard_map/pallas_call | solution.py:421
  74.4 4.5 %collective-permute-start.13 = (bf16[272,128]{1,0:T(8,128)(2,1)S(1)}, bf16[272,128]{1,0:T(8,128)(2,1)S(1)}, u32[]{:S(2)}, u32[]{:S(2)}) collective-permute-start(bf16[272,128]{1,0:T(8,128)(2,1)S(1)} %get-tuple-element.157), channel_id=1, source_target_pairs={{0,8},{8,16},{16,24},{1,9},{9,17},{17,25},{2,10},{10,18},{18,26},{... | collective-permute-start | bytes 208904 | tf_op jit(solution)/shard_map/ppermute | solution.py:33
  79.0 8.7 %collective-permute-done.19.refs_6_ = bf16[320,1024]{1,0:T(8,128)(2,1)S(1)} collective-permute-done((bf16[320,1024]{1,0:T(8,128)(2,1)S(1)}, bf16[320,1024]{1,0:T(8,128)(2,1)S(1)}, u32[]{:S(2)}, u32[]{:S(2)}) %collective-permute-start.19) | collective-permute-done | bytes 655392 | tf_op jit(solution)/shard_map/ppermute | solution.py:33
  89.7 3.6 %collective-permute-done.22 = bf16[48,1024]{1,0:T(8,128)(2,1)S(1)} collective-permute-done((bf16[48,1024]{1,0:T(8,128)(2,1)S(1)}, bf16[48,1024]{1,0:T(8,128)(2,1)S(1)}, u32[]{:S(2)}, u32[]{:S(2)}) %collective-permute-start.22) | collective-permute-done | bytes 98336 | tf_op jit(solution)/shard_map/ppermute | solution.py:33
  104.6 4.8 %shard_map.313 = (f32[512,512]{1,0:T(8,128)S(1)}, bf16[512,512]{1,0:T(8,128)(2,1)S(1)}, f32[512,512]{1,0:T(8,128)S(1)}, f32[272,128]{1,0:T(8,128)S(1)}, f32[8,128]{1,0:T(8,128)}) custom-call(bf16[512,512]{1,0:T(8,128)(2,1)S(1)} %get-tuple-element.154.refs_0_.refs_8_, bf16[512,512]{1,0:T(8,128)(2,1)S(1)} %get-tuple-element.155.refs_1_, ...), custom_call_target="tpu_custom_call" | custom-call | tf_op jit(solution)/shard_map/pallas_call | solution.py:421
  118.3 5.7 %shard_map.316 = (f32[512,1024]{1,0:T(8,128)S(1)}, bf16[512,1024]{1,0:T(8,128)(2,1)S(1)}, bf16[512,2048]{1,0:T(8,128)(2,1)S(1)}, f32[512,2048]{1,0:T(8,128)S(1)}) custom-call(bf16[512,1024]{1,0:T(8,128)(2,1)S(1)} %shard_map.304.refs_0_.refs_2_, f32[512,1024]{1,0:T(8,128)S(1)} %get-tuple-element.169.refs_1_, ...), custom_call_target="tpu_custom_call" | custom-call | tf_op jit(solution)/shard_map/pallas_call | solution.py:421
  129.8 4.6 %collective-permute-done.31.refs_3_ = bf16[2,48,1024]{2,1,0:T(8,128)(2,1)S(1)} collective-permute-done((bf16[2,48,1024]{2,1,0:T(8,128)(2,1)S(1)}, bf16[2,48,1024]{2,1,0:T(8,128)(2,1)S(1)}, u32[]{:S(2)}, u32[]{:S(2)}) %collective-permute-start.31) | collective-permute-done | bytes 196640 | tf_op jit(solution)/shard_map/ppermute | solution.py:27
  137.8 5.6 %shard_map.319 = (bf16[512,2048]{1,0:T(8,128)(2,1)S(1)}, f32[512,1024]{1,0:T(8,128)S(1)}, bf16[512,1024]{1,0:T(8,128)(2,1)S(1)}) custom-call(bf16[512,1024]{1,0:T(8,128)(2,1)S(1)} %shard_map.312.refs_5_.refs_0_.refs_4_, bf16[2048,1024]{1,0:T(8,128)(2,1)S(1)} %shard_map.318.refs_1_.refs_2_, f32[512,2048]{1,0:T(8,128)S(1)} %get-tuple-element.179.refs_2_, ...), custom_call_target="tpu_custom_call" | custom-call | tf_op jit(solution)/shard_map/pallas_call | solution.py:421
  143.5 3.0 %shard_map.321.refs_4_.refs_9_.refs_0_ = bf16[1024,2048]{1,0:T(8,128)(2,1)S(1)} custom-call(bf16[512,1024]{1,0:T(8,128)(2,1)S(1)} %get-tuple-element.187.refs_0_, bf16[512,2048]{1,0:T(8,128)(2,1)S(1)} %get-tuple-element.188.refs_1_), custom_call_target="tpu_custom_call" | custom-call | tf_op jit(solution)/shard_map/pallas_call | solution.py:421
  146.5 11.5 %collective-permute-done.36.refs_1_ = bf16[2,4,64,1024]{3,2,1,0:T(8,128)(2,1)S(1)} collective-permute-done((bf16[2,4,64,1024]{3,2,1,0:T(8,128)(2,1)S(1)}, bf16[2,4,64,1024]{3,2,1,0:T(8,128)(2,1)S(1)}, u32[]{:S(2)}, u32[]{:S(2)}) %collective-permute-start.36) | collective-permute-done | bytes 1048608 | tf_op jit(solution)/shard_map/ppermute | solution.py:27
  161.1 3.5 %shard_map.323 = (f32[512,1024]{1,0:T(8,128)S(1)}, bf16[512,1024]{1,0:T(8,128)(2,1)S(1)}, bf16[512,512]{1,0:T(8,128)(2,1)S(1)}, f32[512,512]{1,0:T(8,128)S(1)}, ...) custom-call(f32[512,1024]{1,0:T(8,128)S(1)} %get-tuple-element.184.refs_0_, ...), custom_call_target="tpu_custom_call" | custom-call | tf_op jit(solution)/shard_map/pallas_call | solution.py:421
  183.3 8.9 %shard_map.325.refs_0_.refs_7_ = bf16[512,1536]{1,0:T(8,128)(2,1)S(1)} custom-call(bf16[512,512]{1,0:T(8,128)(2,1)S(1)} %get-tuple-element.154.refs_0_.refs_8_, bf16[512,512]{1,0:T(8,128)(2,1)S(1)} %get-tuple-element.155.refs_1_, bf16[512,512]{1,0:T(8,128)(2,1)S(1)} %get-tuple-element.156.refs_2_, f32[512,1024]{1,0:T(8,128)S(1)} %get-tuple-element.183.refs_3_, ...), custom_call_target="tpu_custom_call" | custom-call | tf_op jit(solution)/shard_map/pallas_call | solution.py:421
  194.0 7.7 %collective-permute-done.47.refs_1_ = bf16[2,4,32,2560]{3,2,1,0:T(8,128)(2,1)S(1)} collective-permute-done((bf16[2,4,32,2560]{3,2,1,0:T(8,128)(2,1)S(1)}, bf16[2,4,32,2560]{3,2,1,0:T(8,128)(2,1)S(1)}, u32[]{:S(2)}, u32[]{:S(2)}) %collective-permute-start.47) | collective-permute-done | bytes 1310752 | tf_op jit(solution)/shard_map/ppermute | solution.py:27
  215.2 3.8 %collective-permute-done.49.refs_4_ = bf16[4,32,2560]{2,1,0:T(8,128)(2,1)S(1)} collective-permute-done((bf16[4,32,2560]{2,1,0:T(8,128)(2,1)S(1)}, bf16[4,32,2560]{2,1,0:T(8,128)(2,1)S(1)}, u32[]{:S(2)}, u32[]{:S(2)}) %collective-permute-start.49) | collective-permute-done | bytes 655392 | tf_op jit(solution)/shard_map/ppermute | solution.py:27
  226.5 3.9 %shard_map.320 = (f32[256,1024]{1,0:T(8,128)S(1)}, bf16[256,1024]{1,0:T(8,128)(2,1)}) custom-call(s32[4]{0:T(128)S(1)} %pad_add_fusion.coords.refs_0_, bf16[512,2048]{1,0:T(8,128)(2,1)S(1)} %get-tuple-element.173.refs_1_, bf16[2048,1024]{1,0:T(8,128)(2,1)S(1)} %shard_map.318.refs_1_.refs_2_, f32[512,1024]{1,0:T(8,128)S(1)} %get-tuple-element.178.refs_3_.refs_2_, ...), custom_call_target="tpu_custom_call" | custom-call | tf_op jit(solution)/shard_map/pallas_call | solution.py:421
  238.1 3.4 %collective-permute-done.56.refs_7_.refs_4_ = bf16[64,2560]{1,0:T(8,128)(2,1)} collective-permute-done((bf16[64,2560]{1,0:T(8,128)(2,1)}, bf16[64,2560]{1,0:T(8,128)(2,1)}, u32[]{:S(2)}, u32[]{:S(2)}) %collective-permute-start.56) | collective-permute-done | bytes 327712 | tf_op jit(solution)/shard_map/ppermute | solution.py:33
  257.7 6.7 %collective-permute-done.59.refs_4_ = bf16[64,1664]{1,0:T(8,128)(2,1)S(1)} collective-permute-done((bf16[64,1664]{1,0:T(8,128)(2,1)S(1)}, bf16[64,1664]{1,0:T(8,128)(2,1)S(1)}, u32[]{:S(2)}, u32[]{:S(2)}) %collective-permute-start.59) | collective-permute-done | bytes 213024 | tf_op jit(solution)/shard_map/ppermute | solution.py:33
  274.5 5.0 %collective-permute-start.67 = (f32[8,128]{1,0:T(8,128)S(1)}, f32[8,128]{1,0:T(8,128)S(1)}, u32[]{:S(2)}, u32[]{:S(2)}) collective-permute-start(f32[8,128]{1,0:T(8,128)S(1)} %add_add_fusion), channel_id=1, source_target_pairs={{0,8},{8,0},{16,24},{24,16},{1,9},{9,1},{17,25},{25,17},{2,10},{10... | collective-permute-start | bytes 12296 | tf_op jit(solution)/shard_map/ppermute | solution.py:200
  286.3 5.3 %shard_map.338 = (f32[32,3072]{1,0:T(8,128)}, f32[32,1024]{1,0:T(8,128)}, f32[32,4096]{1,0:T(8,128)}, f32[128,1024]{1,0:T(8,128)}, f32[4,32]{1,0:T(4,128)}, /*in...) custom-call(s32[4]{0:T(128)} %copy-done.37, ...), custom_call_target="tpu_custom_call" | custom-call | tf_op jit(solution)/shard_map/pallas_call | solution.py:242
  (270 shorter events, 143.8 us)
Async XLA Ops:
  3.7 20.8 %collective-permute-start = (bf16[256,1024]{1,0:T(8,128)(2,1)}, bf16[256,1024]{1,0:T(8,128)(2,1)S(1)}, u32[]{:S(2)}, u32[]{:S(2)}) collective-permute-start(bf16[256,1024]{1,0:T(8,128)(2,1)} %bitcast.31), channel_id=1, source_target_pairs={{0,4},{4,0},{1,5},{5,1},{2,6},{6,2},{3,7},{7,3},{8,12},{12,8},{9,1... | collective-permute-start | bytes 1572872 | tf_op jit(solution)/shard_map/ppermute | solution.py:27
  16.2 17.2 %collective-permute-start.7 = (bf16[64,1664]{1,0:T(8,128)(2,1)S(1)}, bf16[64,1664]{1,0:T(8,128)(2,1)S(1)}, u32[]{:S(2)}, u32[]{:S(2)}) collective-permute-start(bf16[64,1664]{1,0:T(8,128)(2,1)S(1)} %shard_map.306), channel_id=1, source_target_pairs={{0,16},{8,24},{16,0},{24,8},{1,17},{9,25},{17,1},{25,9},{2,18},{10... | collective-permute-start | bytes 638984 | tf_op jit(solution)/shard_map/ppermute | solution.py:33
  33.5 20.4 %collective-permute-start.10 = (bf16[4,64,1664]{2,1,0:T(8,128)(2,1)S(1)}, bf16[4,64,1664]{2,1,0:T(8,128)(2,1)S(1)}, u32[]{:S(2)}, u32[]{:S(2)}) collective-permute-start(bf16[4,64,1664]{2,1,0:T(8,128)(2,1)S(1)} %pad_maximum_fusion.1.refs_0_), channel_id=1, source_target_pairs={{0,2},{2,0},{1,3},{3,1},{4,6},{6,4},{5,7},{7,5},{8,10},{10,8},{9,1... | collective-permute-start | bytes 2555912 | tf_op jit(solution)/shard_map/ppermute | solution.py:27
  35.1 20.4 %collective-permute-start.9 = (bf16[4,64,1664]{2,1,0:T(8,128)(2,1)S(1)}, bf16[4,64,1664]{2,1,0:T(8,128)(2,1)S(1)}, u32[]{:S(2)}, u32[]{:S(2)}) collective-permute-start(bf16[4,64,1664]{2,1,0:T(8,128)(2,1)S(1)} %pad_maximum_fusion.1.refs_0_), channel_id=1, source_target_pairs={{0,1},{1,0},{2,3},{3,2},{4,5},{5,4},{6,7},{7,6},{8,9},{9,8},{10,11... | collective-permute-start | bytes 2555912 | tf_op jit(solution)/shard_map/ppermute | solution.py:27
  35.6 20.7 %collective-permute-start.17 = (bf16[64,2560]{1,0:T(8,128)(2,1)S(1)}, bf16[64,2560]{1,0:T(8,128)(2,1)S(1)}, u32[]{:S(2)}, u32[]{:S(2)}) collective-permute-start(bf16[64,2560]{1,0:T(8,128)(2,1)S(1)} %shard_map.309), channel_id=1, source_target_pairs={{0,24},{8,0},{16,8},{24,16},{1,25},{9,1},{17,9},{25,17},{2,26},{10... | collective-permute-start | bytes 983048 | tf_op jit(solution)/shard_map/ppermute | solution.py:33
  38.1 29.5 %collective-permute-start.16 = (bf16[64,2560]{1,0:T(8,128)(2,1)S(1)}, bf16[64,2560]{1,0:T(8,128)(2,1)S(1)}, u32[]{:S(2)}, u32[]{:S(2)}) collective-permute-start(bf16[64,2560]{1,0:T(8,128)(2,1)S(1)} %shard_map.309), channel_id=1, source_target_pairs={{0,16},{8,24},{16,0},{24,8},{1,17},{9,25},{17,1},{25,9},{2,18},{10... | collective-permute-start | bytes 983048 | tf_op jit(solution)/shard_map/ppermute | solution.py:33
  39.1 28.4 %collective-permute-start.15 = (bf16[64,2560]{1,0:T(8,128)(2,1)S(1)}, bf16[64,2560]{1,0:T(8,128)(2,1)S(1)}, u32[]{:S(2)}, u32[]{:S(2)}) collective-permute-start(bf16[64,2560]{1,0:T(8,128)(2,1)S(1)} %shard_map.309), channel_id=1, source_target_pairs={{0,8},{8,16},{16,24},{24,0},{1,9},{9,17},{17,25},{25,1},{2,10},{10... | collective-permute-start | bytes 983048 | tf_op jit(solution)/shard_map/ppermute | solution.py:33
  67.8 31.9 %collective-permute-start.24 = (bf16[4,64,2560]{2,1,0:T(8,128)(2,1)S(1)}, bf16[4,64,2560]{2,1,0:T(8,128)(2,1)S(1)}, u32[]{:S(2)}, u32[]{:S(2)}) collective-permute-start(bf16[4,64,2560]{2,1,0:T(8,128)(2,1)S(1)} %pad_maximum_fusion.refs_0_), channel_id=1, source_target_pairs={{0,2},{2,0},{1,3},{3,1},{4,6},{6,4},{5,7},{7,5},{8,10},{10,8},{9,1... | collective-permute-start | bytes 3932168 | tf_op jit(solution)/shard_map/ppermute | solution.py:27
  68.3 31.4 %collective-permute-start.23 = (bf16[4,64,2560]{2,1,0:T(8,128)(2,1)S(1)}, bf16[4,64,2560]{2,1,0:T(8,128)(2,1)S(1)}, u32[]{:S(2)}, u32[]{:S(2)}) collective-permute-start(bf16[4,64,2560]{2,1,0:T(8,128)(2,1)S(1)} %pad_maximum_fusion.refs_0_), channel_id=1, source_target_pairs={{0,1},{1,0},{2,3},{3,2},{4,5},{5,4},{6,7},{7,6},{8,9},{9,8},{10,11... | collective-permute-start | bytes 3932168 | tf_op jit(solution)/shard_map/ppermute | solution.py:27
  69.8 17.9 %collective-permute-start.19 = (bf16[320,1024]{1,0:T(8,128)(2,1)S(1)}, bf16[320,1024]{1,0:T(8,128)(2,1)S(1)}, u32[]{:S(2)}, u32[]{:S(2)}) collective-permute-start(bf16[320,1024]{1,0:T(8,128)(2,1)S(1)} %constant_dynamic-update-slice_fusion.refs_5_), channel_id=1, source_target_pairs={{0,8},{8,16},{16,24},{24,0},{1,9},{9,17},{17,25},{25,1},{2,10},{10... | collective-permute-start | bytes 1966088 | tf_op jit(solution)/shard_map/ppermute | solution.py:33
  97.2 15.3 %collective-permute-start.27 = (bf16[320,1024]{1,0:T(8,128)(2,1)S(1)}, bf16[320,1024]{1,0:T(8,128)(2,1)S(1)}, u32[]{:S(2)}, u32[]{:S(2)}) collective-permute-start(bf16[320,1024]{1,0:T(8,128)(2,1)S(1)} %collective-permute-done.19.refs_6_), channel_id=1, source_target_pairs={{0,8},{8,16},{16,24},{24,0},{1,9},{9,17},{17,25},{25,1},{2,10},{10... | collective-permute-start | bytes 1966088 | tf_op jit(solution)/shard_map/ppermute | solution.py:33
  115.1 21.9 %collective-permute-start.33 = (bf16[320,1024]{1,0:T(8,128)(2,1)S(1)}, bf16[320,1024]{1,0:T(8,128)(2,1)S(1)}, u32[]{:S(2)}, u32[]{:S(2)}) collective-permute-start(bf16[320,1024]{1,0:T(8,128)(2,1)S(1)} %collective-permute-done.27.refs_5_.refs_7_), channel_id=1, source_target_pairs={{0,8},{8,16},{16,24},{24,0},{1,9},{9,17},{17,25},{25,1},{2,10},{10... | collective-permute-start | bytes 1966088 | tf_op jit(solution)/shard_map/ppermute | solution.py:33
  135.0 23.0 %collective-permute-start.36 = (bf16[2,4,64,1024]{3,2,1,0:T(8,128)(2,1)S(1)}, bf16[2,4,64,1024]{3,2,1,0:T(8,128)(2,1)S(1)}, u32[]{:S(2)}, u32[]{:S(2)}) collective-permute-start(bf16[2,4,64,1024]{3,2,1,0:T(8,128)(2,1)S(1)} %get-tuple-element.190.refs_9_), channel_id=1, source_target_pairs={{0,1},{1,0},{2,3},{3,2},{4,5},{5,4},{6,7},{7,6},{8,9},{9,8},{10,11... | collective-permute-start | bytes 3145736 | tf_op jit(solution)/shard_map/ppermute | solution.py:27
  136.2 23.0 %collective-permute-start.37 = (bf16[2,4,64,1024]{3,2,1,0:T(8,128)(2,1)S(1)}, bf16[2,4,64,1024]{3,2,1,0:T(8,128)(2,1)S(1)}, u32[]{:S(2)}, u32[]{:S(2)}) collective-permute-start(bf16[2,4,64,1024]{3,2,1,0:T(8,128)(2,1)S(1)} %get-tuple-element.193), channel_id=1, source_target_pairs={{0,2},{2,0},{1,3},{3,1},{4,6},{6,4},{5,7},{7,5},{8,10},{10,8},{9,1... | collective-permute-start | bytes 3145736 | tf_op jit(solution)/shard_map/ppermute | solution.py:27
  143.4 17.7 %collective-permute-start.35 = (bf16[512,1024]{1,0:T(8,128)(2,1)S(1)}, bf16[512,1024]{1,0:T(8,128)(2,1)S(1)}, u32[]{:S(2)}, u32[]{:S(2)}) collective-permute-start(bf16[512,1024]{1,0:T(8,128)(2,1)S(1)} %get-tuple-element.180.refs_4_), channel_id=1, source_target_pairs={{0,4},{4,0},{1,5},{5,1},{2,6},{6,2},{3,7},{7,3},{8,12},{12,8},{9,1... | collective-permute-start | bytes 3145736 | tf_op jit(solution)/shard_map/ppermute | solution.py:27
  159.4 14.8 %collective-permute-start.43 = (bf16[4,64,1024]{2,1,0:T(8,128)(2,1)S(1)}, bf16[4,64,1024]{2,1,0:T(8,128)(2,1)S(1)}, u32[]{:S(2)}, u32[]{:S(2)}) collective-permute-start(bf16[4,64,1024]{2,1,0:T(8,128)(2,1)S(1)} %get-tuple-element.205), channel_id=1, source_target_pairs={{0,1},{1,0},{2,3},{3,2},{4,5},{5,4},{6,7},{7,6},{8,9},{9,8},{10,11... | collective-permute-start | bytes 1572872 | tf_op jit(solution)/shard_map/ppermute | solution.py:27
  174.2 27.6 %collective-permute-start.47 = (bf16[2,4,32,2560]{3,2,1,0:T(8,128)(2,1)S(1)}, bf16[2,4,32,2560]{3,2,1,0:T(8,128)(2,1)S(1)}, u32[]{:S(2)}, u32[]{:S(2)}) collective-permute-start(bf16[2,4,32,2560]{3,2,1,0:T(8,128)(2,1)S(1)} %get-tuple-element.214.refs_10_), channel_id=1, source_target_pairs={{0,1},{1,0},{2,3},{3,2},{4,5},{5,4},{6,7},{7,6},{8,9},{9,8},{10,11... | collective-permute-start | bytes 3932168 | tf_op jit(solution)/shard_map/ppermute | solution.py:27
  175.7 28.5 %collective-permute-start.48 = (bf16[2,4,32,2560]{3,2,1,0:T(8,128)(2,1)S(1)}, bf16[2,4,32,2560]{3,2,1,0:T(8,128)(2,1)S(1)}, u32[]{:S(2)}, u32[]{:S(2)}) collective-permute-start(bf16[2,4,32,2560]{3,2,1,0:T(8,128)(2,1)S(1)} %get-tuple-element.217), channel_id=1, source_target_pairs={{0,2},{2,0},{1,3},{3,1},{4,6},{6,4},{5,7},{7,5},{8,10},{10,8},{9,1... | collective-permute-start | bytes 3932168 | tf_op jit(solution)/shard_map/ppermute | solution.py:27
  177.0 15.3 %collective-permute-start.44 = (bf16[128,1024]{1,0:T(8,128)(2,1)S(1)}, bf16[128,1024]{1,0:T(8,128)(2,1)S(1)}, u32[]{:S(2)}, u32[]{:S(2)}) collective-permute-start(bf16[128,1024]{1,0:T(8,128)(2,1)S(1)} %get-tuple-element.207), channel_id=1, source_target_pairs={{0,8},{8,16},{16,24},{24,0},{1,9},{9,17},{17,25},{25,1},{2,10},{10... | collective-permute-start | bytes 786440 | tf_op jit(solution)/shard_map/ppermute | solution.py:33
  178.4 15.6 %collective-permute-start.45 = (bf16[128,1024]{1,0:T(8,128)(2,1)S(1)}, bf16[128,1024]{1,0:T(8,128)(2,1)S(1)}, u32[]{:S(2)}, u32[]{:S(2)}) collective-permute-start(bf16[128,1024]{1,0:T(8,128)(2,1)S(1)} %get-tuple-element.208), channel_id=1, source_target_pairs={{0,16},{8,24},{16,0},{24,8},{1,17},{9,25},{17,1},{25,9},{2,18},{10... | collective-permute-start | bytes 786440 | tf_op jit(solution)/shard_map/ppermute | solution.py:33
  220.9 15.3 %collective-permute-start.52 = (bf16[2,4,32,1664]{3,2,1,0:T(8,128)(2,1)}, bf16[2,4,32,1664]{3,2,1,0:T(8,128)(2,1)S(1)}, u32[]{:S(2)}, u32[]{:S(2)}) collective-permute-start(bf16[2,4,32,1664]{3,2,1,0:T(8,128)(2,1)} %get-tuple-element.224), channel_id=1, source_target_pairs={{0,2},{2,0},{1,3},{3,1},{4,6},{6,4},{5,7},{7,5},{8,10},{10,8},{9,1... | collective-permute-start | bytes 2555912 | tf_op jit(solution)/shard_map/ppermute | solution.py:27
  223.8 17.8 %collective-permute-start.56 = (bf16[64,2560]{1,0:T(8,128)(2,1)}, bf16[64,2560]{1,0:T(8,128)(2,1)}, u32[]{:S(2)}, u32[]{:S(2)}) collective-permute-start(bf16[64,2560]{1,0:T(8,128)(2,1)} %get-tuple-element.228), channel_id=1, source_target_pairs={{0,16},{8,24},{16,0},{24,8},{1,17},{9,25},{17,1},{25,9},{2,18},{10... | collective-permute-start | bytes 983048 | tf_op jit(solution)/shard_map/ppermute | solution.py:33
  231.4 22.7 %collective-permute-start.34 = (bf16[256,1024]{1,0:T(8,128)(2,1)}, bf16[256,1024]{1,0:T(8,128)(2,1)}, u32[]{:S(2)}, u32[]{:S(2)}) collective-permute-start(bf16[256,1024]{1,0:T(8,128)(2,1)} %get-tuple-element.182), channel_id=1, source_target_pairs={{0,4},{4,0},{1,5},{5,1},{2,6},{6,2},{3,7},{7,3},{8,12},{12,8},{9,1... | collective-permute-start | bytes 1572872 | tf_op jit(solution)/shard_map/ppermute | solution.py:27
  247.7 16.7 %collective-permute-start.59 = (bf16[64,1664]{1,0:T(8,128)(2,1)S(1)}, bf16[64,1664]{1,0:T(8,128)(2,1)S(1)}, u32[]{:S(2)}, u32[]{:S(2)}) collective-permute-start(bf16[64,1664]{1,0:T(8,128)(2,1)S(1)} %get-tuple-element.235), channel_id=1, source_target_pairs={{0,16},{8,24},{16,0},{24,8},{1,17},{9,25},{17,1},{25,9},{2,18},{10... | collective-permute-start | bytes 638984 | tf_op jit(solution)/shard_map/ppermute | solution.py:33
  (93 other events, 986.9 us)

commit v4 on v3

--- a/solution.py
+++ b/solution.py
@@ -860,11 +860,11 @@
         qkv_mine, qkv_give = cast_qkv(qkv_weight, norm_params, 3 * depth)
         qkv_part = join_rows(qkv_mine, swap(qkv_give, "c"))
         down_one, down_two = cast_down(down_weight, last)
-        up_mine, up_give, out_part = cast_rest(after(up_weight, qkv_part), out_weight, depth)
+        two_plane = plane_first(after(down_two, qkv_part))
+        up_mine, up_give, out_part = cast_rest(after(up_weight, two_plane), out_weight, depth)
         inputs = join_rows(own_x, swap(own_x, "c"))
         up_part = join_rows(up_mine, swap(up_give, "c"), out_part)
         qkv_column = column_first(qkv_part)
-        two_plane = plane_first(after(down_two, qkv_part))
         qkv_column = [after(part, two_plane, up_part, inputs) for part in qkv_column]
         up_column = column_first(after(up_part, *qkv_column))
         qkv_parts = plane_last(jnp.stack(qkv_column))

time: 292 us -> 290 us (level)
  waiting for transfers between devices: 126 us -> 113 us
  starting transfers between devices: 78.3 us -> 90.2 us
    ppermute x26, starting transfers between devices: 39.2 us -> 47.2 us  [shift(): return lax.ppermute(value, 'z', pairs)]
    ppermute x26, waiting for transfers between devices: 54.9 us -> 48 us  [shift(): return lax.ppermute(value, 'z', pairs)]
    ppermute x39, waiting for transfers between devices: 65.8 us -> 60 us  [swap(): return lax.ppermute(value, axis, SWAP)]
    ppermute x39, starting transfers between devices: 30.1 us -> 33.9 us  [swap(): return lax.ppermute(value, axis, SWAP)]
  transfers between devices with their start and end apart: 69 -> 69, of which waited for: 37 -> 35; matrix products, arithmetic and copies ran while one was open for 3% -> 3% of each run, Pallas kernels for 19% -> 19%
where the time goes in v4:
time: 290 us; the launch traced here: 289 us
  waiting for transfers between devices  113 us (39%)
  starting transfers between devices  90.2 us (31%)
  Pallas kernels  64.5 us (22%)
  local copies, waits for them, and re-layouts  12 us (4%)
  matrix products  5.01 us (2%)
    ppermute x39, waiting for transfers between devices, swap(): return lax.ppermute(value, axis, SWAP)  60 us
    pallas_call x21, Pallas kernels, run(): pl.pallas_call(body_of, out_shape=out_shape, in_specs=([pl.BlockSpec(memo...  49.2 us
    ppermute x26, waiting for transfers between devices, shift(): return lax.ppermute(value, 'z', pairs)  48 us
    ppermute x26, starting transfers between devices, shift(): return lax.ppermute(value, 'z', pairs)  47.2 us
    ppermute x39, starting transfers between devices, swap(): return lax.ppermute(value, axis, SWAP)  33.9 us
    unnamed x99, local copies, waits for them, and re-layouts  11.6 us
    ppermute x2, starting transfers between devices, sum_chips(): lax.ppermute(value, 'z', [(i, i ^ near) for i in range(size)])  6.03 us
  transfers between devices with their start and end apart: 69, of which 35 were waited for; matrix products, arithmetic and copies ran while one was open for 3% of the time, Pallas kernels for 19%

profile of v4, /device:TPU:0, one launch (start us, length us, event | category | flops | bytes accessed | tf_op | source)
XLA Modules:
  0.0 289.1 jit_solution(7533165367011359156)
XLA Ops:
  8.2 3.6 %collective-permute-start.8 = (bf16[64,1664]{1,0:T(8,128)(2,1)S(1)}, bf16[64,1664]{1,0:T(8,128)(2,1)S(1)}, u32[]{:S(2)}, u32[]{:S(2)}) collective-permute-start(bf16[64,1664]{1,0:T(8,128)(2,1)S(1)} %shard_map.306), channel_id=1, source_target_pairs={{0,24},{8,0},{16,8},{24,16},{1,25},{9,1},{17,9},{25,17},{2,26},{10... | collective-permute-start | bytes 638984 | tf_op jit(solution)/shard_map/ppermute | solution.py:33
  15.5 6.1 %collective-permute-done.3 = bf16[80,1024]{1,0:T(8,128)(2,1)S(1)} collective-permute-done((bf16[80,1024]{1,0:T(8,128)(2,1)S(1)}, bf16[80,1024]{1,0:T(8,128)(2,1)S(1)}, u32[]{:S(2)}, u32[]{:S(2)}) %collective-permute-start.3) | collective-permute-done | bytes 163872 | tf_op jit(solution)/shard_map/ppermute | solution.py:27
  25.7 4.9 %collective-permute-done.7 = bf16[64,1664]{1,0:T(8,128)(2,1)S(1)} collective-permute-done((bf16[64,1664]{1,0:T(8,128)(2,1)S(1)}, bf16[64,1664]{1,0:T(8,128)(2,1)S(1)}, u32[]{:S(2)}, u32[]{:S(2)}) %collective-permute-start.7) | collective-permute-done | bytes 213024 | tf_op jit(solution)/shard_map/ppermute | solution.py:33
  32.8 3.4 %collective-permute-start.17 = (bf16[64,2560]{1,0:T(8,128)(2,1)S(1)}, bf16[64,2560]{1,0:T(8,128)(2,1)S(1)}, u32[]{:S(2)}, u32[]{:S(2)}) collective-permute-start(bf16[64,2560]{1,0:T(8,128)(2,1)S(1)} %shard_map.309), channel_id=1, source_target_pairs={{0,24},{8,0},{16,8},{24,16},{1,25},{9,1},{17,9},{25,17},{2,26},{10... | collective-permute-start | bytes 983048 | tf_op jit(solution)/shard_map/ppermute | solution.py:33
  37.6 13.7 %collective-permute-done.10.refs_2_ = bf16[4,64,1664]{2,1,0:T(8,128)(2,1)S(1)} collective-permute-done((bf16[4,64,1664]{2,1,0:T(8,128)(2,1)S(1)}, bf16[4,64,1664]{2,1,0:T(8,128)(2,1)S(1)}, u32[]{:S(2)}, u32[]{:S(2)}) %collective-permute-start.10) | collective-permute-done | bytes 852000 | tf_op jit(solution)/shard_map/ppermute | solution.py:27
  53.6 9.8 %collective-permute-done.16 = bf16[64,2560]{1,0:T(8,128)(2,1)S(1)} collective-permute-done((bf16[64,2560]{1,0:T(8,128)(2,1)S(1)}, bf16[64,2560]{1,0:T(8,128)(2,1)S(1)}, u32[]{:S(2)}, u32[]{:S(2)}) %collective-permute-start.16) | collective-permute-done | bytes 327712 | tf_op jit(solution)/shard_map/ppermute | solution.py:33
  70.7 4.5 %collective-permute-start.13 = (bf16[272,128]{1,0:T(8,128)(2,1)S(1)}, bf16[272,128]{1,0:T(8,128)(2,1)S(1)}, u32[]{:S(2)}, u32[]{:S(2)}) collective-permute-start(bf16[272,128]{1,0:T(8,128)(2,1)S(1)} %get-tuple-element.157), channel_id=1, source_target_pairs={{0,8},{8,16},{16,24},{1,9},{9,17},{17,25},{2,10},{10,18},{18,26},{... | collective-permute-start | bytes 208904 | tf_op jit(solution)/shard_map/ppermute | solution.py:33
  75.3 6.6 %collective-permute-done.19.refs_6_ = bf16[320,1024]{1,0:T(8,128)(2,1)S(1)} collective-permute-done((bf16[320,1024]{1,0:T(8,128)(2,1)S(1)}, bf16[320,1024]{1,0:T(8,128)(2,1)S(1)}, u32[]{:S(2)}, u32[]{:S(2)}) %collective-permute-start.19) | collective-permute-done | bytes 655392 | tf_op jit(solution)/shard_map/ppermute | solution.py:33
  89.0 4.4 %collective-permute-start.14 = (bf16[272,128]{1,0:T(8,128)(2,1)S(1)}, bf16[272,128]{1,0:T(8,128)(2,1)S(1)}, u32[]{:S(2)}, u32[]{:S(2)}) collective-permute-start(bf16[272,128]{1,0:T(8,128)(2,1)S(1)} %add_convert_fusion.1), channel_id=1, source_target_pairs={{0,16},{8,24},{1,17},{9,25},{2,18},{10,26},{3,19},{11,27},{4,20},{... | collective-permute-start | bytes 208904 | tf_op jit(solution)/shard_map/ppermute | solution.py:33
  100.8 4.8 %shard_map.313 = (f32[512,512]{1,0:T(8,128)S(1)}, bf16[512,512]{1,0:T(8,128)(2,1)S(1)}, f32[512,512]{1,0:T(8,128)S(1)}, f32[272,128]{1,0:T(8,128)S(1)}, f32[8,128]{1,0:T(8,128)}) custom-call(bf16[512,512]{1,0:T(8,128)(2,1)S(1)} %get-tuple-element.154.refs_0_.refs_8_, bf16[512,512]{1,0:T(8,128)(2,1)S(1)} %get-tuple-element.155.refs_1_, ...), custom_call_target="tpu_custom_call" | custom-call | tf_op jit(solution)/shard_map/pallas_call | solution.py:421
  106.7 3.3 %collective-permute-done.27.refs_5_.refs_7_ = bf16[320,1024]{1,0:T(8,128)(2,1)S(1)} collective-permute-done((bf16[320,1024]{1,0:T(8,128)(2,1)S(1)}, bf16[320,1024]{1,0:T(8,128)(2,1)S(1)}, u32[]{:S(2)}, u32[]{:S(2)}) %collective-permute-start.27) | collective-permute-done | bytes 655392 | tf_op jit(solution)/shard_map/ppermute | solution.py:33
  115.6 5.7 %shard_map.316 = (f32[512,1024]{1,0:T(8,128)S(1)}, bf16[512,1024]{1,0:T(8,128)(2,1)S(1)}, bf16[512,2048]{1,0:T(8,128)(2,1)S(1)}, f32[512,2048]{1,0:T(8,128)S(1)}) custom-call(bf16[512,1024]{1,0:T(8,128)(2,1)S(1)} %shard_map.304.refs_0_.refs_2_, f32[512,1024]{1,0:T(8,128)S(1)} %get-tuple-element.169.refs_1_, ...), custom_call_target="tpu_custom_call" | custom-call | tf_op jit(solution)/shard_map/pallas_call | solution.py:421
  127.9 3.5 %collective-permute-done.31.refs_3_ = bf16[2,48,1024]{2,1,0:T(8,128)(2,1)S(1)} collective-permute-done((bf16[2,48,1024]{2,1,0:T(8,128)(2,1)S(1)}, bf16[2,48,1024]{2,1,0:T(8,128)(2,1)S(1)}, u32[]{:S(2)}, u32[]{:S(2)}) %collective-permute-start.31) | collective-permute-done | bytes 196640 | tf_op jit(solution)/shard_map/ppermute | solution.py:27
  135.0 5.6 %shard_map.319 = (bf16[512,2048]{1,0:T(8,128)(2,1)S(1)}, f32[512,1024]{1,0:T(8,128)S(1)}, bf16[512,1024]{1,0:T(8,128)(2,1)S(1)}) custom-call(bf16[512,1024]{1,0:T(8,128)(2,1)S(1)} %shard_map.312.refs_5_.refs_0_.refs_4_, bf16[2048,1024]{1,0:T(8,128)(2,1)S(1)} %shard_map.318.refs_1_.refs_2_, f32[512,2048]{1,0:T(8,128)S(1)} %get-tuple-element.179.refs_2_, ...), custom_call_target="tpu_custom_call" | custom-call | tf_op jit(solution)/shard_map/pallas_call | solution.py:421
  143.7 11.7 %collective-permute-done.36.refs_1_ = bf16[2,4,64,1024]{3,2,1,0:T(8,128)(2,1)S(1)} collective-permute-done((bf16[2,4,64,1024]{3,2,1,0:T(8,128)(2,1)S(1)}, bf16[2,4,64,1024]{3,2,1,0:T(8,128)(2,1)S(1)}, u32[]{:S(2)}, u32[]{:S(2)}) %collective-permute-start.36) | collective-permute-done | bytes 1048608 | tf_op jit(solution)/shard_map/ppermute | solution.py:27
  158.6 3.5 %shard_map.323 = (f32[512,1024]{1,0:T(8,128)S(1)}, bf16[512,1024]{1,0:T(8,128)(2,1)S(1)}, bf16[512,512]{1,0:T(8,128)(2,1)S(1)}, f32[512,512]{1,0:T(8,128)S(1)}, ...) custom-call(f32[512,1024]{1,0:T(8,128)S(1)} %get-tuple-element.184.refs_0_, ...), custom_call_target="tpu_custom_call" | custom-call | tf_op jit(solution)/shard_map/pallas_call | solution.py:421
  180.0 8.9 %shard_map.325.refs_0_.refs_7_ = bf16[512,1536]{1,0:T(8,128)(2,1)S(1)} custom-call(bf16[512,512]{1,0:T(8,128)(2,1)S(1)} %get-tuple-element.154.refs_0_.refs_8_, bf16[512,512]{1,0:T(8,128)(2,1)S(1)} %get-tuple-element.155.refs_1_, bf16[512,512]{1,0:T(8,128)(2,1)S(1)} %get-tuple-element.156.refs_2_, f32[512,1024]{1,0:T(8,128)S(1)} %get-tuple-element.183.refs_3_, ...), custom_call_target="tpu_custom_call" | custom-call | tf_op jit(solution)/shard_map/pallas_call | solution.py:421
  191.0 8.3 %collective-permute-done.47.refs_1_ = bf16[2,4,32,2560]{3,2,1,0:T(8,128)(2,1)S(1)} collective-permute-done((bf16[2,4,32,2560]{3,2,1,0:T(8,128)(2,1)S(1)}, bf16[2,4,32,2560]{3,2,1,0:T(8,128)(2,1)S(1)}, u32[]{:S(2)}, u32[]{:S(2)}) %collective-permute-start.47) | collective-permute-done | bytes 1310752 | tf_op jit(solution)/shard_map/ppermute | solution.py:27
  222.2 3.4 %collective-permute-start.56 = (bf16[64,2560]{1,0:T(8,128)(2,1)}, bf16[64,2560]{1,0:T(8,128)(2,1)}, u32[]{:S(2)}, u32[]{:S(2)}) collective-permute-start(bf16[64,2560]{1,0:T(8,128)(2,1)} %get-tuple-element.228), channel_id=1, source_target_pairs={{0,16},{8,24},{16,0},{24,8},{1,17},{9,25},{17,1},{25,9},{2,18},{10... | collective-permute-start | bytes 983048 | tf_op jit(solution)/shard_map/ppermute | solution.py:33
  225.6 3.9 %shard_map.320 = (f32[256,1024]{1,0:T(8,128)S(1)}, bf16[256,1024]{1,0:T(8,128)(2,1)}) custom-call(s32[4]{0:T(128)S(1)} %pad_add_fusion.coords.refs_0_, bf16[512,2048]{1,0:T(8,128)(2,1)S(1)} %get-tuple-element.173.refs_1_, bf16[2048,1024]{1,0:T(8,128)(2,1)S(1)} %shard_map.318.refs_1_.refs_2_, f32[512,1024]{1,0:T(8,128)S(1)} %get-tuple-element.178.refs_3_.refs_2_, ...), custom_call_target="tpu_custom_call" | custom-call | tf_op jit(solution)/shard_map/pallas_call | solution.py:421
  236.3 4.4 %collective-permute-done.56.refs_7_.refs_4_ = bf16[64,2560]{1,0:T(8,128)(2,1)} collective-permute-done((bf16[64,2560]{1,0:T(8,128)(2,1)}, bf16[64,2560]{1,0:T(8,128)(2,1)}, u32[]{:S(2)}, u32[]{:S(2)}) %collective-permute-start.56) | collective-permute-done | bytes 327712 | tf_op jit(solution)/shard_map/ppermute | solution.py:33
  255.0 7.3 %collective-permute-done.59.refs_4_ = bf16[64,1664]{1,0:T(8,128)(2,1)S(1)} collective-permute-done((bf16[64,1664]{1,0:T(8,128)(2,1)S(1)}, bf16[64,1664]{1,0:T(8,128)(2,1)S(1)}, u32[]{:S(2)}, u32[]{:S(2)}) %collective-permute-start.59) | collective-permute-done | bytes 213024 | tf_op jit(solution)/shard_map/ppermute | solution.py:33
  271.8 5.0 %collective-permute-start.67 = (f32[8,128]{1,0:T(8,128)S(1)}, f32[8,128]{1,0:T(8,128)S(1)}, u32[]{:S(2)}, u32[]{:S(2)}) collective-permute-start(f32[8,128]{1,0:T(8,128)S(1)} %add_add_fusion), channel_id=1, source_target_pairs={{0,8},{8,0},{16,24},{24,16},{1,9},{9,1},{17,25},{25,17},{2,10},{10... | collective-permute-start | bytes 12296 | tf_op jit(solution)/shard_map/ppermute | solution.py:200
  283.6 5.3 %shard_map.338 = (f32[32,3072]{1,0:T(8,128)}, f32[32,1024]{1,0:T(8,128)}, f32[32,4096]{1,0:T(8,128)}, f32[128,1024]{1,0:T(8,128)}, f32[4,32]{1,0:T(4,128)}, /*in...) custom-call(s32[4]{0:T(128)} %copy-done.37, ...), custom_call_target="tpu_custom_call" | custom-call | tf_op jit(solution)/shard_map/pallas_call | solution.py:242
  (270 shorter events, 145.7 us)
Async XLA Ops:
  8.2 16.8 %collective-permute-start = (bf16[256,1024]{1,0:T(8,128)(2,1)}, bf16[256,1024]{1,0:T(8,128)(2,1)S(1)}, u32[]{:S(2)}, u32[]{:S(2)}) collective-permute-start(bf16[256,1024]{1,0:T(8,128)(2,1)} %bitcast.31), channel_id=1, source_target_pairs={{0,4},{4,0},{1,5},{5,1},{2,6},{6,2},{3,7},{7,3},{8,12},{12,8},{9,1... | collective-permute-start | bytes 1572872 | tf_op jit(solution)/shard_map/ppermute | solution.py:27
  8.2 17.5 %collective-permute-start.8 = (bf16[64,1664]{1,0:T(8,128)(2,1)S(1)}, bf16[64,1664]{1,0:T(8,128)(2,1)S(1)}, u32[]{:S(2)}, u32[]{:S(2)}) collective-permute-start(bf16[64,1664]{1,0:T(8,128)(2,1)S(1)} %shard_map.306), channel_id=1, source_target_pairs={{0,24},{8,0},{16,8},{24,16},{1,25},{9,1},{17,9},{25,17},{2,26},{10... | collective-permute-start | bytes 638984 | tf_op jit(solution)/shard_map/ppermute | solution.py:33
  11.8 18.8 %collective-permute-start.7 = (bf16[64,1664]{1,0:T(8,128)(2,1)S(1)}, bf16[64,1664]{1,0:T(8,128)(2,1)S(1)}, u32[]{:S(2)}, u32[]{:S(2)}) collective-permute-start(bf16[64,1664]{1,0:T(8,128)(2,1)S(1)} %shard_map.306), channel_id=1, source_target_pairs={{0,16},{8,24},{16,0},{24,8},{1,17},{9,25},{17,1},{25,9},{2,18},{10... | collective-permute-start | bytes 638984 | tf_op jit(solution)/shard_map/ppermute | solution.py:33
  30.7 20.6 %collective-permute-start.10 = (bf16[4,64,1664]{2,1,0:T(8,128)(2,1)S(1)}, bf16[4,64,1664]{2,1,0:T(8,128)(2,1)S(1)}, u32[]{:S(2)}, u32[]{:S(2)}) collective-permute-start(bf16[4,64,1664]{2,1,0:T(8,128)(2,1)S(1)} %pad_maximum_fusion.1.refs_0_), channel_id=1, source_target_pairs={{0,2},{2,0},{1,3},{3,1},{4,6},{6,4},{5,7},{7,5},{8,10},{10,8},{9,1... | collective-permute-start | bytes 2555912 | tf_op jit(solution)/shard_map/ppermute | solution.py:27
  32.3 20.3 %collective-permute-start.9 = (bf16[4,64,1664]{2,1,0:T(8,128)(2,1)S(1)}, bf16[4,64,1664]{2,1,0:T(8,128)(2,1)S(1)}, u32[]{:S(2)}, u32[]{:S(2)}) collective-permute-start(bf16[4,64,1664]{2,1,0:T(8,128)(2,1)S(1)} %pad_maximum_fusion.1.refs_0_), channel_id=1, source_target_pairs={{0,1},{1,0},{2,3},{3,2},{4,5},{5,4},{6,7},{7,6},{8,9},{9,8},{10,11... | collective-permute-start | bytes 2555912 | tf_op jit(solution)/shard_map/ppermute | solution.py:27
  32.8 20.8 %collective-permute-start.17 = (bf16[64,2560]{1,0:T(8,128)(2,1)S(1)}, bf16[64,2560]{1,0:T(8,128)(2,1)S(1)}, u32[]{:S(2)}, u32[]{:S(2)}) collective-permute-start(bf16[64,2560]{1,0:T(8,128)(2,1)S(1)} %shard_map.309), channel_id=1, source_target_pairs={{0,24},{8,0},{16,8},{24,16},{1,25},{9,1},{17,9},{25,17},{2,26},{10... | collective-permute-start | bytes 983048 | tf_op jit(solution)/shard_map/ppermute | solution.py:33
  36.2 27.2 %collective-permute-start.16 = (bf16[64,2560]{1,0:T(8,128)(2,1)S(1)}, bf16[64,2560]{1,0:T(8,128)(2,1)S(1)}, u32[]{:S(2)}, u32[]{:S(2)}) collective-permute-start(bf16[64,2560]{1,0:T(8,128)(2,1)S(1)} %shard_map.309), channel_id=1, source_target_pairs={{0,16},{8,24},{16,0},{24,8},{1,17},{9,25},{17,1},{25,9},{2,18},{10... | collective-permute-start | bytes 983048 | tf_op jit(solution)/shard_map/ppermute | solution.py:33
  36.2 27.2 %collective-permute-start.15 = (bf16[64,2560]{1,0:T(8,128)(2,1)S(1)}, bf16[64,2560]{1,0:T(8,128)(2,1)S(1)}, u32[]{:S(2)}, u32[]{:S(2)}) collective-permute-start(bf16[64,2560]{1,0:T(8,128)(2,1)S(1)} %shard_map.309), channel_id=1, source_target_pairs={{0,8},{8,16},{16,24},{24,0},{1,9},{9,17},{17,25},{25,1},{2,10},{10... | collective-permute-start | bytes 983048 | tf_op jit(solution)/shard_map/ppermute | solution.py:33
  63.6 32.5 %collective-permute-start.24 = (bf16[4,64,2560]{2,1,0:T(8,128)(2,1)S(1)}, bf16[4,64,2560]{2,1,0:T(8,128)(2,1)S(1)}, u32[]{:S(2)}, u32[]{:S(2)}) collective-permute-start(bf16[4,64,2560]{2,1,0:T(8,128)(2,1)S(1)} %pad_maximum_fusion.refs_0_), channel_id=1, source_target_pairs={{0,2},{2,0},{1,3},{3,1},{4,6},{6,4},{5,7},{7,5},{8,10},{10,8},{9,1... | collective-permute-start | bytes 3932168 | tf_op jit(solution)/shard_map/ppermute | solution.py:27
  64.2 31.9 %collective-permute-start.23 = (bf16[4,64,2560]{2,1,0:T(8,128)(2,1)S(1)}, bf16[4,64,2560]{2,1,0:T(8,128)(2,1)S(1)}, u32[]{:S(2)}, u32[]{:S(2)}) collective-permute-start(bf16[4,64,2560]{2,1,0:T(8,128)(2,1)S(1)} %pad_maximum_fusion.refs_0_), channel_id=1, source_target_pairs={{0,1},{1,0},{2,3},{3,2},{4,5},{5,4},{6,7},{7,6},{8,9},{9,8},{10,11... | collective-permute-start | bytes 3932168 | tf_op jit(solution)/shard_map/ppermute | solution.py:27
  65.7 16.2 %collective-permute-start.19 = (bf16[320,1024]{1,0:T(8,128)(2,1)S(1)}, bf16[320,1024]{1,0:T(8,128)(2,1)S(1)}, u32[]{:S(2)}, u32[]{:S(2)}) collective-permute-start(bf16[320,1024]{1,0:T(8,128)(2,1)S(1)} %constant_dynamic-update-slice_fusion.refs_5_), channel_id=1, source_target_pairs={{0,8},{8,16},{16,24},{24,0},{1,9},{9,17},{17,25},{25,1},{2,10},{10... | collective-permute-start | bytes 1966088 | tf_op jit(solution)/shard_map/ppermute | solution.py:33
  70.7 16.2 %collective-permute-start.13 = (bf16[272,128]{1,0:T(8,128)(2,1)S(1)}, bf16[272,128]{1,0:T(8,128)(2,1)S(1)}, u32[]{:S(2)}, u32[]{:S(2)}) collective-permute-start(bf16[272,128]{1,0:T(8,128)(2,1)S(1)} %get-tuple-element.157), channel_id=1, source_target_pairs={{0,8},{8,16},{16,24},{1,9},{9,17},{17,25},{2,10},{10,18},{18,26},{... | collective-permute-start | bytes 208904 | tf_op jit(solution)/shard_map/ppermute | solution.py:33
  111.7 22.4 %collective-permute-start.33 = (bf16[320,1024]{1,0:T(8,128)(2,1)S(1)}, bf16[320,1024]{1,0:T(8,128)(2,1)S(1)}, u32[]{:S(2)}, u32[]{:S(2)}) collective-permute-start(bf16[320,1024]{1,0:T(8,128)(2,1)S(1)} %collective-permute-done.27.refs_5_.refs_7_), channel_id=1, source_target_pairs={{0,8},{8,16},{16,24},{24,0},{1,9},{9,17},{17,25},{25,1},{2,10},{10... | collective-permute-start | bytes 1966088 | tf_op jit(solution)/shard_map/ppermute | solution.py:33
  132.3 23.0 %collective-permute-start.36 = (bf16[2,4,64,1024]{3,2,1,0:T(8,128)(2,1)S(1)}, bf16[2,4,64,1024]{3,2,1,0:T(8,128)(2,1)S(1)}, u32[]{:S(2)}, u32[]{:S(2)}) collective-permute-start(bf16[2,4,64,1024]{3,2,1,0:T(8,128)(2,1)S(1)} %get-tuple-element.190.refs_9_), channel_id=1, source_target_pairs={{0,1},{1,0},{2,3},{3,2},{4,5},{5,4},{6,7},{7,6},{8,9},{9,8},{10,11... | collective-permute-start | bytes 3145736 | tf_op jit(solution)/shard_map/ppermute | solution.py:27
  133.2 22.7 %collective-permute-start.37 = (bf16[2,4,64,1024]{3,2,1,0:T(8,128)(2,1)S(1)}, bf16[2,4,64,1024]{3,2,1,0:T(8,128)(2,1)S(1)}, u32[]{:S(2)}, u32[]{:S(2)}) collective-permute-start(bf16[2,4,64,1024]{3,2,1,0:T(8,128)(2,1)S(1)} %get-tuple-element.193), channel_id=1, source_target_pairs={{0,2},{2,0},{1,3},{3,1},{4,6},{6,4},{5,7},{7,5},{8,10},{10,8},{9,1... | collective-permute-start | bytes 3145736 | tf_op jit(solution)/shard_map/ppermute | solution.py:27
  140.6 18.0 %collective-permute-start.35 = (bf16[512,1024]{1,0:T(8,128)(2,1)S(1)}, bf16[512,1024]{1,0:T(8,128)(2,1)S(1)}, u32[]{:S(2)}, u32[]{:S(2)}) collective-permute-start(bf16[512,1024]{1,0:T(8,128)(2,1)S(1)} %get-tuple-element.180.refs_4_), channel_id=1, source_target_pairs={{0,4},{4,0},{1,5},{5,1},{2,6},{6,2},{3,7},{7,3},{8,12},{12,8},{9,1... | collective-permute-start | bytes 3145736 | tf_op jit(solution)/shard_map/ppermute | solution.py:27
  156.2 15.5 %collective-permute-start.43 = (bf16[4,64,1024]{2,1,0:T(8,128)(2,1)S(1)}, bf16[4,64,1024]{2,1,0:T(8,128)(2,1)S(1)}, u32[]{:S(2)}, u32[]{:S(2)}) collective-permute-start(bf16[4,64,1024]{2,1,0:T(8,128)(2,1)S(1)} %get-tuple-element.205), channel_id=1, source_target_pairs={{0,1},{1,0},{2,3},{3,2},{4,5},{5,4},{6,7},{7,6},{8,9},{9,8},{10,11... | collective-permute-start | bytes 1572872 | tf_op jit(solution)/shard_map/ppermute | solution.py:27
  171.6 27.6 %collective-permute-start.47 = (bf16[2,4,32,2560]{3,2,1,0:T(8,128)(2,1)S(1)}, bf16[2,4,32,2560]{3,2,1,0:T(8,128)(2,1)S(1)}, u32[]{:S(2)}, u32[]{:S(2)}) collective-permute-start(bf16[2,4,32,2560]{3,2,1,0:T(8,128)(2,1)S(1)} %get-tuple-element.214.refs_10_), channel_id=1, source_target_pairs={{0,1},{1,0},{2,3},{3,2},{4,5},{5,4},{6,7},{7,6},{8,9},{9,8},{10,11... | collective-permute-start | bytes 3932168 | tf_op jit(solution)/shard_map/ppermute | solution.py:27
  172.4 28.5 %collective-permute-start.48 = (bf16[2,4,32,2560]{3,2,1,0:T(8,128)(2,1)S(1)}, bf16[2,4,32,2560]{3,2,1,0:T(8,128)(2,1)S(1)}, u32[]{:S(2)}, u32[]{:S(2)}) collective-permute-start(bf16[2,4,32,2560]{3,2,1,0:T(8,128)(2,1)S(1)} %get-tuple-element.217), channel_id=1, source_target_pairs={{0,2},{2,0},{1,3},{3,1},{4,6},{6,4},{5,7},{7,5},{8,10},{10,8},{9,1... | collective-permute-start | bytes 3932168 | tf_op jit(solution)/shard_map/ppermute | solution.py:27
  175.4 15.6 %collective-permute-start.45 = (bf16[128,1024]{1,0:T(8,128)(2,1)S(1)}, bf16[128,1024]{1,0:T(8,128)(2,1)S(1)}, u32[]{:S(2)}, u32[]{:S(2)}) collective-permute-start(bf16[128,1024]{1,0:T(8,128)(2,1)S(1)} %get-tuple-element.208), channel_id=1, source_target_pairs={{0,16},{8,24},{16,0},{24,8},{1,17},{9,25},{17,1},{25,9},{2,18},{10... | collective-permute-start | bytes 786440 | tf_op jit(solution)/shard_map/ppermute | solution.py:33
  202.4 15.1 %collective-permute-start.50 = (bf16[4,32,2560]{2,1,0:T(8,128)(2,1)S(1)}, bf16[4,32,2560]{2,1,0:T(8,128)(2,1)S(1)}, u32[]{:S(2)}, u32[]{:S(2)}) collective-permute-start(bf16[4,32,2560]{2,1,0:T(8,128)(2,1)S(1)} %get-tuple-element.219), channel_id=1, source_target_pairs={{0,1},{1,0},{2,3},{3,2},{4,5},{5,4},{6,7},{7,6},{8,9},{9,8},{10,11... | collective-permute-start | bytes 1966088 | tf_op jit(solution)/shard_map/ppermute | solution.py:27
  222.2 18.5 %collective-permute-start.56 = (bf16[64,2560]{1,0:T(8,128)(2,1)}, bf16[64,2560]{1,0:T(8,128)(2,1)}, u32[]{:S(2)}, u32[]{:S(2)}) collective-permute-start(bf16[64,2560]{1,0:T(8,128)(2,1)} %get-tuple-element.228), channel_id=1, source_target_pairs={{0,16},{8,24},{16,0},{24,8},{1,17},{9,25},{17,1},{25,9},{2,18},{10... | collective-permute-start | bytes 983048 | tf_op jit(solution)/shard_map/ppermute | solution.py:33
  230.5 20.9 %collective-permute-start.34 = (bf16[256,1024]{1,0:T(8,128)(2,1)}, bf16[256,1024]{1,0:T(8,128)(2,1)}, u32[]{:S(2)}, u32[]{:S(2)}) collective-permute-start(bf16[256,1024]{1,0:T(8,128)(2,1)} %get-tuple-element.182), channel_id=1, source_target_pairs={{0,4},{4,0},{1,5},{5,1},{2,6},{6,2},{3,7},{7,3},{8,12},{12,8},{9,1... | collective-permute-start | bytes 1572872 | tf_op jit(solution)/shard_map/ppermute | solution.py:27
  245.8 16.5 %collective-permute-start.59 = (bf16[64,1664]{1,0:T(8,128)(2,1)S(1)}, bf16[64,1664]{1,0:T(8,128)(2,1)S(1)}, u32[]{:S(2)}, u32[]{:S(2)}) collective-permute-start(bf16[64,1664]{1,0:T(8,128)(2,1)S(1)} %get-tuple-element.235), channel_id=1, source_target_pairs={{0,16},{8,24},{16,0},{24,8},{1,17},{9,25},{17,1},{25,9},{2,18},{10... | collective-permute-start | bytes 638984 | tf_op jit(solution)/shard_map/ppermute | solution.py:33
  (93 other events, 1019.1 us)

commit v5 on v4

--- a/solution.py
+++ b/solution.py
@@ -62,9 +62,9 @@
     return (column, along_x, along_y) + far
 
 
-def plane_first(shard):
-    far = lax.ppermute(shard, ("y", "x"), [(i, 3 - i) for i in range(4)])
-    return jnp.concatenate([shard, swap(shard, "x"), swap(shard, "y"), far])
+def plane_first(shard, along_x, along_y, *before):
+    far = lax.ppermute(after(shard, *before), ("y", "x"), [(i, 3 - i) for i in range(4)])
+    return jnp.concatenate([shard, along_x, along_y, far])
 
 
 def column_last(plane):
@@ -860,11 +860,13 @@
         qkv_mine, qkv_give = cast_qkv(qkv_weight, norm_params, 3 * depth)
         qkv_part = join_rows(qkv_mine, swap(qkv_give, "c"))
         down_one, down_two = cast_down(down_weight, last)
-        two_plane = plane_first(after(down_two, qkv_part))
-        up_mine, up_give, out_part = cast_rest(after(up_weight, two_plane), out_weight, depth)
+        down_two = after(down_two, qkv_part)
+        along = swap(down_two, "x"), swap(down_two, "y")
+        up_mine, up_give, out_part = cast_rest(after(up_weight, along[0]), out_weight, depth)
         inputs = join_rows(own_x, swap(own_x, "c"))
         up_part = join_rows(up_mine, swap(up_give, "c"), out_part)
         qkv_column = column_first(qkv_part)
+        two_plane = plane_first(down_two, *along, qkv_column[1])
         qkv_column = [after(part, two_plane, up_part, inputs) for part in qkv_column]
         up_column = column_first(after(up_part, *qkv_column))
         qkv_parts = plane_last(jnp.stack(qkv_column))

time: 290 us -> 291 us (level)
  waiting for transfers between devices: 113 us -> 118 us
  starting transfers between devices: 90.2 us -> 85.7 us
    ppermute x39, starting transfers between devices: 33.9 us -> 27.8 us  [swap(): return lax.ppermute(value, axis, SWAP)]
    ppermute x39, waiting for transfers between devices: 60 us -> 64.7 us  [swap(): return lax.ppermute(value, axis, SWAP)]
  transfers between devices with their start and end apart: 69 -> 69, of which waited for: 35 -> 40; matrix products, arithmetic and copies ran while one was open for 3% -> 3% of each run, Pallas kernels for 19% -> 19%
where the time goes in v5:
time: 291 us
  waiting for transfers between devices  118 us (41%)
  starting transfers between devices  85.7 us (29%)
  Pallas kernels  64.5 us (22%)
  local copies, waits for them, and re-layouts  13.8 us (5%)
  matrix products  5.01 us (2%)
    ppermute x39, waiting for transfers between devices, swap(): return lax.ppermute(value, axis, SWAP)  64.7 us
    pallas_call x21, Pallas kernels, run(): pl.pallas_call(body_of, out_shape=out_shape, in_specs=([pl.BlockSpec(memo...  49.2 us
    ppermute x26, starting transfers between devices, shift(): return lax.ppermute(value, 'z', pairs)  48.8 us
    ppermute x26, waiting for transfers between devices, shift(): return lax.ppermute(value, 'z', pairs)  46.1 us
    ppermute x39, starting transfers between devices, swap(): return lax.ppermute(value, axis, SWAP)  27.8 us
    unnamed x99, local copies, waits for them, and re-layouts  13.5 us
    ppermute x2, starting transfers between devices, sum_chips(): lax.ppermute(value, 'z', [(i, i ^ near) for i in range(size)])  6.09 us
  transfers between devices with their start and end apart: 69, of which 40 were waited for; matrix products, arithmetic and copies ran while one was open for 3% of the time, Pallas kernels for 19%

profile of v5, /device:TPU:0, one launch (start us, length us, event | category | flops | bytes accessed | tf_op | source)
XLA Modules:
  0.0 290.9 jit_solution(14901209889242363271)
XLA Ops:
  26.7 7.2 %collective-permute-done.7 = bf16[64,1664]{1,0:T(8,128)(2,1)S(1)} collective-permute-done((bf16[64,1664]{1,0:T(8,128)(2,1)S(1)}, bf16[64,1664]{1,0:T(8,128)(2,1)S(1)}, u32[]{:S(2)}, u32[]{:S(2)}) %collective-permute-start.7) | collective-permute-done | bytes 213024 | tf_op jit(solution)/shard_map/ppermute | solution.py:33
  37.8 16.5 %collective-permute-done.10.refs_2_ = bf16[4,64,1664]{2,1,0:T(8,128)(2,1)S(1)} collective-permute-done((bf16[4,64,1664]{2,1,0:T(8,128)(2,1)S(1)}, bf16[4,64,1664]{2,1,0:T(8,128)(2,1)S(1)}, u32[]{:S(2)}, u32[]{:S(2)}) %collective-permute-start.10) | collective-permute-done | bytes 852000 | tf_op jit(solution)/shard_map/ppermute | solution.py:27
  56.2 7.1 %collective-permute-done.16 = bf16[64,2560]{1,0:T(8,128)(2,1)S(1)} collective-permute-done((bf16[64,2560]{1,0:T(8,128)(2,1)S(1)}, bf16[64,2560]{1,0:T(8,128)(2,1)S(1)}, u32[]{:S(2)}, u32[]{:S(2)}) %collective-permute-start.16) | collective-permute-done | bytes 327712 | tf_op jit(solution)/shard_map/ppermute | solution.py:33
  68.4 3.2 %shard_map.311 = (f32[8,1024]{1,0:T(8,128)S(1)}, bf16[512,1024]{1,0:T(8,128)(2,1)S(1)}, f32[512,1024]{1,0:T(8,128)S(1)}, bf16[512,512]{1,0:T(8,128)(2,1)S(1)}, b...) custom-call(bf16[512,1024]{1,0:T(8,128)(2,1)S(1)} %shard_map.304.refs_0_.refs_2_, ...), custom_call_target="tpu_custom_call" | custom-call | tf_op jit(solution)/shard_map/pallas_call | solution.py:421
  71.6 4.5 %collective-permute-start.13 = (bf16[272,128]{1,0:T(8,128)(2,1)S(1)}, bf16[272,128]{1,0:T(8,128)(2,1)S(1)}, u32[]{:S(2)}, u32[]{:S(2)}) collective-permute-start(bf16[272,128]{1,0:T(8,128)(2,1)S(1)} %get-tuple-element.159), channel_id=1, source_target_pairs={{0,8},{8,16},{16,24},{1,9},{9,17},{17,25},{2,10},{10,18},{18,26},{... | collective-permute-start | bytes 208904 | tf_op jit(solution)/shard_map/ppermute | solution.py:33
  76.2 5.9 %collective-permute-done.19.refs_6_ = bf16[320,1024]{1,0:T(8,128)(2,1)S(1)} collective-permute-done((bf16[320,1024]{1,0:T(8,128)(2,1)S(1)}, bf16[320,1024]{1,0:T(8,128)(2,1)S(1)}, u32[]{:S(2)}, u32[]{:S(2)}) %collective-permute-start.19) | collective-permute-done | bytes 655392 | tf_op jit(solution)/shard_map/ppermute | solution.py:33
  82.1 3.1 %collective-permute-start.22 = (bf16[48,1024]{1,0:T(8,128)(2,1)S(1)}, bf16[48,1024]{1,0:T(8,128)(2,1)S(1)}, u32[]{:S(2)}, u32[]{:S(2)}) collective-permute-start(bf16[48,1024]{1,0:T(8,128)(2,1)S(1)} %get-tuple-element.166), channel_id=1, source_target_pairs={{0,24},{8,0},{16,8},{24,16},{1,25},{9,1},{17,9},{25,17},{2,26},{10... | collective-permute-start | bytes 294920 | tf_op jit(solution)/shard_map/ppermute | solution.py:33
  87.9 4.0 %collective-permute-start.14 = (bf16[272,128]{1,0:T(8,128)(2,1)S(1)}, bf16[272,128]{1,0:T(8,128)(2,1)S(1)}, u32[]{:S(2)}, u32[]{:S(2)}) collective-permute-start(bf16[272,128]{1,0:T(8,128)(2,1)S(1)} %add_convert_fusion.1), channel_id=1, source_target_pairs={{0,16},{8,24},{1,17},{9,25},{2,18},{10,26},{3,19},{11,27},{4,20},{... | collective-permute-start | bytes 208904 | tf_op jit(solution)/shard_map/ppermute | solution.py:33
  101.0 4.8 %shard_map.313 = (f32[512,512]{1,0:T(8,128)S(1)}, bf16[512,512]{1,0:T(8,128)(2,1)S(1)}, f32[512,512]{1,0:T(8,128)S(1)}, f32[272,128]{1,0:T(8,128)S(1)}, f32[8,128]{1,0:T(8,128)}) custom-call(bf16[512,512]{1,0:T(8,128)(2,1)S(1)} %get-tuple-element.156.refs_0_.refs_8_, bf16[512,512]{1,0:T(8,128)(2,1)S(1)} %get-tuple-element.157.refs_1_, ...), custom_call_target="tpu_custom_call" | custom-call | tf_op jit(solution)/shard_map/pallas_call | solution.py:421
  106.9 4.1 %collective-permute-done.27.refs_5_.refs_7_ = bf16[320,1024]{1,0:T(8,128)(2,1)S(1)} collective-permute-done((bf16[320,1024]{1,0:T(8,128)(2,1)S(1)}, bf16[320,1024]{1,0:T(8,128)(2,1)S(1)}, u32[]{:S(2)}, u32[]{:S(2)}) %collective-permute-start.27) | collective-permute-done | bytes 655392 | tf_op jit(solution)/shard_map/ppermute | solution.py:33
  115.3 5.7 %shard_map.316 = (f32[512,1024]{1,0:T(8,128)S(1)}, bf16[512,1024]{1,0:T(8,128)(2,1)S(1)}, bf16[512,2048]{1,0:T(8,128)(2,1)S(1)}, f32[512,2048]{1,0:T(8,128)S(1)}) custom-call(bf16[512,1024]{1,0:T(8,128)(2,1)S(1)} %shard_map.304.refs_0_.refs_2_, f32[512,1024]{1,0:T(8,128)S(1)} %get-tuple-element.171.refs_1_, ...), custom_call_target="tpu_custom_call" | custom-call | tf_op jit(solution)/shard_map/pallas_call | solution.py:421
  127.9 4.1 %collective-permute-done.31.refs_3_ = bf16[2,48,1024]{2,1,0:T(8,128)(2,1)S(1)} collective-permute-done((bf16[2,48,1024]{2,1,0:T(8,128)(2,1)S(1)}, bf16[2,48,1024]{2,1,0:T(8,128)(2,1)S(1)}, u32[]{:S(2)}, u32[]{:S(2)}) %collective-permute-start.31) | collective-permute-done | bytes 196640 | tf_op jit(solution)/shard_map/ppermute | solution.py:27
  135.6 5.6 %shard_map.319 = (bf16[512,2048]{1,0:T(8,128)(2,1)S(1)}, f32[512,1024]{1,0:T(8,128)S(1)}, bf16[512,1024]{1,0:T(8,128)(2,1)S(1)}) custom-call(bf16[512,1024]{1,0:T(8,128)(2,1)S(1)} %shard_map.312.refs_5_.refs_0_.refs_4_, bf16[2048,1024]{1,0:T(8,128)(2,1)S(1)} %shard_map.318.refs_1_.refs_2_, f32[512,2048]{1,0:T(8,128)S(1)} %get-tuple-element.181.refs_2_, ...), custom_call_target="tpu_custom_call" | custom-call | tf_op jit(solution)/shard_map/pallas_call | solution.py:421
  144.3 11.4 %collective-permute-done.36.refs_1_ = bf16[2,4,64,1024]{3,2,1,0:T(8,128)(2,1)S(1)} collective-permute-done((bf16[2,4,64,1024]{3,2,1,0:T(8,128)(2,1)S(1)}, bf16[2,4,64,1024]{3,2,1,0:T(8,128)(2,1)S(1)}, u32[]{:S(2)}, u32[]{:S(2)}) %collective-permute-start.36) | collective-permute-done | bytes 1048608 | tf_op jit(solution)/shard_map/ppermute | solution.py:27
  158.6 3.5 %shard_map.323 = (f32[512,1024]{1,0:T(8,128)S(1)}, bf16[512,1024]{1,0:T(8,128)(2,1)S(1)}, bf16[512,512]{1,0:T(8,128)(2,1)S(1)}, f32[512,512]{1,0:T(8,128)S(1)}, ...) custom-call(f32[512,1024]{1,0:T(8,128)S(1)} %get-tuple-element.186.refs_0_, ...), custom_call_target="tpu_custom_call" | custom-call | tf_op jit(solution)/shard_map/pallas_call | solution.py:421
  181.0 8.9 %shard_map.325.refs_0_.refs_7_ = bf16[512,1536]{1,0:T(8,128)(2,1)S(1)} custom-call(bf16[512,512]{1,0:T(8,128)(2,1)S(1)} %get-tuple-element.156.refs_0_.refs_8_, bf16[512,512]{1,0:T(8,128)(2,1)S(1)} %get-tuple-element.157.refs_1_, bf16[512,512]{1,0:T(8,128)(2,1)S(1)} %get-tuple-element.158.refs_2_, f32[512,1024]{1,0:T(8,128)S(1)} %get-tuple-element.185.refs_3_, ...), custom_call_target="tpu_custom_call" | custom-call | tf_op jit(solution)/shard_map/pallas_call | solution.py:421
  191.4 7.4 %collective-permute-done.47.refs_1_ = bf16[2,4,32,2560]{3,2,1,0:T(8,128)(2,1)S(1)} collective-permute-done((bf16[2,4,32,2560]{3,2,1,0:T(8,128)(2,1)S(1)}, bf16[2,4,32,2560]{3,2,1,0:T(8,128)(2,1)S(1)}, u32[]{:S(2)}, u32[]{:S(2)}) %collective-permute-start.47) | collective-permute-done | bytes 1310752 | tf_op jit(solution)/shard_map/ppermute | solution.py:27
  212.7 3.3 %collective-permute-done.49.refs_4_ = bf16[4,32,2560]{2,1,0:T(8,128)(2,1)S(1)} collective-permute-done((bf16[4,32,2560]{2,1,0:T(8,128)(2,1)S(1)}, bf16[4,32,2560]{2,1,0:T(8,128)(2,1)S(1)}, u32[]{:S(2)}, u32[]{:S(2)}) %collective-permute-start.49) | collective-permute-done | bytes 655392 | tf_op jit(solution)/shard_map/ppermute | solution.py:27
  221.4 3.3 %collective-permute-start.56 = (bf16[64,2560]{1,0:T(8,128)(2,1)}, bf16[64,2560]{1,0:T(8,128)(2,1)}, u32[]{:S(2)}, u32[]{:S(2)}) collective-permute-start(bf16[64,2560]{1,0:T(8,128)(2,1)} %get-tuple-element.230), channel_id=1, source_target_pairs={{0,16},{8,24},{16,0},{24,8},{1,17},{9,25},{17,1},{25,9},{2,18},{10... | collective-permute-start | bytes 983048 | tf_op jit(solution)/shard_map/ppermute | solution.py:33
  224.6 3.9 %shard_map.320 = (f32[256,1024]{1,0:T(8,128)S(1)}, bf16[256,1024]{1,0:T(8,128)(2,1)}) custom-call(s32[4]{0:T(128)S(1)} %pad_add_fusion.coords.refs_0_, bf16[512,2048]{1,0:T(8,128)(2,1)S(1)} %get-tuple-element.175.refs_1_, bf16[2048,1024]{1,0:T(8,128)(2,1)S(1)} %shard_map.318.refs_1_.refs_2_, f32[512,1024]{1,0:T(8,128)S(1)} %get-tuple-element.180.refs_3_.refs_2_, ...), custom_call_target="tpu_custom_call" | custom-call | tf_op jit(solution)/shard_map/pallas_call | solution.py:421
  235.6 4.2 %collective-permute-done.56.refs_7_.refs_4_ = bf16[64,2560]{1,0:T(8,128)(2,1)} collective-permute-done((bf16[64,2560]{1,0:T(8,128)(2,1)}, bf16[64,2560]{1,0:T(8,128)(2,1)}, u32[]{:S(2)}, u32[]{:S(2)}) %collective-permute-start.56) | collective-permute-done | bytes 327712 | tf_op jit(solution)/shard_map/ppermute | solution.py:33
  256.8 6.7 %collective-permute-done.59.refs_4_ = bf16[64,1664]{1,0:T(8,128)(2,1)S(1)} collective-permute-done((bf16[64,1664]{1,0:T(8,128)(2,1)S(1)}, bf16[64,1664]{1,0:T(8,128)(2,1)S(1)}, u32[]{:S(2)}, u32[]{:S(2)}) %collective-permute-start.59) | collective-permute-done | bytes 213024 | tf_op jit(solution)/shard_map/ppermute | solution.py:33
  273.5 5.1 %collective-permute-start.67 = (f32[8,128]{1,0:T(8,128)S(1)}, f32[8,128]{1,0:T(8,128)S(1)}, u32[]{:S(2)}, u32[]{:S(2)}) collective-permute-start(f32[8,128]{1,0:T(8,128)S(1)} %add_add_fusion), channel_id=1, source_target_pairs={{0,8},{8,0},{16,24},{24,16},{1,9},{9,1},{17,25},{25,17},{2,10},{10... | collective-permute-start | bytes 12296 | tf_op jit(solution)/shard_map/ppermute | solution.py:200
  285.4 5.3 %shard_map.338 = (f32[32,3072]{1,0:T(8,128)}, f32[32,1024]{1,0:T(8,128)}, f32[32,4096]{1,0:T(8,128)}, f32[128,1024]{1,0:T(8,128)}, f32[4,32]{1,0:T(4,128)}, /*in...) custom-call(s32[4]{0:T(128)} %copy-done.37, ...), custom_call_target="tpu_custom_call" | custom-call | tf_op jit(solution)/shard_map/pallas_call | solution.py:242
  (270 shorter events, 150.6 us)
Async XLA Ops:
  8.2 17.9 %collective-permute-start = (bf16[256,1024]{1,0:T(8,128)(2,1)}, bf16[256,1024]{1,0:T(8,128)(2,1)S(1)}, u32[]{:S(2)}, u32[]{:S(2)}) collective-permute-start(bf16[256,1024]{1,0:T(8,128)(2,1)} %bitcast.31), channel_id=1, source_target_pairs={{0,4},{4,0},{1,5},{5,1},{2,6},{6,2},{3,7},{7,3},{8,12},{12,8},{9,1... | collective-permute-start | bytes 1572872 | tf_op jit(solution)/shard_map/ppermute | solution.py:27
  10.8 15.9 %collective-permute-start.8 = (bf16[64,1664]{1,0:T(8,128)(2,1)S(1)}, bf16[64,1664]{1,0:T(8,128)(2,1)S(1)}, u32[]{:S(2)}, u32[]{:S(2)}) collective-permute-start(bf16[64,1664]{1,0:T(8,128)(2,1)S(1)} %shard_map.306), channel_id=1, source_target_pairs={{0,24},{8,0},{16,8},{24,16},{1,25},{9,1},{17,9},{25,17},{2,26},{10... | collective-permute-start | bytes 638984 | tf_op jit(solution)/shard_map/ppermute | solution.py:33
  34.1 20.2 %collective-permute-start.10 = (bf16[4,64,1664]{2,1,0:T(8,128)(2,1)S(1)}, bf16[4,64,1664]{2,1,0:T(8,128)(2,1)S(1)}, u32[]{:S(2)}, u32[]{:S(2)}) collective-permute-start(bf16[4,64,1664]{2,1,0:T(8,128)(2,1)S(1)} %pad_maximum_fusion.1.refs_0_), channel_id=1, source_target_pairs={{0,2},{2,0},{1,3},{3,1},{4,6},{6,4},{5,7},{7,5},{8,10},{10,8},{9,1... | collective-permute-start | bytes 2555912 | tf_op jit(solution)/shard_map/ppermute | solution.py:27
  34.6 20.3 %collective-permute-start.9 = (bf16[4,64,1664]{2,1,0:T(8,128)(2,1)S(1)}, bf16[4,64,1664]{2,1,0:T(8,128)(2,1)S(1)}, u32[]{:S(2)}, u32[]{:S(2)}) collective-permute-start(bf16[4,64,1664]{2,1,0:T(8,128)(2,1)S(1)} %pad_maximum_fusion.1.refs_0_), channel_id=1, source_target_pairs={{0,1},{1,0},{2,3},{3,2},{4,5},{5,4},{6,7},{7,6},{8,9},{9,8},{10,11... | collective-permute-start | bytes 2555912 | tf_op jit(solution)/shard_map/ppermute | solution.py:27
  35.2 21.1 %collective-permute-start.17 = (bf16[64,2560]{1,0:T(8,128)(2,1)S(1)}, bf16[64,2560]{1,0:T(8,128)(2,1)S(1)}, u32[]{:S(2)}, u32[]{:S(2)}) collective-permute-start(bf16[64,2560]{1,0:T(8,128)(2,1)S(1)} %shard_map.309), channel_id=1, source_target_pairs={{0,24},{8,0},{16,8},{24,16},{1,25},{9,1},{17,9},{25,17},{2,26},{10... | collective-permute-start | bytes 983048 | tf_op jit(solution)/shard_map/ppermute | solution.py:33
  37.3 26.1 %collective-permute-start.16 = (bf16[64,2560]{1,0:T(8,128)(2,1)S(1)}, bf16[64,2560]{1,0:T(8,128)(2,1)S(1)}, u32[]{:S(2)}, u32[]{:S(2)}) collective-permute-start(bf16[64,2560]{1,0:T(8,128)(2,1)S(1)} %shard_map.309), channel_id=1, source_target_pairs={{0,16},{8,24},{16,0},{24,8},{1,17},{9,25},{17,1},{25,9},{2,18},{10... | collective-permute-start | bytes 983048 | tf_op jit(solution)/shard_map/ppermute | solution.py:33
  37.3 26.1 %collective-permute-start.15 = (bf16[64,2560]{1,0:T(8,128)(2,1)S(1)}, bf16[64,2560]{1,0:T(8,128)(2,1)S(1)}, u32[]{:S(2)}, u32[]{:S(2)}) collective-permute-start(bf16[64,2560]{1,0:T(8,128)(2,1)S(1)} %shard_map.309), channel_id=1, source_target_pairs={{0,8},{8,16},{16,24},{24,0},{1,9},{9,17},{17,25},{25,1},{2,10},{10... | collective-permute-start | bytes 983048 | tf_op jit(solution)/shard_map/ppermute | solution.py:33
  65.0 31.7 %collective-permute-start.24 = (bf16[4,64,2560]{2,1,0:T(8,128)(2,1)S(1)}, bf16[4,64,2560]{2,1,0:T(8,128)(2,1)S(1)}, u32[]{:S(2)}, u32[]{:S(2)}) collective-permute-start(bf16[4,64,2560]{2,1,0:T(8,128)(2,1)S(1)} %pad_maximum_fusion.refs_0_), channel_id=1, source_target_pairs={{0,2},{2,0},{1,3},{3,1},{4,6},{6,4},{5,7},{7,5},{8,10},{10,8},{9,1... | collective-permute-start | bytes 3932168 | tf_op jit(solution)/shard_map/ppermute | solution.py:27
  66.2 30.6 %collective-permute-start.23 = (bf16[4,64,2560]{2,1,0:T(8,128)(2,1)S(1)}, bf16[4,64,2560]{2,1,0:T(8,128)(2,1)S(1)}, u32[]{:S(2)}, u32[]{:S(2)}) collective-permute-start(bf16[4,64,2560]{2,1,0:T(8,128)(2,1)S(1)} %pad_maximum_fusion.refs_0_), channel_id=1, source_target_pairs={{0,1},{1,0},{2,3},{3,2},{4,5},{5,4},{6,7},{7,6},{8,9},{9,8},{10,11... | collective-permute-start | bytes 3932168 | tf_op jit(solution)/shard_map/ppermute | solution.py:27
  67.0 15.0 %collective-permute-start.19 = (bf16[320,1024]{1,0:T(8,128)(2,1)S(1)}, bf16[320,1024]{1,0:T(8,128)(2,1)S(1)}, u32[]{:S(2)}, u32[]{:S(2)}) collective-permute-start(bf16[320,1024]{1,0:T(8,128)(2,1)S(1)} %constant_dynamic-update-slice_fusion.refs_5_), channel_id=1, source_target_pairs={{0,8},{8,16},{16,24},{24,0},{1,9},{9,17},{17,25},{25,1},{2,10},{10... | collective-permute-start | bytes 1966088 | tf_op jit(solution)/shard_map/ppermute | solution.py:33
  93.9 17.0 %collective-permute-start.27 = (bf16[320,1024]{1,0:T(8,128)(2,1)S(1)}, bf16[320,1024]{1,0:T(8,128)(2,1)S(1)}, u32[]{:S(2)}, u32[]{:S(2)}) collective-permute-start(bf16[320,1024]{1,0:T(8,128)(2,1)S(1)} %collective-permute-done.19.refs_6_), channel_id=1, source_target_pairs={{0,8},{8,16},{16,24},{24,0},{1,9},{9,17},{17,25},{25,1},{2,10},{10... | collective-permute-start | bytes 1966088 | tf_op jit(solution)/shard_map/ppermute | solution.py:33
  112.7 22.0 %collective-permute-start.33 = (bf16[320,1024]{1,0:T(8,128)(2,1)S(1)}, bf16[320,1024]{1,0:T(8,128)(2,1)S(1)}, u32[]{:S(2)}, u32[]{:S(2)}) collective-permute-start(bf16[320,1024]{1,0:T(8,128)(2,1)S(1)} %collective-permute-done.27.refs_5_.refs_7_), channel_id=1, source_target_pairs={{0,8},{8,16},{16,24},{24,0},{1,9},{9,17},{17,25},{25,1},{2,10},{10... | collective-permute-start | bytes 1966088 | tf_op jit(solution)/shard_map/ppermute | solution.py:33
  132.3 23.3 %collective-permute-start.36 = (bf16[2,4,64,1024]{3,2,1,0:T(8,128)(2,1)S(1)}, bf16[2,4,64,1024]{3,2,1,0:T(8,128)(2,1)S(1)}, u32[]{:S(2)}, u32[]{:S(2)}) collective-permute-start(bf16[2,4,64,1024]{3,2,1,0:T(8,128)(2,1)S(1)} %get-tuple-element.192.refs_9_), channel_id=1, source_target_pairs={{0,1},{1,0},{2,3},{3,2},{4,5},{5,4},{6,7},{7,6},{8,9},{9,8},{10,11... | collective-permute-start | bytes 3145736 | tf_op jit(solution)/shard_map/ppermute | solution.py:27
  133.8 22.7 %collective-permute-start.37 = (bf16[2,4,64,1024]{3,2,1,0:T(8,128)(2,1)S(1)}, bf16[2,4,64,1024]{3,2,1,0:T(8,128)(2,1)S(1)}, u32[]{:S(2)}, u32[]{:S(2)}) collective-permute-start(bf16[2,4,64,1024]{3,2,1,0:T(8,128)(2,1)S(1)} %get-tuple-element.195), channel_id=1, source_target_pairs={{0,2},{2,0},{1,3},{3,1},{4,6},{6,4},{5,7},{7,5},{8,10},{10,8},{9,1... | collective-permute-start | bytes 3145736 | tf_op jit(solution)/shard_map/ppermute | solution.py:27
  141.2 17.4 %collective-permute-start.35 = (bf16[512,1024]{1,0:T(8,128)(2,1)S(1)}, bf16[512,1024]{1,0:T(8,128)(2,1)S(1)}, u32[]{:S(2)}, u32[]{:S(2)}) collective-permute-start(bf16[512,1024]{1,0:T(8,128)(2,1)S(1)} %get-tuple-element.182.refs_4_), channel_id=1, source_target_pairs={{0,4},{4,0},{1,5},{5,1},{2,6},{6,2},{3,7},{7,3},{8,12},{12,8},{9,1... | collective-permute-start | bytes 3145736 | tf_op jit(solution)/shard_map/ppermute | solution.py:27
  171.7 27.2 %collective-permute-start.47 = (bf16[2,4,32,2560]{3,2,1,0:T(8,128)(2,1)S(1)}, bf16[2,4,32,2560]{3,2,1,0:T(8,128)(2,1)S(1)}, u32[]{:S(2)}, u32[]{:S(2)}) collective-permute-start(bf16[2,4,32,2560]{3,2,1,0:T(8,128)(2,1)S(1)} %get-tuple-element.216.refs_10_), channel_id=1, source_target_pairs={{0,1},{1,0},{2,3},{3,2},{4,5},{5,4},{6,7},{7,6},{8,9},{9,8},{10,11... | collective-permute-start | bytes 3932168 | tf_op jit(solution)/shard_map/ppermute | solution.py:27
  172.9 28.5 %collective-permute-start.48 = (bf16[2,4,32,2560]{3,2,1,0:T(8,128)(2,1)S(1)}, bf16[2,4,32,2560]{3,2,1,0:T(8,128)(2,1)S(1)}, u32[]{:S(2)}, u32[]{:S(2)}) collective-permute-start(bf16[2,4,32,2560]{3,2,1,0:T(8,128)(2,1)S(1)} %get-tuple-element.219), channel_id=1, source_target_pairs={{0,2},{2,0},{1,3},{3,1},{4,6},{6,4},{5,7},{7,5},{8,10},{10,8},{9,1... | collective-permute-start | bytes 3932168 | tf_op jit(solution)/shard_map/ppermute | solution.py:27
  174.4 15.5 %collective-permute-start.44 = (bf16[128,1024]{1,0:T(8,128)(2,1)S(1)}, bf16[128,1024]{1,0:T(8,128)(2,1)S(1)}, u32[]{:S(2)}, u32[]{:S(2)}) collective-permute-start(bf16[128,1024]{1,0:T(8,128)(2,1)S(1)} %get-tuple-element.209), channel_id=1, source_target_pairs={{0,8},{8,16},{16,24},{24,0},{1,9},{9,17},{17,25},{25,1},{2,10},{10... | collective-permute-start | bytes 786440 | tf_op jit(solution)/shard_map/ppermute | solution.py:33
  175.9 15.6 %collective-permute-start.45 = (bf16[128,1024]{1,0:T(8,128)(2,1)S(1)}, bf16[128,1024]{1,0:T(8,128)(2,1)S(1)}, u32[]{:S(2)}, u32[]{:S(2)}) collective-permute-start(bf16[128,1024]{1,0:T(8,128)(2,1)S(1)} %get-tuple-element.210), channel_id=1, source_target_pairs={{0,16},{8,24},{16,0},{24,8},{1,17},{9,25},{17,1},{25,9},{2,18},{10... | collective-permute-start | bytes 786440 | tf_op jit(solution)/shard_map/ppermute | solution.py:33
  202.9 15.3 %collective-permute-start.50 = (bf16[4,32,2560]{2,1,0:T(8,128)(2,1)S(1)}, bf16[4,32,2560]{2,1,0:T(8,128)(2,1)S(1)}, u32[]{:S(2)}, u32[]{:S(2)}) collective-permute-start(bf16[4,32,2560]{2,1,0:T(8,128)(2,1)S(1)} %get-tuple-element.221), channel_id=1, source_target_pairs={{0,1},{1,0},{2,3},{3,2},{4,5},{5,4},{6,7},{7,6},{8,9},{9,8},{10,11... | collective-permute-start | bytes 1966088 | tf_op jit(solution)/shard_map/ppermute | solution.py:27
  221.4 18.4 %collective-permute-start.56 = (bf16[64,2560]{1,0:T(8,128)(2,1)}, bf16[64,2560]{1,0:T(8,128)(2,1)}, u32[]{:S(2)}, u32[]{:S(2)}) collective-permute-start(bf16[64,2560]{1,0:T(8,128)(2,1)} %get-tuple-element.230), channel_id=1, source_target_pairs={{0,16},{8,24},{16,0},{24,8},{1,17},{9,25},{17,1},{25,9},{2,18},{10... | collective-permute-start | bytes 983048 | tf_op jit(solution)/shard_map/ppermute | solution.py:33
  229.5 23.7 %collective-permute-start.34 = (bf16[256,1024]{1,0:T(8,128)(2,1)}, bf16[256,1024]{1,0:T(8,128)(2,1)}, u32[]{:S(2)}, u32[]{:S(2)}) collective-permute-start(bf16[256,1024]{1,0:T(8,128)(2,1)} %get-tuple-element.184), channel_id=1, source_target_pairs={{0,4},{4,0},{1,5},{5,1},{2,6},{6,2},{3,7},{7,3},{8,12},{12,8},{9,1... | collective-permute-start | bytes 1572872 | tf_op jit(solution)/shard_map/ppermute | solution.py:27
  246.8 16.8 %collective-permute-start.59 = (bf16[64,1664]{1,0:T(8,128)(2,1)S(1)}, bf16[64,1664]{1,0:T(8,128)(2,1)S(1)}, u32[]{:S(2)}, u32[]{:S(2)}) collective-permute-start(bf16[64,1664]{1,0:T(8,128)(2,1)S(1)} %get-tuple-element.237), channel_id=1, source_target_pairs={{0,16},{8,24},{16,0},{24,8},{1,17},{9,25},{17,1},{25,9},{2,18},{10... | collective-permute-start | bytes 638984 | tf_op jit(solution)/shard_map/ppermute | solution.py:33
  247.9 15.6 %collective-permute-start.60 = (bf16[64,1664]{1,0:T(8,128)(2,1)S(1)}, bf16[64,1664]{1,0:T(8,128)(2,1)S(1)}, u32[]{:S(2)}, u32[]{:S(2)}) collective-permute-start(bf16[64,1664]{1,0:T(8,128)(2,1)S(1)} %get-tuple-element.238), channel_id=1, source_target_pairs={{0,24},{8,0},{16,8},{24,16},{1,25},{9,1},{17,9},{25,17},{2,26},{10... | collective-permute-start | bytes 638984 | tf_op jit(solution)/shard_map/ppermute | solution.py:33
  (93 other events, 990.6 us)
